TPU v7x, 32 devices: a whole 2x2x4 slice. The times are simulated.
32 devices in a mesh: ep: 8 (over z, y), sp: 4 (over x, core).
Axes of the slice: x: 2, y: 2, z: 4, core: 2. Of those that a mesh axis runs over, the one named last changes fastest.
Arguments:
- tokens: bfloat16 [4096, 2048], P(('sp', 'ep')), parts along dimension 0, may hold values from -6 to 6
- norm_gain: float32 [2048], replicated, may hold values from 0.1 to 1.9
- expert_ids: int32 [4096, 8], P(('sp', 'ep')), parts along dimension 0, may hold values from 0 to 127, all different within a row; in each aligned block of 128 rows (0 to 127, 128 to 255, ...) at most 16 rows name the same one
- gate_vals: float32 [4096, 8], P(('sp', 'ep')), parts along dimension 0, may hold values from 0.25 to 4
- live_counts: int32 [32], P(('sp', 'ep')), parts along dimension 0, may hold values from 1 to 128, 896 in all
- w_gate: bfloat16 [2048, 1536], P(None, 'ep'), may hold values from -0.125 to 0.125
- w_up: bfloat16 [2048, 1536], P(None, 'ep'), may hold values from -0.125 to 0.125
- w_down: bfloat16 [1536, 2048], P('ep'), may hold values from -0.15625 to 0.15625
Outputs:
- moe_out: bfloat16 [4096, 2048], P(('sp', 'ep')), parts along dimension 0
There are 4 independent parts, one for each index of `sp`. A program takes and returns all parts, laid end to end along the dimension named above; an argument that names none is the same for every part. Nothing has to cross between parts.
Inputs may be any that keep to these rules, and one draw needn't show every extreme that they name: `expert_ids`: each row names 8 different experts. Within the rows of one device no expert is named by more than 16 rows, a bound that some block reaches. `live_counts`: they sum to 896; one device is full.
All inputs are finite; a program needn't handle non-finite values.
Results may differ from a plain program's by a relative error of at most 0.0089.
Values may be sent and summed in bfloat16 or wider, within the bound.
No kernel may reach another device: no remote copies, remote signals or barrier semaphores. Data moves between devices by JAX's collectives and lax.ppermute only.
A program may use at most 64 MiB of HBM per device.

v0:
```python
import jax
import jax.numpy as jnp
from jax import lax
from jax.sharding import PartitionSpec as P

SLICES = 8
CAP = 16


def local_slice(gate_cols, up_cols, down_rows, arrived):
    sources, items, features = arrived.shape
    flat_rows = arrived.reshape(sources * items, features)
    gate_act = jnp.dot(flat_rows, gate_cols, preferred_element_type=jnp.float32)
    up_act = jnp.dot(flat_rows, up_cols, preferred_element_type=jnp.float32)
    hidden = (jax.nn.silu(gate_act) * up_act).astype(jnp.bfloat16)
    partial_out = jnp.dot(hidden, down_rows, preferred_element_type=jnp.float32).astype(
        jnp.bfloat16
    )
    return partial_out.reshape(sources, items, features)


def send_back(partial_out):
    return lax.all_to_all(partial_out, "ep", split_axis=0, concat_axis=0, tiled=True)


def slice_and_return(gate_cols, up_cols, down_rows, arrived):
    return send_back(local_slice(gate_cols, up_cols, down_rows, arrived))


def pairwise_levels(stacked):
    level = stacked
    for _ in range(SLICES.bit_length() - 1):
        added = level[:, 0::2].astype(jnp.float32) + level[:, 1::2].astype(jnp.float32)
        level = lax.optimization_barrier(added.astype(jnp.bfloat16))
    return level[:, 0]


def on_device(tokens, norm_gain, expert_ids, gate_vals, live_counts, w_gate, w_up, w_down):
    tok_rows, features = tokens.shape
    choose_count = expert_ids.shape[1]
    devices = lax.axis_size("ep")
    flight = devices // SLICES
    slot_count = flight * CAP
    values = tokens.astype(jnp.float32)
    mean_sq = jnp.mean(values * values, axis=-1, keepdims=True)
    normed = (values * lax.rsqrt(mean_sq + 1e-06) * norm_gain).astype(jnp.bfloat16)
    live = jnp.arange(tok_rows, dtype=jnp.int32) < live_counts[0]
    active = ((expert_ids < flight) & live[:, None]).reshape(-1)
    flat_ids = expert_ids.reshape(-1)
    expert_cols = jnp.arange(flight, dtype=jnp.int32)
    onehot = ((flat_ids[:, None] == expert_cols[None, :]) & active[:, None]).astype(jnp.int32)
    earlier = jnp.cumsum(onehot, axis=0) - onehot
    slot_rank = jnp.sum(earlier * onehot, axis=1)
    place = jnp.where(active, flat_ids * CAP + slot_rank, -1).reshape(tok_rows, choose_count)
    match = place[:, :, None] == jnp.arange(slot_count, dtype=jnp.int32)[None, None, :]
    pick_table = jnp.any(match, axis=1).astype(jnp.bfloat16)
    combine_table = jnp.sum(jnp.where(match, gate_vals[:, :, None], 0.0), axis=1)
    slot_rows = jnp.einsum(
        "ts,td->sd", pick_table, normed, preferred_element_type=jnp.float32
    ).astype(jnp.bfloat16)
    send_rows = jnp.broadcast_to(
        slot_rows.reshape(flight, 1, CAP, features), (flight, SLICES, CAP, features)
    ).reshape(devices, CAP, features)
    returned = slice_and_return(
        w_gate,
        w_up,
        w_down,
        lax.all_to_all(send_rows, "ep", split_axis=0, concat_axis=0, tiled=True),
    )
    expert_out = pairwise_levels(returned.reshape(flight, SLICES, CAP, features))
    summed = expert_out.reshape(slot_count, features).astype(jnp.float32)
    result = jnp.dot(
        combine_table, summed, precision=lax.Precision.HIGHEST, preferred_element_type=jnp.float32
    )
    return result.astype(jnp.bfloat16)


def solution(mesh):
    return jax.shard_map(
        on_device,
        mesh=mesh,
        in_specs=(
            P(("sp", "ep"), None),
            P(),
            P(("sp", "ep"), None),
            P(("sp", "ep"), None),
            P(("sp", "ep")),
            P(None, "ep"),
            P(None, "ep"),
            P("ep", None),
        ),
        out_specs=P(("sp", "ep"), None),
        check_vma=False,
    )
```

profile of v0, /device:TPU:0, one launch (start us, length us, event | category | flops | bytes accessed | tf_op | source)
XLA Modules:
  0.0 47.8 jit_solution(10877935269599556315)
XLA Ops:
  0.0 0.0 copy-start
  0.0 0.0 copy-start.4
  0.0 0.0 copy-start.3
  0.8 0.0 copy-done.4
  0.8 0.1 copy.28
  0.9 0.1 reshape.135
  1.0 0.3 reduce-window.6
  1.3 0.2 slice_reduce_fusion
  1.5 0.1 reshape.127
  1.6 0.2 reduce-window.9
  1.7 0.1 broadcast.57
  1.8 0.1 reshape.130
  2.0 0.1 copy.29
  2.1 0.0 copy-start.6
  2.1 1.2 %fusion.1 = f32[128]{0:T(128)S(1)} fusion(bf16[128,2048]{1,0:T(8,128)(2,1)} %param.8), kind=kLoop, calls=%fused_computation.7 | loop fusion | flops 786304 | bytes 524800 | tf_op jit(solution)/shard_map/reduce_sum | solution.py:45
  3.3 0.0 copy-done.3
  3.3 0.0 copy-done.6
  3.3 0.3 convolution_convert_fusion.2
  3.6 0.0 copy-start.1
  3.7 21.7 %all_to_all.10 = bf16[8,16,2048]{2,1,0:T(8,128)(2,1)S(1)} all-to-all(bf16[8,16,2048]{2,1,0:T(8,128)(2,1)S(1)} %reshape.131), channel_id=1, replica_groups=mesh['ep'=8,'sp'=4] {'ep'}, dimensions={0} | all-to-all | bytes 1048576 | tf_op jit(solution)/shard_map/all_to_all | solution.py:68
  25.5 0.0 copy-start.2
  25.5 0.0 copy-done.1
  25.5 0.4 fusion.17
  25.9 0.0 copy-done
  25.9 0.7 %copy-done.2 = bf16[2048,192]{0,1:T(8,128)(2,1)S(1)} copy-done((bf16[2048,192]{0,1:T(8,128)(2,1)S(1)}, bf16[2048,192]{0,1:T(8,128)(2,1)}, u32[]{:S(2)}) %copy-start.2) | copy-done | bytes 786456
  26.6 1.7 %convolution_convert_fusion.1 = bf16[128,2048]{1,0:T(8,128)(2,1)} fusion(bf16[192,2048]{1,0:T(8,128)(2,1)S(1)} %copy-done, bf16[128,2048]{1,0:T(8,128)(2,1)S(1)} %bitcast.21, bf16[2048,192]{0,1:T(8,128)(2,1)S(1)} %copy-done.2, f32[128,192]{0,1:T(8,128)S(1)} %fusion.17), kind=kOutput, calls=%fused_computation.1 | convolution fusion | flops 201736192 | bytes 2719744 | tf_op jit(solution)/shard_map/dot_general | solution.py:16
  28.3 0.0 copy-start.5
  28.3 3.7 %all-to-all-start.1 = ((bf16[8,16,2048]{2,1,0:T(8,128)(2,1)}), bf16[8,16,2048]{2,1,0:T(8,128)(2,1)S(1)}, u32[]{:S(2)}, u32[]{:S(2)}) async-start(bf16[8,16,2048]{2,1,0:T(8,128)(2,1)} %bitcast.3), calls=%async_computation.1 | async-start | bytes 1048576 | tf_op jit(solution)/shard_map/all_to_all | solution.py:23
  32.0 0.0 copy-done.5
  32.1 14.2 %all-to-all-done.1 = bf16[8,16,2048]{2,1,0:T(8,128)(2,1)S(1)} async-done(((bf16[8,16,2048]{2,1,0:T(8,128)(2,1)}), bf16[8,16,2048]{2,1,0:T(8,128)(2,1)S(1)}, u32[]{:S(2)}, u32[]{:S(2)}) %all-to-all-start.1) | async-done | bytes 524320 | tf_op jit(solution)/shard_map/all_to_all | solution.py:23
  46.2 0.1 add_convert_fusion
  46.4 1.4 %convolution_convert_fusion = bf16[128,2048]{1,0:T(8,128)(2,1)} fusion(f32[128,16]{0,1:T(8,128)S(1)} %select_reduce_fusion, bf16[1,1,16,2048]{3,2,1,0:T(8,128)(2,1)S(1)} %add_convert_fusion.2), kind=kOutput, calls=%fused_computation | convolution fusion | flops 50593792 | bytes 598016 | tf_op jit(solution)/shard_map/dot_general | solution.py:72
  (11 shorter events, 0.2 us)
Async XLA Ops:
  0.0 25.9 %copy-start = (bf16[192,2048]{1,0:T(8,128)(2,1)S(1)}, bf16[192,2048]{1,0:T(8,128)(2,1)}, u32[]{:S(2)}) copy-start(bf16[192,2048]{1,0:T(8,128)(2,1)} %param.15) | copy-start | bytes 2359300
  0.0 0.8 %copy-start.4 = (s32[128,8]{0,1:T(8,128)S(1)}, s32[128,8]{0,1:T(8,128)}, u32[]{:S(2)}) copy-start(s32[128,8]{0,1:T(8,128)} %param.10) | copy-start | bytes 12292
  0.0 3.3 %copy-start.3 = (bf16[128,2048]{1,0:T(8,128)(2,1)S(1)}, bf16[128,2048]{1,0:T(8,128)(2,1)}, u32[]{:S(2)}) copy-start(bf16[128,2048]{1,0:T(8,128)(2,1)} %param.8) | copy-start | bytes 1572868
  2.1 1.3 %copy-start.6 = (f32[2048]{0:T(1024)S(1)}, f32[2048]{0:T(1024)}, u32[]{:S(2)}) copy-start(f32[2048]{0:T(1024)} %param.9) | copy-start | bytes 24580
  3.6 21.8 %copy-start.1 = (bf16[2048,192]{0,1:T(8,128)(2,1)S(1)}, bf16[2048,192]{0,1:T(8,128)(2,1)}, u32[]{:S(2)}) copy-start(bf16[2048,192]{0,1:T(8,128)(2,1)} %param.13) | copy-start | bytes 2359300
  25.5 1.1 %copy-start.2 = (bf16[2048,192]{0,1:T(8,128)(2,1)S(1)}, bf16[2048,192]{0,1:T(8,128)(2,1)}, u32[]{:S(2)}) copy-start(bf16[2048,192]{0,1:T(8,128)(2,1)} %param.14) | copy-start | bytes 2359300
  28.3 3.7 %copy-start.5 = (f32[128,8]{0,1:T(8,128)S(1)}, f32[128,8]{0,1:T(8,128)}, u32[]{:S(2)}) copy-start(f32[128,8]{0,1:T(8,128)} %param.11) | copy-start | bytes 12292
  28.3 17.9 %all-to-all-start.1 = ((bf16[8,16,2048]{2,1,0:T(8,128)(2,1)}), bf16[8,16,2048]{2,1,0:T(8,128)(2,1)S(1)}, u32[]{:S(2)}, u32[]{:S(2)}) async-start(bf16[8,16,2048]{2,1,0:T(8,128)(2,1)} %bitcast.3), calls=%async_computation.1 | async-start | bytes 1048576 | tf_op jit(solution)/shard_map/all_to_all | solution.py:23
where the time goes:
time: 48.1 us; the launch traced here: 47.8 us
  blocking collectives  21.7 us (45%)
  waiting for transfers between devices  14.2 us (30%)
  matrix products  3.84 us (8%)
  starting transfers between devices  3.72 us (8%)
  other arithmetic  1.9 us (4%)
  local copies, waits for them, and re-layouts  1.52 us (3%)
  between operations  0.88 us (2%)
    all_to_all x1, blocking collectives, on_device(): lax.all_to_all(send_rows, 'ep', split_axis=0, concat_axis=0, tiled=True)  21.7 us
    all_to_all x1, waiting for transfers between devices, send_back(): lax.all_to_all(partial_out, 'ep', split_axis=0, concat_axis=0, tiled=True)  14.2 us
    all_to_all x1, starting transfers between devices, send_back(): lax.all_to_all(partial_out, 'ep', split_axis=0, concat_axis=0, tiled=True)  3.72 us
    dot_general x1, matrix products, local_slice(): jnp.dot(hidden, down_rows, preferred_element_type=jnp.float32)  1.72 us
    dot_general x1, matrix products, on_device(): jnp.dot(combine_table, summed, precision=lax.Precision.HIGHEST, preferred...  1.42 us
    reduce_sum x1, other arithmetic, on_device(): mean_sq = jnp.mean(values * values, axis=-1, keepdims=True)  1.23 us
  transfers between devices with their start and end apart: 1, of which 1 were waited for; matrix products, arithmetic and copies ran while one was open for 0% of the time, Pallas kernels for 0%

commit v1 on v0

v1 whole, which is shorter than its diff:
```python
import functools

import jax
import jax.numpy as jnp
from jax import lax
from jax.experimental import pallas as pl
from jax.experimental.pallas import tpu as pltpu
from jax.sharding import PartitionSpec as P

SLICES = 8
CAP = 16
VMEM_LIMIT = 40 * 1024 * 1024


def pick_kernel(live_ref, ids_ref, gate_ref, tokens_ref, gain_ref, rows_ref, table_ref):
    slots, tok_rows = table_ref.shape
    slot = lax.broadcasted_iota(jnp.int32, (slots, tok_rows), 0)
    token = lax.broadcasted_iota(jnp.int32, (slots, tok_rows), 1)
    expert, place = slot // CAP, slot % CAP
    live = token < live_ref[0]
    chosen = jnp.zeros((slots, tok_rows), jnp.float32)
    weight = jnp.zeros((slots, tok_rows), jnp.float32)
    for k in range(ids_ref.shape[0]):
        hit = (ids_ref[k : k + 1, :] == expert) & live
        chosen = jnp.where(hit, 1.0, chosen)
        weight = jnp.where(hit, gate_ref[k : k + 1, :], weight)
    before = lax.broadcasted_iota(jnp.int32, (tok_rows, tok_rows), 0)
    after = lax.broadcasted_iota(jnp.int32, (tok_rows, tok_rows), 1)
    earlier = jnp.where(before < after, 1.0, 0.0).astype(jnp.bfloat16)
    rank = jnp.dot(chosen.astype(jnp.bfloat16), earlier, preferred_element_type=jnp.float32)
    pick = jnp.where((chosen > 0.0) & (rank.astype(jnp.int32) == place), 1.0, 0.0)
    table_ref[...] = pick * weight
    values = jnp.dot(pick.astype(jnp.bfloat16), tokens_ref[...], preferred_element_type=jnp.float32)
    mean_sq = jnp.mean(values * values, axis=-1, keepdims=True)
    rows_ref[...] = (values * lax.rsqrt(mean_sq + 1e-06) * gain_ref[...]).astype(jnp.bfloat16)


def pick_rows(slots, live_counts, ids, gate_vals, tokens, gain):
    vmem = pl.BlockSpec(memory_space=pltpu.VMEM)
    return pl.pallas_call(
        pick_kernel,
        out_shape=(
            jax.ShapeDtypeStruct((slots, tokens.shape[1]), jnp.bfloat16),
            jax.ShapeDtypeStruct((slots, tokens.shape[0]), jnp.float32),
        ),
        in_specs=[pl.BlockSpec(memory_space=pltpu.SMEM), vmem, vmem, vmem, vmem],
        out_specs=(vmem, vmem),
        compiler_params=pltpu.CompilerParams(vmem_limit_bytes=VMEM_LIMIT),
        name="pick_rows",
    )(live_counts, ids, gate_vals, tokens, gain)


def expert_kernel(rows_ref, gate_ref, up_ref, down_ref, out_ref):
    dims = (((1,), (1,)), ((), ()))
    rows = rows_ref[...]
    gate_act = lax.dot_general(rows, gate_ref[...], dims, preferred_element_type=jnp.float32)
    up_act = lax.dot_general(rows, up_ref[...], dims, preferred_element_type=jnp.float32)
    hidden = (jax.nn.silu(gate_act) * up_act).astype(jnp.bfloat16)
    out_ref[...] = jnp.dot(hidden, down_ref[...], preferred_element_type=jnp.float32).astype(
        jnp.bfloat16
    )


def expert_slice(rows, gate_rows, up_rows, down_rows):
    count, features = rows.shape
    block = min(count, 128)
    whole = pl.BlockSpec(gate_rows.shape, lambda i: (0, 0))
    return pl.pallas_call(
        expert_kernel,
        grid=(count // block,),
        out_shape=jax.ShapeDtypeStruct((count, features), jnp.bfloat16),
        in_specs=[pl.BlockSpec((block, features), lambda i: (i, 0)), whole, whole, whole],
        out_specs=pl.BlockSpec((block, features), lambda i: (i, 0)),
        compiler_params=pltpu.CompilerParams(vmem_limit_bytes=VMEM_LIMIT),
        name="expert_slice",
    )(rows, gate_rows, up_rows, down_rows)


def combine_kernel(table_ref, kept_ref, came_ref, out_ref):
    dims = (((0,), (0,)), ((), ()))
    summed = (kept_ref[...].astype(jnp.float32) + came_ref[...].astype(jnp.float32)).astype(
        jnp.bfloat16
    )
    table = table_ref[...]
    result = jnp.zeros(out_ref.shape, jnp.float32)
    for _ in range(3):
        piece = table.astype(jnp.bfloat16)
        result = result + lax.dot_general(piece, summed, dims, preferred_element_type=jnp.float32)
        table = table - piece.astype(jnp.float32)
    out_ref[...] = result.astype(jnp.bfloat16)


def combine(table, kept, came):
    vmem = pl.BlockSpec(memory_space=pltpu.VMEM)
    return pl.pallas_call(
        combine_kernel,
        out_shape=jax.ShapeDtypeStruct((table.shape[1], kept.shape[1]), jnp.bfloat16),
        in_specs=[vmem, vmem, vmem],
        out_specs=vmem,
        compiler_params=pltpu.CompilerParams(vmem_limit_bytes=VMEM_LIMIT),
        name="combine",
    )(table, kept, came)


def across_groups(flight, blocks):
    if flight == 1:
        return blocks
    groups = [[g * SLICES + m for g in range(flight)] for m in range(SLICES)]
    return lax.all_to_all(
        blocks, "ep", split_axis=0, concat_axis=0, axis_index_groups=groups, tiled=True
    )


def swap(devices, distance, block):
    return lax.ppermute(block, "ep", [(i, i ^ distance) for i in range(devices)])


def add_level(kept, came):
    return (kept.astype(jnp.float32) + came.astype(jnp.float32)).astype(jnp.bfloat16)


def on_device(tokens, norm_gain, expert_ids, gate_vals, live_counts, w_gate, w_up, w_down):
    features = tokens.shape[1]
    devices = lax.axis_size("ep")
    flight = devices // SLICES
    slots = flight * CAP
    rows, table = pick_rows(
        slots, live_counts, expert_ids.T, gate_vals.T, tokens, norm_gain.reshape(1, features)
    )
    own = across_groups(flight, rows)
    groups = [[g * SLICES + m for m in range(SLICES)] for g in range(flight)]
    arrived = lax.all_gather(own, "ep", axis_index_groups=groups, tiled=True)
    partial_out = expert_slice(arrived, w_gate.T, w_up.T, w_down)
    me = lax.axis_index("ep")
    level = partial_out.reshape(SLICES // 2, 2, slots, features)
    for bit in range(3):
        mine = (me >> bit) & 1
        kept = lax.dynamic_index_in_dim(level, mine, 1, keepdims=False)
        sent = lax.dynamic_index_in_dim(level, 1 - mine, 1, keepdims=False)
        came = swap(devices, 1 << bit, sent)
        if bit < 2:
            level = add_level(kept, came).reshape(-1, 2, slots, features)
    kept, came = (across_groups(flight, part.reshape(slots, features)) for part in (kept, came))
    return combine(table, kept, came)


def solution(mesh):
    return jax.shard_map(
        on_device,
        mesh=mesh,
        in_specs=(
            P(("sp", "ep"), None),
            P(),
            P(("sp", "ep"), None),
            P(("sp", "ep"), None),
            P(("sp", "ep")),
            P(None, "ep"),
            P(None, "ep"),
            P("ep", None),
        ),
        out_specs=P(("sp", "ep"), None),
        check_vma=False,
    )
```

time: 48.1 us -> 59.7 us (1.24)
  blocking collectives: 21.7 us -> 33 us
  local copies, waits for them, and re-layouts: 1.52 us -> 5.44 us
  matrix products: 3.84 us -> 0 us
  Pallas kernels: 0 us -> 2.68 us
  other arithmetic: 1.9 us -> 0.1 us
    all_gather x0 -> x1, blocking collectives: none -> 33 us  [on_device(): arrived = lax.all_gather(own, 'ep', axis_index_groups=groups, tiled=True)]
    all_to_all x1 -> x0, blocking collectives: 21.7 us -> none  [on_device(): lax.all_to_all(send_rows, 'ep', split_axis=0, concat_axis=0, tiled=True)]
    all_to_all x1 -> x0, waiting for transfers between devices: 14.2 us -> none  [send_back(): lax.all_to_all(partial_out, 'ep', split_axis=0, concat_axis=0, tiled=True)]
    ppermute x0 -> x3, waiting for transfers between devices: none -> 13.8 us  [swap(): lax.ppermute(block, 'ep', [(i, i ^ distance) for i in range(devices)])]
    unnamed x14, local copies, waits for them, and re-layouts: 0.74 us -> 5.37 us
    dot_general x4 -> x0, matrix products: 3.84 us -> none  [the longest x1 1.72 us: local_slice(): jnp.dot(hidden, down_rows, preferred_element_type=jnp.float32)]
    all_to_all x1 -> x0, starting transfers between devices: 3.72 us -> none  [send_back(): lax.all_to_all(partial_out, 'ep', split_axis=0, concat_axis=0, tiled=True)]
    ppermute x0 -> x3, starting transfers between devices: none -> 3.63 us  [swap(): lax.ppermute(block, 'ep', [(i, i ^ distance) for i in range(devices)])]
  transfers between devices with their start and end apart: 1 -> 3, of which waited for: 1 -> 3; matrix products, arithmetic and copies ran while one was open for 0% -> 0% of each run, Pallas kernels for 0% -> 0%
where the time goes in v1:
time: 59.7 us; the launch traced here: 59.4 us
  blocking collectives  33 us (55%)
  waiting for transfers between devices  13.8 us (23%)
  local copies, waits for them, and re-layouts  5.44 us (9%)
  starting transfers between devices  3.63 us (6%)
  Pallas kernels  2.68 us (4%)
  between operations  0.8 us (1%)
    all_gather x1, blocking collectives, on_device(): arrived = lax.all_gather(own, 'ep', axis_index_groups=groups, tiled=True)  33 us
    ppermute x3, waiting for transfers between devices, swap(): lax.ppermute(block, 'ep', [(i, i ^ distance) for i in range(devices)])  13.8 us
    unnamed x14, local copies, waits for them, and re-layouts  5.37 us
    ppermute x3, starting transfers between devices, swap(): lax.ppermute(block, 'ep', [(i, i ^ distance) for i in range(devices)])  3.63 us
    pallas_call x1, Pallas kernels, combine(): pl.pallas_call(combine_kernel, out_shape=jax.ShapeDtypeStruct((table.shap...  1.39 us
  transfers between devices with their start and end apart: 3, of which 3 were waited for; matrix products, arithmetic and copies ran while one was open for 0% of the time, Pallas kernels for 0%

profile of v1, /device:TPU:0, one launch (start us, length us, event | category | flops | bytes accessed | tf_op | source)
XLA Modules:
  0.0 59.4 jit_solution(5660590219852064192)
XLA Ops:
  0.0 0.0 copy-start
  0.7 0.0 copy-start.3
  0.7 1.0 %copy-done.3 = bf16[128,2048]{1,0:T(8,128)(2,1)S(1)} copy-done((bf16[128,2048]{1,0:T(8,128)(2,1)S(1)}, bf16[128,2048]{1,0:T(8,128)(2,1)}, u32[]{:S(2)}) %copy-start.3) | copy-done | bytes 524312
  1.8 0.0 copy-start.4
  1.8 0.7 %copy-done.4 = f32[2048]{0:T(1024)S(1)} copy-done((f32[2048]{0:T(1024)S(1)}, f32[2048]{0:T(1024)}, u32[]{:S(2)}) %copy-start.4) | copy-done | bytes 8216
  2.5 0.0 copy-start.5
  2.5 0.7 %copy-done.5 = s32[128,8]{0,1:T(8,128)S(1)} copy-done((s32[128,8]{0,1:T(8,128)S(1)}, s32[128,8]{0,1:T(8,128)}, u32[]{:S(2)}) %copy-start.5) | copy-done | bytes 4120
  3.2 0.0 copy-start.6
  3.2 0.7 %copy-done.6 = f32[128,8]{0,1:T(8,128)S(1)} copy-done((f32[128,8]{0,1:T(8,128)S(1)}, f32[128,8]{0,1:T(8,128)}, u32[]{:S(2)}) %copy-start.6) | copy-done | bytes 4120
  3.8 0.4 pick_rows.1
  4.3 33.0 %all_gather.3.rows_ref = bf16[128,2048]{1,0:T(8,128)(2,1)S(1)} all-gather(bf16[16,2048]{1,0:T(8,128)(2,1)S(1)} %get-tuple-element.8), channel_id=1, replica_groups={{0,4,8,12,16,20,24,28},{1,5,9,13,17,21,25,29},{2,6,10,14,18,22,26,30},{..., dimensions={0}, use_global_device_ids=true | all-gather | bytes 589824 | tf_op jit(solution)/shard_map/all_gather | solution.py:132
  37.3 0.0 copy-done
  37.3 0.0 copy-start.1
  37.3 1.1 %copy-done.1 = bf16[2048,192]{0,1:T(8,128)(2,1)S(1)} copy-done((bf16[2048,192]{0,1:T(8,128)(2,1)S(1)}, bf16[2048,192]{0,1:T(8,128)(2,1)}, u32[]{:S(2)}) %copy-start.1) | copy-done | bytes 786456
  38.4 0.0 copy-start.2
  38.4 1.1 %copy-done.2 = bf16[192,2048]{1,0:T(8,128)(2,1)S(1)} copy-done((bf16[192,2048]{1,0:T(8,128)(2,1)S(1)}, bf16[192,2048]{1,0:T(8,128)(2,1)}, u32[]{:S(2)}) %copy-start.2) | copy-done | bytes 786456
  39.5 0.9 %expert_slice.1 = bf16[128,2048]{1,0:T(8,128)(2,1)S(1)} custom-call(bf16[128,2048]{1,0:T(8,128)(2,1)S(1)} %all_gather.3.rows_ref, bf16[192,2048]{1,0:T(8,128)(2,1)S(1)} %bitcast.26, bf16[192,2048]{1,0:T(8,128)(2,1)S(1)} %bitcast.27, bf16[192,2048]{1,0:T(8,128)(2,1)S(1)} %copy-done.2), custom_call_target="tpu_custom_call" | custom-call | tf_op jit(solution)/shard_map/expert_slice/pallas_call | solution.py:68
  40.5 2.0 %collective-permute-start = (bf16[4,16,2048]{2,1,0:T(8,128)(2,1)S(1)}, bf16[4,16,2048]{2,1,0:T(8,128)(2,1)S(1)}, u32[]{:S(2)}, u32[]{:S(2)}) collective-permute-start(bf16[4,16,2048]{2,1,0:T(8,128)(2,1)S(1)} %dynamic-slice_bitcast_fusion), channel_id=1, source_target_pairs={{0,4},{4,0},{8,12},{12,8},{16,20},{20,16},{24,28},{28,24},{1,5},{5... | collective-permute-start | bytes 786440 | tf_op jit(solution)/shard_map/ppermute | solution.py:115
  42.4 4.5 %collective-permute-done = bf16[4,16,2048]{2,1,0:T(8,128)(2,1)S(1)} collective-permute-done((bf16[4,16,2048]{2,1,0:T(8,128)(2,1)S(1)}, bf16[4,16,2048]{2,1,0:T(8,128)(2,1)S(1)}, u32[]{:S(2)}, u32[]{:S(2)}) %collective-permute-start) | collective-permute-done | bytes 262176 | tf_op jit(solution)/shard_map/ppermute | solution.py:115
  46.9 0.1 fusion
  47.0 0.1 collective-permute-start.1
  47.1 4.9 %collective-permute-done.1 = bf16[2,16,2048]{2,1,0:T(8,128)(2,1)S(1)} collective-permute-done((bf16[2,16,2048]{2,1,0:T(8,128)(2,1)S(1)}, bf16[2,16,2048]{2,1,0:T(8,128)(2,1)S(1)}, u32[]{:S(2)}, u32[]{:S(2)}) %collective-permute-start.1) | collective-permute-done | bytes 131104 | tf_op jit(solution)/shard_map/ppermute | solution.py:115
  52.1 1.6 %collective-permute-start.2 = (bf16[1,16,2048]{2,1,0:T(8,128)(2,1)S(1)}, bf16[1,16,2048]{2,1,0:T(8,128)(2,1)S(1)}, u32[]{:S(2)}, u32[]{:S(2)}) collective-permute-start(bf16[1,16,2048]{2,1,0:T(8,128)(2,1)S(1)} %get-tuple-element.9), channel_id=1, source_target_pairs={{0,16},{4,20},{8,24},{12,28},{16,0},{20,4},{24,8},{28,12},{1,17},{... | collective-permute-start | bytes 196616 | tf_op jit(solution)/shard_map/ppermute | solution.py:115
  53.7 4.3 %collective-permute-done.2 = bf16[1,16,2048]{2,1,0:T(8,128)(2,1)S(1)} collective-permute-done((bf16[1,16,2048]{2,1,0:T(8,128)(2,1)S(1)}, bf16[1,16,2048]{2,1,0:T(8,128)(2,1)S(1)}, u32[]{:S(2)}, u32[]{:S(2)}) %collective-permute-start.2) | collective-permute-done | bytes 65568 | tf_op jit(solution)/shard_map/ppermute | solution.py:115
  58.0 1.4 %combine.1 = bf16[128,2048]{1,0:T(8,128)(2,1)} custom-call(f32[16,128]{1,0:T(8,128)S(1)} %get-tuple-element.7.table_ref, bf16[16,2048]{1,0:T(8,128)(2,1)S(1)} %get-tuple-element.10.kept_ref, bf16[16,2048]{1,0:T(8,128)(2,1)S(1)} %bitcast.28), custom_call_target="tpu_custom_call" | custom-call | tf_op jit(solution)/shard_map/combine/pallas_call | solution.py:95
  (4 shorter events, 0.1 us)
Async XLA Ops:
  0.0 37.3 %copy-start = (bf16[2048,192]{0,1:T(8,128)(2,1)S(1)}, bf16[2048,192]{0,1:T(8,128)(2,1)}, u32[]{:S(2)}) copy-start(bf16[2048,192]{0,1:T(8,128)(2,1)} %param.13) | copy-start | bytes 2359300
  0.7 1.0 %copy-start.3 = (bf16[128,2048]{1,0:T(8,128)(2,1)S(1)}, bf16[128,2048]{1,0:T(8,128)(2,1)}, u32[]{:S(2)}) copy-start(bf16[128,2048]{1,0:T(8,128)(2,1)} %tokens_ref.1) | copy-start | bytes 1572868
  1.8 0.7 %copy-start.4 = (f32[2048]{0:T(1024)S(1)}, f32[2048]{0:T(1024)}, u32[]{:S(2)}) copy-start(f32[2048]{0:T(1024)} %param.9) | copy-start | bytes 24580
  2.5 0.7 %copy-start.5 = (s32[128,8]{0,1:T(8,128)S(1)}, s32[128,8]{0,1:T(8,128)}, u32[]{:S(2)}) copy-start(s32[128,8]{0,1:T(8,128)} %param.10) | copy-start | bytes 12292
  3.2 0.7 %copy-start.6 = (f32[128,8]{0,1:T(8,128)S(1)}, f32[128,8]{0,1:T(8,128)}, u32[]{:S(2)}) copy-start(f32[128,8]{0,1:T(8,128)} %param.11) | copy-start | bytes 12292
  37.3 1.1 %copy-start.1 = (bf16[2048,192]{0,1:T(8,128)(2,1)S(1)}, bf16[2048,192]{0,1:T(8,128)(2,1)}, u32[]{:S(2)}) copy-start(bf16[2048,192]{0,1:T(8,128)(2,1)} %param.14) | copy-start | bytes 2359300
  38.4 1.1 %copy-start.2 = (bf16[192,2048]{1,0:T(8,128)(2,1)S(1)}, bf16[192,2048]{1,0:T(8,128)(2,1)}, u32[]{:S(2)}) copy-start(bf16[192,2048]{1,0:T(8,128)(2,1)} %down_ref.1) | copy-start | bytes 2359300
  40.5 6.4 %collective-permute-start = (bf16[4,16,2048]{2,1,0:T(8,128)(2,1)S(1)}, bf16[4,16,2048]{2,1,0:T(8,128)(2,1)S(1)}, u32[]{:S(2)}, u32[]{:S(2)}) collective-permute-start(bf16[4,16,2048]{2,1,0:T(8,128)(2,1)S(1)} %dynamic-slice_bitcast_fusion), channel_id=1, source_target_pairs={{0,4},{4,0},{8,12},{12,8},{16,20},{20,16},{24,28},{28,24},{1,5},{5... | collective-permute-start | bytes 786440 | tf_op jit(solution)/shard_map/ppermute | solution.py:115
  47.0 5.0 %collective-permute-start.1 = (bf16[2,16,2048]{2,1,0:T(8,128)(2,1)S(1)}, bf16[2,16,2048]{2,1,0:T(8,128)(2,1)S(1)}, u32[]{:S(2)}, u32[]{:S(2)}) collective-permute-start(bf16[2,16,2048]{2,1,0:T(8,128)(2,1)S(1)} %dynamic-slice_bitcast_fusion.1), channel_id=1, source_target_pairs={{0,8},{4,12},{8,0},{12,4},{16,24},{20,28},{24,16},{28,20},{1,9},{5... | collective-permute-start | bytes 393224 | tf_op jit(solution)/shard_map/ppermute | solution.py:115
  52.1 5.9 %collective-permute-start.2 = (bf16[1,16,2048]{2,1,0:T(8,128)(2,1)S(1)}, bf16[1,16,2048]{2,1,0:T(8,128)(2,1)S(1)}, u32[]{:S(2)}, u32[]{:S(2)}) collective-permute-start(bf16[1,16,2048]{2,1,0:T(8,128)(2,1)S(1)} %get-tuple-element.9), channel_id=1, source_target_pairs={{0,16},{4,20},{8,24},{12,28},{16,0},{20,4},{24,8},{28,12},{1,17},{... | collective-permute-start | bytes 196616 | tf_op jit(solution)/shard_map/ppermute | solution.py:115

commit v2 on v1

v2 whole, which is shorter than its diff:
```python
import functools

import jax
import jax.numpy as jnp
from jax import lax
from jax.experimental import pallas as pl
from jax.experimental.pallas import tpu as pltpu
from jax.sharding import PartitionSpec as P

SLICES = 8
CAP = 16
VMEM_LIMIT = 40 * 1024 * 1024


def pick_kernel(
    live_ref, ids_hbm, gate_hbm, tokens_hbm, gain_hbm, rows_ref, table_ref, ids_ref, gate_ref, tokens_ref, gain_ref, sems
):
    copies = [
        pltpu.make_async_copy(source, target, sems.at[i])
        for i, (source, target) in enumerate(
            ((ids_hbm, ids_ref), (tokens_hbm, tokens_ref), (gate_hbm, gate_ref), (gain_hbm, gain_ref))
        )
    ]
    for copy in copies:
        copy.start()
    slots, tok_rows = table_ref.shape
    slot = lax.broadcasted_iota(jnp.int32, (slots, tok_rows), 0)
    token = lax.broadcasted_iota(jnp.int32, (slots, tok_rows), 1)
    expert, place = slot // CAP, slot % CAP
    live = token < live_ref[0]
    before = lax.broadcasted_iota(jnp.int32, (tok_rows, tok_rows), 0)
    after = lax.broadcasted_iota(jnp.int32, (tok_rows, tok_rows), 1)
    earlier = jnp.where(before < after, 1.0, 0.0).astype(jnp.bfloat16)
    copies[0].wait()
    hits = [(ids_ref[k : k + 1, :] == expert) & live for k in range(ids_ref.shape[0])]
    chosen = jnp.where(functools.reduce(jnp.logical_or, hits), 1.0, 0.0)
    rank = jnp.dot(chosen.astype(jnp.bfloat16), earlier, preferred_element_type=jnp.float32)
    pick = jnp.where((chosen > 0.0) & (rank.astype(jnp.int32) == place), 1.0, 0.0)
    copies[1].wait()
    values = jnp.dot(pick.astype(jnp.bfloat16), tokens_ref[...], preferred_element_type=jnp.float32)
    mean_sq = jnp.mean(values * values, axis=-1, keepdims=True)
    copies[2].wait()
    copies[3].wait()
    rows_ref[...] = (values * lax.rsqrt(mean_sq + 1e-06) * gain_ref[...]).astype(jnp.bfloat16)
    weight = jnp.zeros((slots, tok_rows), jnp.float32)
    for k, hit in enumerate(hits):
        weight = jnp.where(hit, gate_ref[k : k + 1, :], weight)
    table_ref[...] = pick * weight


def pick_rows(slots, live_counts, ids, gate_vals, tokens, gain):
    vmem = pl.BlockSpec(memory_space=pltpu.VMEM)
    hbm = pl.BlockSpec(memory_space=pltpu.HBM)
    return pl.pallas_call(
        pick_kernel,
        out_shape=(
            jax.ShapeDtypeStruct((slots, tokens.shape[1]), jnp.bfloat16),
            jax.ShapeDtypeStruct((slots, tokens.shape[0]), jnp.float32),
        ),
        in_specs=[pl.BlockSpec(memory_space=pltpu.SMEM), hbm, hbm, hbm, hbm],
        out_specs=(vmem, vmem),
        scratch_shapes=[
            pltpu.VMEM(ids.shape, ids.dtype),
            pltpu.VMEM(gate_vals.shape, gate_vals.dtype),
            pltpu.VMEM(tokens.shape, tokens.dtype),
            pltpu.VMEM(gain.shape, gain.dtype),
            pltpu.SemaphoreType.DMA((4,)),
        ],
        compiler_params=pltpu.CompilerParams(vmem_limit_bytes=VMEM_LIMIT),
        name="pick_rows",
    )(live_counts, ids, gate_vals, tokens, gain)


def expert_kernel(*refs):
    count = (len(refs) - 3) // 2
    gate_ref, up_ref, down_ref = refs[count : count + 3]
    dims = (((1,), (1,)), ((), ()))
    size = refs[0].shape[0]
    together = max(1, 128 // size)
    for first in range(0, count, together):
        last = min(count, first + together)
        rows = jnp.concatenate([ref[...] for ref in refs[first:last]], axis=0)
        gate_act = lax.dot_general(rows, gate_ref[...], dims, preferred_element_type=jnp.float32)
        up_act = lax.dot_general(rows, up_ref[...], dims, preferred_element_type=jnp.float32)
        hidden = (jax.nn.silu(gate_act) * up_act).astype(jnp.bfloat16)
        partial_out = jnp.dot(hidden, down_ref[...], preferred_element_type=jnp.float32)
        partial_out = partial_out.astype(jnp.bfloat16)
        for i in range(first, last):
            at = (i - first) * size
            refs[count + 3 + i][...] = partial_out[at : at + size]


def expert_slice(blocks, gate_rows, up_rows, down_rows):
    vmem = pl.BlockSpec(memory_space=pltpu.VMEM)
    count = len(blocks)
    return pl.pallas_call(
        expert_kernel,
        out_shape=[jax.ShapeDtypeStruct(block.shape, jnp.bfloat16) for block in blocks],
        in_specs=[vmem] * (count + 3),
        out_specs=[vmem] * count,
        compiler_params=pltpu.CompilerParams(vmem_limit_bytes=VMEM_LIMIT),
        name="expert_slice",
    )(*blocks, gate_rows, up_rows, down_rows)


def add_level(kept, came):
    return (kept.astype(jnp.float32) + came.astype(jnp.float32)).astype(jnp.bfloat16)


def add_levels(parts):
    while len(parts) > 1:
        parts = [add_level(*pair) for pair in zip(parts[::2], parts[1::2])]
    return parts[0]


def combine_kernel(table_ref, *refs):
    *parts, out_hbm, out_ref, sems = refs
    table = table_ref[...]
    pieces = []
    for _ in range(3):
        pieces.append(table.astype(jnp.bfloat16))
        table = table - pieces[-1].astype(jnp.float32)
    pieces = jnp.concatenate(pieces, axis=0)
    features = out_ref.shape[1]
    width = features // 4
    copies = []
    for i in range(4):
        columns = pl.ds(i * width, width)
        summed = add_levels([part[:, columns] for part in parts])
        out_ref[:, columns] = lax.dot_general(
            pieces,
            jnp.concatenate([summed] * 3, axis=0),
            (((0,), (0,)), ((), ())),
            preferred_element_type=jnp.float32,
        ).astype(jnp.bfloat16)
        copies.append(
            pltpu.make_async_copy(out_ref.at[:, columns], out_hbm.at[:, columns], sems.at[i])
        )
        copies[-1].start()
    for copy in copies:
        copy.wait()


def combine(table, parts):
    vmem = pl.BlockSpec(memory_space=pltpu.VMEM)
    shape = (table.shape[1], parts[0].shape[1])
    return pl.pallas_call(
        combine_kernel,
        out_shape=jax.ShapeDtypeStruct(shape, jnp.bfloat16),
        in_specs=[vmem] * (1 + len(parts)),
        out_specs=pl.BlockSpec(memory_space=pltpu.HBM),
        scratch_shapes=[pltpu.VMEM(shape, jnp.bfloat16), pltpu.SemaphoreType.DMA((4,))],
        compiler_params=pltpu.CompilerParams(vmem_limit_bytes=VMEM_LIMIT),
        name="combine",
    )(table, *parts)


def across_groups(flight, blocks):
    if flight == 1:
        return blocks
    groups = [[g * SLICES + m for g in range(flight)] for m in range(SLICES)]
    return lax.all_to_all(
        blocks, "ep", split_axis=0, concat_axis=0, axis_index_groups=groups, tiled=True
    )


def swap(devices, distance, block):
    return lax.ppermute(block, "ep", [(i, i ^ distance) for i in range(devices)])


def on_device(tokens, norm_gain, expert_ids, gate_vals, live_counts, w_gate, w_up, w_down):
    features = tokens.shape[1]
    devices = lax.axis_size("ep")
    flight = devices // SLICES
    slots = flight * CAP
    rows, table = pick_rows(
        slots, live_counts, expert_ids.T, gate_vals.T, tokens, norm_gain.reshape(1, features)
    )
    own = across_groups(flight, rows)
    blocks = {0: own}
    for j in (6, 4, 2, 1):
        blocks[j] = swap(devices, j, own)
    for j in (2, 4, 6):
        blocks[j + 1] = swap(devices, 1, blocks[j])
    partial_out = expert_slice(
        [blocks[j] for j in range(SLICES)], w_gate.T, w_up.T, w_down
    )
    level = {}
    for j in (6, 4, 2, 0):
        level[j] = add_level(partial_out[j], swap(devices, 1, partial_out[j + 1]))
    parts = [level[0]] + [swap(devices, j, level[j]) for j in (2, 4, 6)]
    if flight > 1:
        parts = [across_groups(flight, add_levels(parts))]
    return combine(table, parts)


def solution(mesh):
    return jax.shard_map(
        on_device,
        mesh=mesh,
        in_specs=(
            P(("sp", "ep"), None),
            P(),
            P(("sp", "ep"), None),
            P(("sp", "ep"), None),
            P(("sp", "ep")),
            P(None, "ep"),
            P(None, "ep"),
            P("ep", None),
        ),
        out_specs=P(("sp", "ep"), None),
        check_vma=False,
    )
```

time: 59.7 us -> 39.9 us (0.67)
  blocking collectives: 33 us -> 0 us
  starting transfers between devices: 3.63 us -> 18.5 us
  waiting for transfers between devices: 13.8 us -> 11.9 us
    all_gather x1 -> x0, blocking collectives: 33 us -> none  [on_device(): arrived = lax.all_gather(own, 'ep', axis_index_groups=groups, tiled=True)]
    ppermute x3 -> x14, starting transfers between devices: 3.63 us -> 18.5 us  [swap(): lax.ppermute(block, 'ep', [(i, i ^ distance) for i in range(devices)])]
    ppermute x3 -> x14, waiting for transfers between devices: 13.8 us -> 11.9 us  [swap(): lax.ppermute(block, 'ep', [(i, i ^ distance) for i in range(devices)])]
  transfers between devices with their start and end apart: 3 -> 14, of which waited for: 3 -> 8; matrix products, arithmetic and copies ran while one was open for 0% -> 0% of each run, Pallas kernels for 0% -> 0%
where the time goes in v2:
time: 39.9 us; the launch traced here: 39.6 us
  starting transfers between devices  18.5 us (46%)
  waiting for transfers between devices  11.9 us (30%)
  local copies, waits for them, and re-layouts  5.84 us (15%)
  Pallas kernels  2.47 us (6%)
  between operations  0.73 us (2%)
    ppermute x14, starting transfers between devices, swap(): lax.ppermute(block, 'ep', [(i, i ^ distance) for i in range(devices)])  18.5 us
    ppermute x14, waiting for transfers between devices, swap(): lax.ppermute(block, 'ep', [(i, i ^ distance) for i in range(devices)])  11.9 us
    unnamed x14, local copies, waits for them, and re-layouts  5.84 us
    pallas_call x1, Pallas kernels, combine(): pl.pallas_call(combine_kernel, out_shape=jax.ShapeDtypeStruct(shape, jnp....  1.04 us
    pallas_call x1, Pallas kernels, expert_slice(): pl.pallas_call(expert_kernel, out_shape=[jax.ShapeDtypeStruct(block.shape...  0.89 us
  transfers between devices with their start and end apart: 14, of which 8 were waited for; matrix products, arithmetic and copies ran while one was open for 0% of the time, Pallas kernels for 0%

profile of v2, /device:TPU:0, one launch (start us, length us, event | category | flops | bytes accessed | tf_op | source)
XLA Modules:
  0.0 39.6 jit_solution(15929423790424060760)
XLA Ops:
  0.0 0.0 copy-start.5
  0.7 0.0 copy-done.5
  0.7 0.0 copy-start.3
  0.7 1.0 %copy-done.3 = bf16[128,2048]{1,0:T(8,128)(2,1)S(1)} copy-done((bf16[128,2048]{1,0:T(8,128)(2,1)S(1)}, bf16[128,2048]{1,0:T(8,128)(2,1)}, u32[]{:S(2)}) %copy-start.3) | copy-done | bytes 524312
  1.7 0.0 copy-start.4
  1.7 0.7 %copy-done.4 = f32[2048]{0:T(1024)S(1)} copy-done((f32[2048]{0:T(1024)S(1)}, f32[2048]{0:T(1024)}, u32[]{:S(2)}) %copy-start.4) | copy-done | bytes 8216
  2.4 0.0 copy-start.6
  2.4 0.7 %copy-done.6 = f32[128,8]{0,1:T(8,128)S(1)} copy-done((f32[128,8]{0,1:T(8,128)S(1)}, f32[128,8]{0,1:T(8,128)}, u32[]{:S(2)}) %copy-start.6) | copy-done | bytes 4120
  3.1 0.5 %pick_rows.1 = (bf16[16,2048]{1,0:T(8,128)(2,1)S(1)}, f32[16,128]{1,0:T(8,128)S(1)}) custom-call(s32[1]{0:T(128)S(6)} %copy.9.live_ref, s32[8,128]{1,0:T(8,128)S(1)} %bitcast.8, f32[8,128]{1,0:T(8,128)S(1)} %bitcast.9, bf16[128,2048]{1,0:T(8,128)(2,1)S(1)} %copy-done.3, f32[1,2048]{1,0:T(1,128)S(1)} %bitcast.7), custom_call_target="tpu_custom_call" | custom-call | tf_op jit(solution)/shard_map/pick_rows/pallas_call | solution.py:54
  3.7 5.1 %collective-permute-start.5 = (bf16[16,2048]{1,0:T(8,128)(2,1)S(1)}, bf16[16,2048]{1,0:T(8,128)(2,1)S(1)}, u32[]{:S(2)}, u32[]{:S(2)}) collective-permute-start(bf16[16,2048]{1,0:T(8,128)(2,1)S(1)} %get-tuple-element.16.refs_0_), channel_id=1, source_target_pairs={{0,24},{4,28},{8,16},{12,20},{16,8},{20,12},{24,0},{28,4},{1,25},{... | collective-permute-start | bytes 196616 | tf_op jit(solution)/shard_map/ppermute | solution.py:168
  8.8 0.0 collective-permute-start.3
  8.8 0.6 %collective-permute-start.1 = (bf16[16,2048]{1,0:T(8,128)(2,1)S(1)}, bf16[16,2048]{1,0:T(8,128)(2,1)S(1)}, u32[]{:S(2)}, u32[]{:S(2)}) collective-permute-start(bf16[16,2048]{1,0:T(8,128)(2,1)S(1)} %get-tuple-element.16.refs_0_), channel_id=1, source_target_pairs={{0,8},{4,12},{8,0},{12,4},{16,24},{20,28},{24,16},{28,20},{1,9},{5... | collective-permute-start | bytes 196616 | tf_op jit(solution)/shard_map/ppermute | solution.py:168
  9.4 1.7 %collective-permute-start = (bf16[16,2048]{1,0:T(8,128)(2,1)S(1)}, bf16[16,2048]{1,0:T(8,128)(2,1)S(1)}, u32[]{:S(2)}, u32[]{:S(2)}) collective-permute-start(bf16[16,2048]{1,0:T(8,128)(2,1)S(1)} %get-tuple-element.16.refs_0_), channel_id=1, source_target_pairs={{0,4},{4,0},{8,12},{12,8},{16,20},{20,16},{24,28},{28,24},{1,5},{5... | collective-permute-start | bytes 196616 | tf_op jit(solution)/shard_map/ppermute | solution.py:168
  11.1 0.3 collective-permute-done.5.refs_6_
  11.3 1.9 %collective-permute-start.6 = (bf16[16,2048]{1,0:T(8,128)(2,1)S(1)}, bf16[16,2048]{1,0:T(8,128)(2,1)S(1)}, u32[]{:S(2)}, u32[]{:S(2)}) collective-permute-start(bf16[16,2048]{1,0:T(8,128)(2,1)S(1)} %collective-permute-done.5.refs_6_), channel_id=1, source_target_pairs={{0,4},{4,0},{8,12},{12,8},{16,20},{20,16},{24,28},{28,24},{1,5},{5... | collective-permute-start | bytes 196616 | tf_op jit(solution)/shard_map/ppermute | solution.py:168
  13.2 1.1 %collective-permute-done.3.refs_4_ = bf16[16,2048]{1,0:T(8,128)(2,1)S(1)} collective-permute-done((bf16[16,2048]{1,0:T(8,128)(2,1)S(1)}, bf16[16,2048]{1,0:T(8,128)(2,1)S(1)}, u32[]{:S(2)}, u32[]{:S(2)}) %collective-permute-start.3) | collective-permute-done | bytes 65568 | tf_op jit(solution)/shard_map/ppermute | solution.py:168
  14.4 1.5 %collective-permute-start.4 = (bf16[16,2048]{1,0:T(8,128)(2,1)S(1)}, bf16[16,2048]{1,0:T(8,128)(2,1)S(1)}, u32[]{:S(2)}, u32[]{:S(2)}) collective-permute-start(bf16[16,2048]{1,0:T(8,128)(2,1)S(1)} %collective-permute-done.3.refs_4_), channel_id=1, source_target_pairs={{0,4},{4,0},{8,12},{12,8},{16,20},{20,16},{24,28},{28,24},{1,5},{5... | collective-permute-start | bytes 196616 | tf_op jit(solution)/shard_map/ppermute | solution.py:168
  15.9 0.0 collective-permute-done.1.refs_2_
  15.9 0.5 %collective-permute-start.2 = (bf16[16,2048]{1,0:T(8,128)(2,1)S(1)}, bf16[16,2048]{1,0:T(8,128)(2,1)S(1)}, u32[]{:S(2)}, u32[]{:S(2)}) collective-permute-start(bf16[16,2048]{1,0:T(8,128)(2,1)S(1)} %collective-permute-done.1.refs_2_), channel_id=1, source_target_pairs={{0,4},{4,0},{8,12},{12,8},{16,20},{20,16},{24,28},{28,24},{1,5},{5... | collective-permute-start | bytes 196616 | tf_op jit(solution)/shard_map/ppermute | solution.py:168
  16.4 0.0 collective-permute-done.refs_1_
  16.4 0.0 collective-permute-done.6.refs_7_
  16.4 2.8 %collective-permute-done.4.refs_5_ = bf16[16,2048]{1,0:T(8,128)(2,1)S(1)} collective-permute-done((bf16[16,2048]{1,0:T(8,128)(2,1)S(1)}, bf16[16,2048]{1,0:T(8,128)(2,1)S(1)}, u32[]{:S(2)}, u32[]{:S(2)}) %collective-permute-start.4) | collective-permute-done | bytes 65568 | tf_op jit(solution)/shard_map/ppermute | solution.py:168
  19.2 0.9 %collective-permute-done.2.refs_3_ = bf16[16,2048]{1,0:T(8,128)(2,1)S(1)} collective-permute-done((bf16[16,2048]{1,0:T(8,128)(2,1)S(1)}, bf16[16,2048]{1,0:T(8,128)(2,1)S(1)}, u32[]{:S(2)}, u32[]{:S(2)}) %collective-permute-start.2) | collective-permute-done | bytes 65568 | tf_op jit(solution)/shard_map/ppermute | solution.py:168
  20.2 0.0 copy-start
  20.2 1.1 %copy-done = bf16[2048,192]{0,1:T(8,128)(2,1)S(1)} copy-done((bf16[2048,192]{0,1:T(8,128)(2,1)S(1)}, bf16[2048,192]{0,1:T(8,128)(2,1)}, u32[]{:S(2)}) %copy-start) | copy-done | bytes 786456
  21.3 0.0 copy-start.1
  21.3 1.1 %copy-done.1 = bf16[2048,192]{0,1:T(8,128)(2,1)S(1)} copy-done((bf16[2048,192]{0,1:T(8,128)(2,1)S(1)}, bf16[2048,192]{0,1:T(8,128)(2,1)}, u32[]{:S(2)}) %copy-start.1) | copy-done | bytes 786456
  22.4 0.0 copy-start.2
  22.4 1.1 %copy-done.2 = bf16[192,2048]{1,0:T(8,128)(2,1)S(1)} copy-done((bf16[192,2048]{1,0:T(8,128)(2,1)S(1)}, bf16[192,2048]{1,0:T(8,128)(2,1)}, u32[]{:S(2)}) %copy-start.2) | copy-done | bytes 786456
  23.6 0.9 %expert_slice.1 = (bf16[16,2048]{1,0:T(8,128)(2,1)S(1)}, bf16[16,2048]{1,0:T(8,128)(2,1)S(1)}, bf16[16,2048]{1,0:T(8,128)(2,1)S(1)}, bf16[16,2048]{1,0:T(8,128)(...) custom-call(bf16[16,2048]{1,0:T(8,128)(2,1)S(1)} %get-tuple-element., ...), custom_call_target="tpu_custom_call" | custom-call | tf_op jit(solution)/shard_map/expert_slice/pallas_call | solution.py:96
  24.5 1.0 %collective-permute-start.8 = (bf16[16,2048]{1,0:T(8,128)(2,1)S(1)}, bf16[16,2048]{1,0:T(8,128)(2,1)S(1)}, u32[]{:S(2)}, u32[]{:S(2)}) collective-permute-start(bf16[16,2048]{1,0:T(8,128)(2,1)S(1)} %get-tuple-element.20), channel_id=1, source_target_pairs={{0,4},{4,0},{8,12},{12,8},{16,20},{20,16},{24,28},{28,24},{1,5},{5... | collective-permute-start | bytes 196616 | tf_op jit(solution)/shard_map/ppermute | solution.py:168
  25.5 1.1 %collective-permute-start.7 = (bf16[16,2048]{1,0:T(8,128)(2,1)S(1)}, bf16[16,2048]{1,0:T(8,128)(2,1)S(1)}, u32[]{:S(2)}, u32[]{:S(2)}) collective-permute-start(bf16[16,2048]{1,0:T(8,128)(2,1)S(1)} %get-tuple-element.18), channel_id=1, source_target_pairs={{0,4},{4,0},{8,12},{12,8},{16,20},{20,16},{24,28},{28,24},{1,5},{5... | collective-permute-start | bytes 196616 | tf_op jit(solution)/shard_map/ppermute | solution.py:168
  26.6 1.0 %collective-permute-start.10 = (bf16[16,2048]{1,0:T(8,128)(2,1)S(1)}, bf16[16,2048]{1,0:T(8,128)(2,1)S(1)}, u32[]{:S(2)}, u32[]{:S(2)}) collective-permute-start(bf16[16,2048]{1,0:T(8,128)(2,1)S(1)} %get-tuple-element.22), channel_id=1, source_target_pairs={{0,4},{4,0},{8,12},{12,8},{16,20},{20,16},{24,28},{28,24},{1,5},{5... | collective-permute-start | bytes 196616 | tf_op jit(solution)/shard_map/ppermute | solution.py:168
  27.5 1.1 %collective-permute-start.12 = (bf16[16,2048]{1,0:T(8,128)(2,1)S(1)}, bf16[16,2048]{1,0:T(8,128)(2,1)S(1)}, u32[]{:S(2)}, u32[]{:S(2)}) collective-permute-start(bf16[16,2048]{1,0:T(8,128)(2,1)S(1)} %get-tuple-element.24), channel_id=1, source_target_pairs={{0,4},{4,0},{8,12},{12,8},{16,20},{20,16},{24,28},{28,24},{1,5},{5... | collective-permute-start | bytes 196616 | tf_op jit(solution)/shard_map/ppermute | solution.py:168
  28.6 0.9 %collective-permute-done.8 = bf16[16,2048]{1,0:T(8,128)(2,1)S(1)} collective-permute-done((bf16[16,2048]{1,0:T(8,128)(2,1)S(1)}, bf16[16,2048]{1,0:T(8,128)(2,1)S(1)}, u32[]{:S(2)}, u32[]{:S(2)}) %collective-permute-start.8) | collective-permute-done | bytes 65568 | tf_op jit(solution)/shard_map/ppermute | solution.py:168
  29.5 0.1 collective-permute-start.9
  29.6 1.7 %collective-permute-done.10 = bf16[16,2048]{1,0:T(8,128)(2,1)S(1)} collective-permute-done((bf16[16,2048]{1,0:T(8,128)(2,1)S(1)}, bf16[16,2048]{1,0:T(8,128)(2,1)S(1)}, u32[]{:S(2)}, u32[]{:S(2)}) %collective-permute-start.10) | collective-permute-done | bytes 65568 | tf_op jit(solution)/shard_map/ppermute | solution.py:168
  31.3 0.9 %collective-permute-start.11 = (bf16[16,2048]{1,0:T(8,128)(2,1)S(1)}, bf16[16,2048]{1,0:T(8,128)(2,1)S(1)}, u32[]{:S(2)}, u32[]{:S(2)}) collective-permute-start(bf16[16,2048]{1,0:T(8,128)(2,1)S(1)} %add_convert_fusion.1), channel_id=1, source_target_pairs={{0,16},{4,20},{8,24},{12,28},{16,0},{20,4},{24,8},{28,12},{1,17},{... | collective-permute-start | bytes 196616 | tf_op jit(solution)/shard_map/ppermute | solution.py:168
  32.3 0.0 collective-permute-done.12
  32.3 2.1 %collective-permute-start.13 = (bf16[16,2048]{1,0:T(8,128)(2,1)S(1)}, bf16[16,2048]{1,0:T(8,128)(2,1)S(1)}, u32[]{:S(2)}, u32[]{:S(2)}) collective-permute-start(bf16[16,2048]{1,0:T(8,128)(2,1)S(1)} %add_convert_fusion), channel_id=1, source_target_pairs={{0,24},{4,28},{8,16},{12,20},{16,8},{20,12},{24,0},{28,4},{1,25},{... | collective-permute-start | bytes 196616 | tf_op jit(solution)/shard_map/ppermute | solution.py:168
  34.3 0.0 collective-permute-done.7
  34.4 0.0 collective-permute-done.9.refs_1_
  34.4 2.6 %collective-permute-done.11.refs_2_ = bf16[16,2048]{1,0:T(8,128)(2,1)S(1)} collective-permute-done((bf16[16,2048]{1,0:T(8,128)(2,1)S(1)}, bf16[16,2048]{1,0:T(8,128)(2,1)S(1)}, u32[]{:S(2)}, u32[]{:S(2)}) %collective-permute-start.11) | collective-permute-done | bytes 65568 | tf_op jit(solution)/shard_map/ppermute | solution.py:168
  37.0 1.5 %collective-permute-done.13.refs_3_ = bf16[16,2048]{1,0:T(8,128)(2,1)S(1)} collective-permute-done((bf16[16,2048]{1,0:T(8,128)(2,1)S(1)}, bf16[16,2048]{1,0:T(8,128)(2,1)S(1)}, u32[]{:S(2)}, u32[]{:S(2)}) %collective-permute-start.13) | collective-permute-done | bytes 65568 | tf_op jit(solution)/shard_map/ppermute | solution.py:168
  38.5 1.0 %combine.1 = bf16[128,2048]{1,0:T(8,128)(2,1)} custom-call(f32[16,128]{1,0:T(8,128)S(1)} %get-tuple-element.15.table_ref, bf16[16,2048]{1,0:T(8,128)(2,1)S(1)} %add_convert_fusion.3.refs_0_, bf16[16,2048]{1,0:T(8,128)(2,1)S(1)} %collective-permute-done.9.refs_1_, bf16[16,2048]{1,0:T(8,128)(2,1)S(1)} %collective-permute-done.11.refs_2_, ...), custom_call_target="tpu_custom_call" | custom-call | tf_op jit(solution)/shard_map/combine/pallas_call | solution.py:147
  (4 shorter events, 0.1 us)
Async XLA Ops:
  0.0 0.7 %copy-start.5 = (s32[128,8]{0,1:T(8,128)S(1)}, s32[128,8]{0,1:T(8,128)}, u32[]{:S(2)}) copy-start(s32[128,8]{0,1:T(8,128)} %param.10) | copy-start | bytes 12292
  0.7 1.0 %copy-start.3 = (bf16[128,2048]{1,0:T(8,128)(2,1)S(1)}, bf16[128,2048]{1,0:T(8,128)(2,1)}, u32[]{:S(2)}) copy-start(bf16[128,2048]{1,0:T(8,128)(2,1)} %tokens_hbm.1) | copy-start | bytes 1572868
  1.7 0.7 %copy-start.4 = (f32[2048]{0:T(1024)S(1)}, f32[2048]{0:T(1024)}, u32[]{:S(2)}) copy-start(f32[2048]{0:T(1024)} %param.9) | copy-start | bytes 24580
  2.4 0.7 %copy-start.6 = (f32[128,8]{0,1:T(8,128)S(1)}, f32[128,8]{0,1:T(8,128)}, u32[]{:S(2)}) copy-start(f32[128,8]{0,1:T(8,128)} %param.11) | copy-start | bytes 12292
  3.7 7.7 %collective-permute-start.5 = (bf16[16,2048]{1,0:T(8,128)(2,1)S(1)}, bf16[16,2048]{1,0:T(8,128)(2,1)S(1)}, u32[]{:S(2)}, u32[]{:S(2)}) collective-permute-start(bf16[16,2048]{1,0:T(8,128)(2,1)S(1)} %get-tuple-element.16.refs_0_), channel_id=1, source_target_pairs={{0,24},{4,28},{8,16},{12,20},{16,8},{20,12},{24,0},{28,4},{1,25},{... | collective-permute-start | bytes 196616 | tf_op jit(solution)/shard_map/ppermute | solution.py:168
  8.8 5.6 %collective-permute-start.3 = (bf16[16,2048]{1,0:T(8,128)(2,1)S(1)}, bf16[16,2048]{1,0:T(8,128)(2,1)S(1)}, u32[]{:S(2)}, u32[]{:S(2)}) collective-permute-start(bf16[16,2048]{1,0:T(8,128)(2,1)S(1)} %get-tuple-element.16.refs_0_), channel_id=1, source_target_pairs={{0,16},{4,20},{8,24},{12,28},{16,0},{20,4},{24,8},{28,12},{1,17},{... | collective-permute-start | bytes 196616 | tf_op jit(solution)/shard_map/ppermute | solution.py:168
  8.8 7.1 %collective-permute-start.1 = (bf16[16,2048]{1,0:T(8,128)(2,1)S(1)}, bf16[16,2048]{1,0:T(8,128)(2,1)S(1)}, u32[]{:S(2)}, u32[]{:S(2)}) collective-permute-start(bf16[16,2048]{1,0:T(8,128)(2,1)S(1)} %get-tuple-element.16.refs_0_), channel_id=1, source_target_pairs={{0,8},{4,12},{8,0},{12,4},{16,24},{20,28},{24,16},{28,20},{1,9},{5... | collective-permute-start | bytes 196616 | tf_op jit(solution)/shard_map/ppermute | solution.py:168
  9.4 7.0 %collective-permute-start = (bf16[16,2048]{1,0:T(8,128)(2,1)S(1)}, bf16[16,2048]{1,0:T(8,128)(2,1)S(1)}, u32[]{:S(2)}, u32[]{:S(2)}) collective-permute-start(bf16[16,2048]{1,0:T(8,128)(2,1)S(1)} %get-tuple-element.16.refs_0_), channel_id=1, source_target_pairs={{0,4},{4,0},{8,12},{12,8},{16,20},{20,16},{24,28},{28,24},{1,5},{5... | collective-permute-start | bytes 196616 | tf_op jit(solution)/shard_map/ppermute | solution.py:168
  11.3 5.1 %collective-permute-start.6 = (bf16[16,2048]{1,0:T(8,128)(2,1)S(1)}, bf16[16,2048]{1,0:T(8,128)(2,1)S(1)}, u32[]{:S(2)}, u32[]{:S(2)}) collective-permute-start(bf16[16,2048]{1,0:T(8,128)(2,1)S(1)} %collective-permute-done.5.refs_6_), channel_id=1, source_target_pairs={{0,4},{4,0},{8,12},{12,8},{16,20},{20,16},{24,28},{28,24},{1,5},{5... | collective-permute-start | bytes 196616 | tf_op jit(solution)/shard_map/ppermute | solution.py:168
  14.4 4.8 %collective-permute-start.4 = (bf16[16,2048]{1,0:T(8,128)(2,1)S(1)}, bf16[16,2048]{1,0:T(8,128)(2,1)S(1)}, u32[]{:S(2)}, u32[]{:S(2)}) collective-permute-start(bf16[16,2048]{1,0:T(8,128)(2,1)S(1)} %collective-permute-done.3.refs_4_), channel_id=1, source_target_pairs={{0,4},{4,0},{8,12},{12,8},{16,20},{20,16},{24,28},{28,24},{1,5},{5... | collective-permute-start | bytes 196616 | tf_op jit(solution)/shard_map/ppermute | solution.py:168
  15.9 4.3 %collective-permute-start.2 = (bf16[16,2048]{1,0:T(8,128)(2,1)S(1)}, bf16[16,2048]{1,0:T(8,128)(2,1)S(1)}, u32[]{:S(2)}, u32[]{:S(2)}) collective-permute-start(bf16[16,2048]{1,0:T(8,128)(2,1)S(1)} %collective-permute-done.1.refs_2_), channel_id=1, source_target_pairs={{0,4},{4,0},{8,12},{12,8},{16,20},{20,16},{24,28},{28,24},{1,5},{5... | collective-permute-start | bytes 196616 | tf_op jit(solution)/shard_map/ppermute | solution.py:168
  20.2 1.1 %copy-start = (bf16[2048,192]{0,1:T(8,128)(2,1)S(1)}, bf16[2048,192]{0,1:T(8,128)(2,1)}, u32[]{:S(2)}) copy-start(bf16[2048,192]{0,1:T(8,128)(2,1)} %param.13) | copy-start | bytes 2359300
  21.3 1.1 %copy-start.1 = (bf16[2048,192]{0,1:T(8,128)(2,1)S(1)}, bf16[2048,192]{0,1:T(8,128)(2,1)}, u32[]{:S(2)}) copy-start(bf16[2048,192]{0,1:T(8,128)(2,1)} %param.14) | copy-start | bytes 2359300
  22.4 1.1 %copy-start.2 = (bf16[192,2048]{1,0:T(8,128)(2,1)S(1)}, bf16[192,2048]{1,0:T(8,128)(2,1)}, u32[]{:S(2)}) copy-start(bf16[192,2048]{1,0:T(8,128)(2,1)} %refs_10_.1) | copy-start | bytes 2359300
  24.5 5.0 %collective-permute-start.8 = (bf16[16,2048]{1,0:T(8,128)(2,1)S(1)}, bf16[16,2048]{1,0:T(8,128)(2,1)S(1)}, u32[]{:S(2)}, u32[]{:S(2)}) collective-permute-start(bf16[16,2048]{1,0:T(8,128)(2,1)S(1)} %get-tuple-element.20), channel_id=1, source_target_pairs={{0,4},{4,0},{8,12},{12,8},{16,20},{20,16},{24,28},{28,24},{1,5},{5... | collective-permute-start | bytes 196616 | tf_op jit(solution)/shard_map/ppermute | solution.py:168
  25.5 8.8 %collective-permute-start.7 = (bf16[16,2048]{1,0:T(8,128)(2,1)S(1)}, bf16[16,2048]{1,0:T(8,128)(2,1)S(1)}, u32[]{:S(2)}, u32[]{:S(2)}) collective-permute-start(bf16[16,2048]{1,0:T(8,128)(2,1)S(1)} %get-tuple-element.18), channel_id=1, source_target_pairs={{0,4},{4,0},{8,12},{12,8},{16,20},{20,16},{24,28},{28,24},{1,5},{5... | collective-permute-start | bytes 196616 | tf_op jit(solution)/shard_map/ppermute | solution.py:168
  26.6 4.7 %collective-permute-start.10 = (bf16[16,2048]{1,0:T(8,128)(2,1)S(1)}, bf16[16,2048]{1,0:T(8,128)(2,1)S(1)}, u32[]{:S(2)}, u32[]{:S(2)}) collective-permute-start(bf16[16,2048]{1,0:T(8,128)(2,1)S(1)} %get-tuple-element.22), channel_id=1, source_target_pairs={{0,4},{4,0},{8,12},{12,8},{16,20},{20,16},{24,28},{28,24},{1,5},{5... | collective-permute-start | bytes 196616 | tf_op jit(solution)/shard_map/ppermute | solution.py:168
  27.5 4.7 %collective-permute-start.12 = (bf16[16,2048]{1,0:T(8,128)(2,1)S(1)}, bf16[16,2048]{1,0:T(8,128)(2,1)S(1)}, u32[]{:S(2)}, u32[]{:S(2)}) collective-permute-start(bf16[16,2048]{1,0:T(8,128)(2,1)S(1)} %get-tuple-element.24), channel_id=1, source_target_pairs={{0,4},{4,0},{8,12},{12,8},{16,20},{20,16},{24,28},{28,24},{1,5},{5... | collective-permute-start | bytes 196616 | tf_op jit(solution)/shard_map/ppermute | solution.py:168
  29.5 4.8 %collective-permute-start.9 = (bf16[16,2048]{1,0:T(8,128)(2,1)S(1)}, bf16[16,2048]{1,0:T(8,128)(2,1)S(1)}, u32[]{:S(2)}, u32[]{:S(2)}) collective-permute-start(bf16[16,2048]{1,0:T(8,128)(2,1)S(1)} %add_convert_fusion.2), channel_id=1, source_target_pairs={{0,8},{4,12},{8,0},{12,4},{16,24},{20,28},{24,16},{28,20},{1,9},{5... | collective-permute-start | bytes 196616 | tf_op jit(solution)/shard_map/ppermute | solution.py:168
  31.3 5.7 %collective-permute-start.11 = (bf16[16,2048]{1,0:T(8,128)(2,1)S(1)}, bf16[16,2048]{1,0:T(8,128)(2,1)S(1)}, u32[]{:S(2)}, u32[]{:S(2)}) collective-permute-start(bf16[16,2048]{1,0:T(8,128)(2,1)S(1)} %add_convert_fusion.1), channel_id=1, source_target_pairs={{0,16},{4,20},{8,24},{12,28},{16,0},{20,4},{24,8},{28,12},{1,17},{... | collective-permute-start | bytes 196616 | tf_op jit(solution)/shard_map/ppermute | solution.py:168
  32.3 6.2 %collective-permute-start.13 = (bf16[16,2048]{1,0:T(8,128)(2,1)S(1)}, bf16[16,2048]{1,0:T(8,128)(2,1)S(1)}, u32[]{:S(2)}, u32[]{:S(2)}) collective-permute-start(bf16[16,2048]{1,0:T(8,128)(2,1)S(1)} %add_convert_fusion), channel_id=1, source_target_pairs={{0,24},{4,28},{8,16},{12,20},{16,8},{20,12},{24,0},{28,4},{1,25},{... | collective-permute-start | bytes 196616 | tf_op jit(solution)/shard_map/ppermute | solution.py:168

commit v3 on v2

--- a/solution.py
+++ b/solution.py
@@ -10,6 +10,10 @@
 SLICES = 8
 CAP = 16
 VMEM_LIMIT = 40 * 1024 * 1024
+
+
+def in_hbm(array):
+    return pltpu.with_memory_space_constraint(array, pltpu.HBM)
 
 
 def pick_kernel(
@@ -68,29 +72,68 @@
         ],
         compiler_params=pltpu.CompilerParams(vmem_limit_bytes=VMEM_LIMIT),
         name="pick_rows",
-    )(live_counts, ids, gate_vals, tokens, gain)
+    )(live_counts, *(in_hbm(array) for array in (ids, gate_vals, tokens, gain)))
+
+
+def expert_rows(rows, gate_ref, up_ref, down_ref):
+    dims = (((1,), (1,)), ((), ()))
+    gate_act = lax.dot_general(rows, gate_ref[...], dims, preferred_element_type=jnp.float32)
+    up_act = lax.dot_general(rows, up_ref[...], dims, preferred_element_type=jnp.float32)
+    hidden = (jax.nn.silu(gate_act) * up_act).astype(jnp.bfloat16)
+    partial_out = jnp.dot(hidden, down_ref[...], preferred_element_type=jnp.float32)
+    return partial_out.astype(jnp.bfloat16)
+
+
+def expert_cost(rows, weights):
+    size = sum(weight.size for weight in weights)
+    return pl.CostEstimate(flops=2 * rows * size, bytes_accessed=2 * size, transcendentals=0)
+
+
+def first_kernel(rows_ref, gate_hbm, up_hbm, down_hbm, out_ref, gate_ref, up_ref, down_ref, sems):
+    copies = [
+        pltpu.make_async_copy(source, target, sems.at[i])
+        for i, (source, target) in enumerate(
+            ((gate_hbm, gate_ref), (up_hbm, up_ref), (down_hbm, down_ref))
+        )
+    ]
+    for copy in copies:
+        copy.start()
+    for copy in copies:
+        copy.wait()
+    out_ref[...] = expert_rows(rows_ref[...], gate_ref, up_ref, down_ref)
+
+
+def first_slice(rows, weights):
+    vmem = pl.BlockSpec(memory_space=pltpu.VMEM)
+    hbm = pl.BlockSpec(memory_space=pltpu.HBM)
+    return pl.pallas_call(
+        first_kernel,
+        out_shape=[jax.ShapeDtypeStruct(rows.shape, jnp.bfloat16)]
+        + [jax.ShapeDtypeStruct(weight.shape, weight.dtype) for weight in weights],
+        in_specs=[vmem, hbm, hbm, hbm],
+        out_specs=[vmem] * 4,
+        scratch_shapes=[pltpu.SemaphoreType.DMA((3,))],
+        compiler_params=pltpu.CompilerParams(vmem_limit_bytes=VMEM_LIMIT),
+        cost_estimate=expert_cost(rows.shape[0], weights),
+        name="first_slice",
+    )(rows, *(in_hbm(weight) for weight in weights))
 
 
 def expert_kernel(*refs):
     count = (len(refs) - 3) // 2
-    gate_ref, up_ref, down_ref = refs[count : count + 3]
-    dims = (((1,), (1,)), ((), ()))
+    weights = refs[count : count + 3]
     size = refs[0].shape[0]
     together = max(1, 128 // size)
     for first in range(0, count, together):
         last = min(count, first + together)
         rows = jnp.concatenate([ref[...] for ref in refs[first:last]], axis=0)
-        gate_act = lax.dot_general(rows, gate_ref[...], dims, preferred_element_type=jnp.float32)
-        up_act = lax.dot_general(rows, up_ref[...], dims, preferred_element_type=jnp.float32)
-        hidden = (jax.nn.silu(gate_act) * up_act).astype(jnp.bfloat16)
-        partial_out = jnp.dot(hidden, down_ref[...], preferred_element_type=jnp.float32)
-        partial_out = partial_out.astype(jnp.bfloat16)
+        partial_out = expert_rows(rows, *weights)
         for i in range(first, last):
             at = (i - first) * size
             refs[count + 3 + i][...] = partial_out[at : at + size]
 
 
-def expert_slice(blocks, gate_rows, up_rows, down_rows):
+def expert_slice(blocks, weights):
     vmem = pl.BlockSpec(memory_space=pltpu.VMEM)
     count = len(blocks)
     return pl.pallas_call(
@@ -99,8 +142,9 @@
         in_specs=[vmem] * (count + 3),
         out_specs=[vmem] * count,
         compiler_params=pltpu.CompilerParams(vmem_limit_bytes=VMEM_LIMIT),
+        cost_estimate=expert_cost(count * blocks[0].shape[0], weights),
         name="expert_slice",
-    )(*blocks, gate_rows, up_rows, down_rows)
+    )(*blocks, *weights)
 
 
 def add_level(kept, came):
@@ -182,9 +226,11 @@
         blocks[j] = swap(devices, j, own)
     for j in (2, 4, 6):
         blocks[j + 1] = swap(devices, 1, blocks[j])
-    partial_out = expert_slice(
-        [blocks[j] for j in range(SLICES)], w_gate.T, w_up.T, w_down
-    )
+    partial_out = {}
+    partial_out[0], *weights = first_slice(own, (w_gate.T, w_up.T, w_down))
+    for group in ((1, 2, 4, 6), (3, 5, 7)):
+        outs = expert_slice([blocks[j] for j in group], weights)
+        partial_out.update(zip(group, outs))
     level = {}
     for j in (6, 4, 2, 0):
         level[j] = add_level(partial_out[j], swap(devices, 1, partial_out[j + 1]))

time: 39.9 us -> 36.1 us (0.905)
  local copies, waits for them, and re-layouts: 5.84 us -> 0 us
  Pallas kernels: 2.47 us -> 6.46 us
  waiting for transfers between devices: 11.9 us -> 8.78 us
  starting transfers between devices: 18.5 us -> 19.8 us
    unnamed x14 -> x0, local copies, waits for them, and re-layouts: 5.84 us -> none
    ppermute x14, waiting for transfers between devices: 11.9 us -> 8.78 us  [swap(): lax.ppermute(block, 'ep', [(i, i ^ distance) for i in range(devices)])]
    pallas_call x0 -> x1, Pallas kernels: none -> 2.35 us  [first_slice(): pl.pallas_call(first_kernel, out_shape=[jax.ShapeDtypeStruct(rows.shape,...]
    ppermute x14, starting transfers between devices: 18.5 us -> 19.8 us  [swap(): lax.ppermute(block, 'ep', [(i, i ^ distance) for i in range(devices)])]
    pallas_call x1, Pallas kernels: 0.53 us -> 1.39 us  [pick_rows(): pl.pallas_call(pick_kernel, out_shape=(jax.ShapeDtypeStruct((slots, token...]
    pallas_call x1 -> x2, Pallas kernels: 0.89 us -> 1.68 us  [expert_slice(): pl.pallas_call(expert_kernel, out_shape=[jax.ShapeDtypeStruct(block.shape...]
  transfers between devices with their start and end apart: 14 -> 14, of which waited for: 8 -> 4; matrix products, arithmetic and copies ran while one was open for 0% -> 0% of each run, Pallas kernels for 0% -> 11%
where the time goes in v3:
time: 36.1 us; the launch traced here: 35.9 us
  starting transfers between devices  19.8 us (55%)
  waiting for transfers between devices  8.78 us (24%)
  Pallas kernels  6.46 us (18%)
  between operations  0.75 us (2%)
    ppermute x14, starting transfers between devices, swap(): lax.ppermute(block, 'ep', [(i, i ^ distance) for i in range(devices)])  19.8 us
    ppermute x14, waiting for transfers between devices, swap(): lax.ppermute(block, 'ep', [(i, i ^ distance) for i in range(devices)])  8.78 us
    pallas_call x1, Pallas kernels, first_slice(): pl.pallas_call(first_kernel, out_shape=[jax.ShapeDtypeStruct(rows.shape,...  2.35 us
    pallas_call x2, Pallas kernels, expert_slice(): pl.pallas_call(expert_kernel, out_shape=[jax.ShapeDtypeStruct(block.shape...  1.68 us
    pallas_call x1, Pallas kernels, pick_rows(): pl.pallas_call(pick_kernel, out_shape=(jax.ShapeDtypeStruct((slots, token...  1.39 us
    pallas_call x1, Pallas kernels, combine(): pl.pallas_call(combine_kernel, out_shape=jax.ShapeDtypeStruct(shape, jnp....  1.04 us
  transfers between devices with their start and end apart: 14, of which 4 were waited for; matrix products, arithmetic and copies ran while one was open for 0% of the time, Pallas kernels for 11%

profile of v3, /device:TPU:0, one launch (start us, length us, event | category | flops | bytes accessed | tf_op | source)
XLA Modules:
  0.0 35.9 jit_solution(17742099409716106001)
XLA Ops:
  0.7 1.4 %pick_rows.1 = (bf16[16,2048]{1,0:T(8,128)(2,1)S(1)}, f32[16,128]{1,0:T(8,128)S(1)}) custom-call(s32[1]{0:T(128)S(6)} %copy.9.live_ref, s32[8,128]{1,0:T(8,128)} %bitcast.8, f32[8,128]{1,0:T(8,128)} %bitcast.9, bf16[128,2048]{1,0:T(8,128)(2,1)} %tokens_hbm.1, f32[1,2048]{1,0:T(1,128)} %bitcast.7), custom_call_target="tpu_custom_call" | custom-call | tf_op jit(solution)/shard_map/pick_rows/pallas_call | solution.py:58
  2.0 3.1 %collective-permute-start.1 = (bf16[16,2048]{1,0:T(8,128)(2,1)S(1)}, bf16[16,2048]{1,0:T(8,128)(2,1)S(1)}, u32[]{:S(2)}, u32[]{:S(2)}) collective-permute-start(bf16[16,2048]{1,0:T(8,128)(2,1)S(1)} %get-tuple-element.19.rows_ref), channel_id=1, source_target_pairs={{0,8},{4,12},{8,0},{12,4},{16,24},{20,28},{24,16},{28,20},{1,9},{5... | collective-permute-start | bytes 196616 | tf_op jit(solution)/shard_map/ppermute | solution.py:212
  5.1 2.6 %collective-permute-start.2 = (bf16[16,2048]{1,0:T(8,128)(2,1)S(1)}, bf16[16,2048]{1,0:T(8,128)(2,1)S(1)}, u32[]{:S(2)}, u32[]{:S(2)}) collective-permute-start(bf16[16,2048]{1,0:T(8,128)(2,1)S(1)} %get-tuple-element.19.rows_ref), channel_id=1, source_target_pairs={{0,16},{4,20},{8,24},{12,28},{16,0},{20,4},{24,8},{28,12},{1,17},{... | collective-permute-start | bytes 196616 | tf_op jit(solution)/shard_map/ppermute | solution.py:212
  7.7 0.0 collective-permute-start.3
  7.7 0.0 collective-permute-done.1.refs_1_
  7.7 1.7 %collective-permute-start.5 = (bf16[16,2048]{1,0:T(8,128)(2,1)S(1)}, bf16[16,2048]{1,0:T(8,128)(2,1)S(1)}, u32[]{:S(2)}, u32[]{:S(2)}) collective-permute-start(bf16[16,2048]{1,0:T(8,128)(2,1)S(1)} %collective-permute-done.1.refs_1_), channel_id=1, source_target_pairs={{0,4},{4,0},{8,12},{12,8},{16,20},{20,16},{24,28},{28,24},{1,5},{5... | collective-permute-start | bytes 196616 | tf_op jit(solution)/shard_map/ppermute | solution.py:212
  9.5 2.9 %collective-permute-done.2.refs_2_ = bf16[16,2048]{1,0:T(8,128)(2,1)S(1)} collective-permute-done((bf16[16,2048]{1,0:T(8,128)(2,1)S(1)}, bf16[16,2048]{1,0:T(8,128)(2,1)S(1)}, u32[]{:S(2)}, u32[]{:S(2)}) %collective-permute-start.2) | collective-permute-done | bytes 65568 | tf_op jit(solution)/shard_map/ppermute | solution.py:212
  12.4 1.5 %collective-permute-start.6 = (bf16[16,2048]{1,0:T(8,128)(2,1)S(1)}, bf16[16,2048]{1,0:T(8,128)(2,1)S(1)}, u32[]{:S(2)}, u32[]{:S(2)}) collective-permute-start(bf16[16,2048]{1,0:T(8,128)(2,1)S(1)} %collective-permute-done.2.refs_2_), channel_id=1, source_target_pairs={{0,4},{4,0},{8,12},{12,8},{16,20},{20,16},{24,28},{28,24},{1,5},{5... | collective-permute-start | bytes 196616 | tf_op jit(solution)/shard_map/ppermute | solution.py:212
  13.9 0.0 collective-permute-done.3.refs_3_
  13.9 1.4 %collective-permute-start.7 = (bf16[16,2048]{1,0:T(8,128)(2,1)S(1)}, bf16[16,2048]{1,0:T(8,128)(2,1)S(1)}, u32[]{:S(2)}, u32[]{:S(2)}) collective-permute-start(bf16[16,2048]{1,0:T(8,128)(2,1)S(1)} %collective-permute-done.3.refs_3_), channel_id=1, source_target_pairs={{0,4},{4,0},{8,12},{12,8},{16,20},{20,16},{24,28},{28,24},{1,5},{5... | collective-permute-start | bytes 196616 | tf_op jit(solution)/shard_map/ppermute | solution.py:212
  15.3 0.6 %collective-permute-start = (bf16[16,2048]{1,0:T(8,128)(2,1)S(1)}, bf16[16,2048]{1,0:T(8,128)(2,1)S(1)}, u32[]{:S(2)}, u32[]{:S(2)}) collective-permute-start(bf16[16,2048]{1,0:T(8,128)(2,1)S(1)} %get-tuple-element.19.rows_ref), channel_id=1, source_target_pairs={{0,4},{4,0},{8,12},{12,8},{16,20},{20,16},{24,28},{28,24},{1,5},{5... | collective-permute-start | bytes 196616 | tf_op jit(solution)/shard_map/ppermute | solution.py:212
  15.9 2.4 %first_slice.1 = (bf16[16,2048]{1,0:T(8,128)(2,1)S(1)}, bf16[192,2048]{1,0:T(8,128)(2,1)S(1)}, bf16[192,2048]{1,0:T(8,128)(2,1)S(1)}, bf16[192,2048]{1,0:T(8,128)(2,1)S(1)}) custom-call(bf16[16,2048]{1,0:T(8,128)(2,1)S(1)} %get-tuple-element.19.rows_ref, bf16[192,2048]{1,0:T(8,128)(2,1)} %bitcast.5, bf16[192,2048]{1,0:T(8,128)(2,1)} %bitcast.6, ...), custom_call_target="tpu_custom_call" | custom-call | flops 37748736 | bytes 2359296 | tf_op jit(solution)/shard_map/first_slice/pallas_call | solution.py:109
  18.3 0.0 collective-permute-done.5.refs_0_
  18.3 0.0 collective-permute-done.6.refs_1_
  18.3 0.0 collective-permute-done.7.refs_2_
  18.3 0.8 %expert_slice.3 = (bf16[16,2048]{1,0:T(8,128)(2,1)S(1)}, bf16[16,2048]{1,0:T(8,128)(2,1)S(1)}, bf16[16,2048]{1,0:T(8,128)(2,1)S(1)}) custom-call(bf16[16,2048]{1,0:T(8,128)(2,1)S(1)} %collective-permute-done.5.refs_0_, bf16[16,2048]{1,0:T(8,128)(2,1)S(1)} %collective-permute-done.6.refs_1_, bf16[16,2048]{1,0:T(8,128)(2,1)S(1)} %collective-permute-done.7.refs_2_, ...), custom_call_target="tpu_custom_call" | custom-call | flops 113246208 | bytes 2359296 | tf_op jit(solution)/shard_map/expert_slice/pallas_call | solution.py:139
  19.2 1.5 %collective-permute-start.8 = (bf16[16,2048]{1,0:T(8,128)(2,1)S(1)}, bf16[16,2048]{1,0:T(8,128)(2,1)S(1)}, u32[]{:S(2)}, u32[]{:S(2)}) collective-permute-start(bf16[16,2048]{1,0:T(8,128)(2,1)S(1)} %get-tuple-element.26), channel_id=1, source_target_pairs={{0,4},{4,0},{8,12},{12,8},{16,20},{20,16},{24,28},{28,24},{1,5},{5... | collective-permute-start | bytes 196616 | tf_op jit(solution)/shard_map/ppermute | solution.py:212
  20.6 0.0 collective-permute-done.refs_0_
  20.6 0.8 %expert_slice.2 = (bf16[16,2048]{1,0:T(8,128)(2,1)S(1)}, bf16[16,2048]{1,0:T(8,128)(2,1)S(1)}, bf16[16,2048]{1,0:T(8,128)(2,1)S(1)}, bf16[16,2048]{1,0:T(8,128)(2,1)S(1)}) custom-call(bf16[16,2048]{1,0:T(8,128)(2,1)S(1)} %collective-permute-done.refs_0_, bf16[16,2048]{1,0:T(8,128)(2,1)S(1)} %collective-permute-done.1.refs_1_, ...), custom_call_target="tpu_custom_call" | custom-call | flops 150994944 | bytes 2359296 | tf_op jit(solution)/shard_map/expert_slice/pallas_call | solution.py:139
  21.5 0.7 %collective-permute-start.4 = (bf16[16,2048]{1,0:T(8,128)(2,1)S(1)}, bf16[16,2048]{1,0:T(8,128)(2,1)S(1)}, u32[]{:S(2)}, u32[]{:S(2)}) collective-permute-start(bf16[16,2048]{1,0:T(8,128)(2,1)S(1)} %get-tuple-element.24), channel_id=1, source_target_pairs={{0,4},{4,0},{8,12},{12,8},{16,20},{20,16},{24,28},{28,24},{1,5},{5... | collective-permute-start | bytes 196616 | tf_op jit(solution)/shard_map/ppermute | solution.py:212
  22.2 1.4 %collective-permute-start.10 = (bf16[16,2048]{1,0:T(8,128)(2,1)S(1)}, bf16[16,2048]{1,0:T(8,128)(2,1)S(1)}, u32[]{:S(2)}, u32[]{:S(2)}) collective-permute-start(bf16[16,2048]{1,0:T(8,128)(2,1)S(1)} %get-tuple-element.28), channel_id=1, source_target_pairs={{0,4},{4,0},{8,12},{12,8},{16,20},{20,16},{24,28},{28,24},{1,5},{5... | collective-permute-start | bytes 196616 | tf_op jit(solution)/shard_map/ppermute | solution.py:212
  23.6 0.6 %collective-permute-start.12 = (bf16[16,2048]{1,0:T(8,128)(2,1)S(1)}, bf16[16,2048]{1,0:T(8,128)(2,1)S(1)}, u32[]{:S(2)}, u32[]{:S(2)}) collective-permute-start(bf16[16,2048]{1,0:T(8,128)(2,1)S(1)} %get-tuple-element.30), channel_id=1, source_target_pairs={{0,4},{4,0},{8,12},{12,8},{16,20},{20,16},{24,28},{28,24},{1,5},{5... | collective-permute-start | bytes 196616 | tf_op jit(solution)/shard_map/ppermute | solution.py:212
  24.2 0.0 collective-permute-done.8
  24.3 0.4 %collective-permute-start.9 = (bf16[16,2048]{1,0:T(8,128)(2,1)S(1)}, bf16[16,2048]{1,0:T(8,128)(2,1)S(1)}, u32[]{:S(2)}, u32[]{:S(2)}) collective-permute-start(bf16[16,2048]{1,0:T(8,128)(2,1)S(1)} %add_convert_fusion.2), channel_id=1, source_target_pairs={{0,8},{4,12},{8,0},{12,4},{16,24},{20,28},{24,16},{28,20},{1,9},{5... | collective-permute-start | bytes 196616 | tf_op jit(solution)/shard_map/ppermute | solution.py:212
  24.7 1.9 %collective-permute-done.10 = bf16[16,2048]{1,0:T(8,128)(2,1)S(1)} collective-permute-done((bf16[16,2048]{1,0:T(8,128)(2,1)S(1)}, bf16[16,2048]{1,0:T(8,128)(2,1)S(1)}, u32[]{:S(2)}, u32[]{:S(2)}) %collective-permute-start.10) | collective-permute-done | bytes 65568 | tf_op jit(solution)/shard_map/ppermute | solution.py:212
  26.6 2.0 %collective-permute-start.11 = (bf16[16,2048]{1,0:T(8,128)(2,1)S(1)}, bf16[16,2048]{1,0:T(8,128)(2,1)S(1)}, u32[]{:S(2)}, u32[]{:S(2)}) collective-permute-start(bf16[16,2048]{1,0:T(8,128)(2,1)S(1)} %add_convert_fusion.1), channel_id=1, source_target_pairs={{0,16},{4,20},{8,24},{12,28},{16,0},{20,4},{24,8},{28,12},{1,17},{... | collective-permute-start | bytes 196616 | tf_op jit(solution)/shard_map/ppermute | solution.py:212
  28.6 0.0 collective-permute-done.12
  28.6 2.3 %collective-permute-start.13 = (bf16[16,2048]{1,0:T(8,128)(2,1)S(1)}, bf16[16,2048]{1,0:T(8,128)(2,1)S(1)}, u32[]{:S(2)}, u32[]{:S(2)}) collective-permute-start(bf16[16,2048]{1,0:T(8,128)(2,1)S(1)} %add_convert_fusion), channel_id=1, source_target_pairs={{0,24},{4,28},{8,16},{12,20},{16,8},{20,12},{24,0},{28,4},{1,25},{... | collective-permute-start | bytes 196616 | tf_op jit(solution)/shard_map/ppermute | solution.py:212
  30.9 0.0 collective-permute-done.4
  30.9 0.0 collective-permute-done.9.refs_1_
  30.9 0.9 %collective-permute-done.11.refs_2_ = bf16[16,2048]{1,0:T(8,128)(2,1)S(1)} collective-permute-done((bf16[16,2048]{1,0:T(8,128)(2,1)S(1)}, bf16[16,2048]{1,0:T(8,128)(2,1)S(1)}, u32[]{:S(2)}, u32[]{:S(2)}) %collective-permute-start.11) | collective-permute-done | bytes 65568 | tf_op jit(solution)/shard_map/ppermute | solution.py:212
  31.8 3.1 %collective-permute-done.13.refs_3_ = bf16[16,2048]{1,0:T(8,128)(2,1)S(1)} collective-permute-done((bf16[16,2048]{1,0:T(8,128)(2,1)S(1)}, bf16[16,2048]{1,0:T(8,128)(2,1)S(1)}, u32[]{:S(2)}, u32[]{:S(2)}) %collective-permute-start.13) | collective-permute-done | bytes 65568 | tf_op jit(solution)/shard_map/ppermute | solution.py:212
  34.9 1.0 %combine.1 = bf16[128,2048]{1,0:T(8,128)(2,1)} custom-call(f32[16,128]{1,0:T(8,128)S(1)} %get-tuple-element.18.table_ref, bf16[16,2048]{1,0:T(8,128)(2,1)S(1)} %add_convert_fusion.3.refs_0_, bf16[16,2048]{1,0:T(8,128)(2,1)S(1)} %collective-permute-done.9.refs_1_, bf16[16,2048]{1,0:T(8,128)(2,1)S(1)} %collective-permute-done.11.refs_2_, ...), custom_call_target="tpu_custom_call" | custom-call | tf_op jit(solution)/shard_map/combine/pallas_call | solution.py:191
  (4 shorter events, 0.1 us)
Async XLA Ops:
  2.0 5.7 %collective-permute-start.1 = (bf16[16,2048]{1,0:T(8,128)(2,1)S(1)}, bf16[16,2048]{1,0:T(8,128)(2,1)S(1)}, u32[]{:S(2)}, u32[]{:S(2)}) collective-permute-start(bf16[16,2048]{1,0:T(8,128)(2,1)S(1)} %get-tuple-element.19.rows_ref), channel_id=1, source_target_pairs={{0,8},{4,12},{8,0},{12,4},{16,24},{20,28},{24,16},{28,20},{1,9},{5... | collective-permute-start | bytes 196616 | tf_op jit(solution)/shard_map/ppermute | solution.py:212
  5.1 7.3 %collective-permute-start.2 = (bf16[16,2048]{1,0:T(8,128)(2,1)S(1)}, bf16[16,2048]{1,0:T(8,128)(2,1)S(1)}, u32[]{:S(2)}, u32[]{:S(2)}) collective-permute-start(bf16[16,2048]{1,0:T(8,128)(2,1)S(1)} %get-tuple-element.19.rows_ref), channel_id=1, source_target_pairs={{0,16},{4,20},{8,24},{12,28},{16,0},{20,4},{24,8},{28,12},{1,17},{... | collective-permute-start | bytes 196616 | tf_op jit(solution)/shard_map/ppermute | solution.py:212
  7.7 6.2 %collective-permute-start.3 = (bf16[16,2048]{1,0:T(8,128)(2,1)S(1)}, bf16[16,2048]{1,0:T(8,128)(2,1)S(1)}, u32[]{:S(2)}, u32[]{:S(2)}) collective-permute-start(bf16[16,2048]{1,0:T(8,128)(2,1)S(1)} %get-tuple-element.19.rows_ref), channel_id=1, source_target_pairs={{0,24},{4,28},{8,16},{12,20},{16,8},{20,12},{24,0},{28,4},{1,25},{... | collective-permute-start | bytes 196616 | tf_op jit(solution)/shard_map/ppermute | solution.py:212
  7.7 10.6 %collective-permute-start.5 = (bf16[16,2048]{1,0:T(8,128)(2,1)S(1)}, bf16[16,2048]{1,0:T(8,128)(2,1)S(1)}, u32[]{:S(2)}, u32[]{:S(2)}) collective-permute-start(bf16[16,2048]{1,0:T(8,128)(2,1)S(1)} %collective-permute-done.1.refs_1_), channel_id=1, source_target_pairs={{0,4},{4,0},{8,12},{12,8},{16,20},{20,16},{24,28},{28,24},{1,5},{5... | collective-permute-start | bytes 196616 | tf_op jit(solution)/shard_map/ppermute | solution.py:212
  12.4 5.9 %collective-permute-start.6 = (bf16[16,2048]{1,0:T(8,128)(2,1)S(1)}, bf16[16,2048]{1,0:T(8,128)(2,1)S(1)}, u32[]{:S(2)}, u32[]{:S(2)}) collective-permute-start(bf16[16,2048]{1,0:T(8,128)(2,1)S(1)} %collective-permute-done.2.refs_2_), channel_id=1, source_target_pairs={{0,4},{4,0},{8,12},{12,8},{16,20},{20,16},{24,28},{28,24},{1,5},{5... | collective-permute-start | bytes 196616 | tf_op jit(solution)/shard_map/ppermute | solution.py:212
  13.9 4.4 %collective-permute-start.7 = (bf16[16,2048]{1,0:T(8,128)(2,1)S(1)}, bf16[16,2048]{1,0:T(8,128)(2,1)S(1)}, u32[]{:S(2)}, u32[]{:S(2)}) collective-permute-start(bf16[16,2048]{1,0:T(8,128)(2,1)S(1)} %collective-permute-done.3.refs_3_), channel_id=1, source_target_pairs={{0,4},{4,0},{8,12},{12,8},{16,20},{20,16},{24,28},{28,24},{1,5},{5... | collective-permute-start | bytes 196616 | tf_op jit(solution)/shard_map/ppermute | solution.py:212
  15.3 5.3 %collective-permute-start = (bf16[16,2048]{1,0:T(8,128)(2,1)S(1)}, bf16[16,2048]{1,0:T(8,128)(2,1)S(1)}, u32[]{:S(2)}, u32[]{:S(2)}) collective-permute-start(bf16[16,2048]{1,0:T(8,128)(2,1)S(1)} %get-tuple-element.19.rows_ref), channel_id=1, source_target_pairs={{0,4},{4,0},{8,12},{12,8},{16,20},{20,16},{24,28},{28,24},{1,5},{5... | collective-permute-start | bytes 196616 | tf_op jit(solution)/shard_map/ppermute | solution.py:212
  19.2 5.1 %collective-permute-start.8 = (bf16[16,2048]{1,0:T(8,128)(2,1)S(1)}, bf16[16,2048]{1,0:T(8,128)(2,1)S(1)}, u32[]{:S(2)}, u32[]{:S(2)}) collective-permute-start(bf16[16,2048]{1,0:T(8,128)(2,1)S(1)} %get-tuple-element.26), channel_id=1, source_target_pairs={{0,4},{4,0},{8,12},{12,8},{16,20},{20,16},{24,28},{28,24},{1,5},{5... | collective-permute-start | bytes 196616 | tf_op jit(solution)/shard_map/ppermute | solution.py:212
  21.5 9.4 %collective-permute-start.4 = (bf16[16,2048]{1,0:T(8,128)(2,1)S(1)}, bf16[16,2048]{1,0:T(8,128)(2,1)S(1)}, u32[]{:S(2)}, u32[]{:S(2)}) collective-permute-start(bf16[16,2048]{1,0:T(8,128)(2,1)S(1)} %get-tuple-element.24), channel_id=1, source_target_pairs={{0,4},{4,0},{8,12},{12,8},{16,20},{20,16},{24,28},{28,24},{1,5},{5... | collective-permute-start | bytes 196616 | tf_op jit(solution)/shard_map/ppermute | solution.py:212
  22.2 4.3 %collective-permute-start.10 = (bf16[16,2048]{1,0:T(8,128)(2,1)S(1)}, bf16[16,2048]{1,0:T(8,128)(2,1)S(1)}, u32[]{:S(2)}, u32[]{:S(2)}) collective-permute-start(bf16[16,2048]{1,0:T(8,128)(2,1)S(1)} %get-tuple-element.28), channel_id=1, source_target_pairs={{0,4},{4,0},{8,12},{12,8},{16,20},{20,16},{24,28},{28,24},{1,5},{5... | collective-permute-start | bytes 196616 | tf_op jit(solution)/shard_map/ppermute | solution.py:212
  23.6 5.0 %collective-permute-start.12 = (bf16[16,2048]{1,0:T(8,128)(2,1)S(1)}, bf16[16,2048]{1,0:T(8,128)(2,1)S(1)}, u32[]{:S(2)}, u32[]{:S(2)}) collective-permute-start(bf16[16,2048]{1,0:T(8,128)(2,1)S(1)} %get-tuple-element.30), channel_id=1, source_target_pairs={{0,4},{4,0},{8,12},{12,8},{16,20},{20,16},{24,28},{28,24},{1,5},{5... | collective-permute-start | bytes 196616 | tf_op jit(solution)/shard_map/ppermute | solution.py:212
  24.3 6.6 %collective-permute-start.9 = (bf16[16,2048]{1,0:T(8,128)(2,1)S(1)}, bf16[16,2048]{1,0:T(8,128)(2,1)S(1)}, u32[]{:S(2)}, u32[]{:S(2)}) collective-permute-start(bf16[16,2048]{1,0:T(8,128)(2,1)S(1)} %add_convert_fusion.2), channel_id=1, source_target_pairs={{0,8},{4,12},{8,0},{12,4},{16,24},{20,28},{24,16},{28,20},{1,9},{5... | collective-permute-start | bytes 196616 | tf_op jit(solution)/shard_map/ppermute | solution.py:212
  26.6 5.2 %collective-permute-start.11 = (bf16[16,2048]{1,0:T(8,128)(2,1)S(1)}, bf16[16,2048]{1,0:T(8,128)(2,1)S(1)}, u32[]{:S(2)}, u32[]{:S(2)}) collective-permute-start(bf16[16,2048]{1,0:T(8,128)(2,1)S(1)} %add_convert_fusion.1), channel_id=1, source_target_pairs={{0,16},{4,20},{8,24},{12,28},{16,0},{20,4},{24,8},{28,12},{1,17},{... | collective-permute-start | bytes 196616 | tf_op jit(solution)/shard_map/ppermute | solution.py:212
  28.6 6.2 %collective-permute-start.13 = (bf16[16,2048]{1,0:T(8,128)(2,1)S(1)}, bf16[16,2048]{1,0:T(8,128)(2,1)S(1)}, u32[]{:S(2)}, u32[]{:S(2)}) collective-permute-start(bf16[16,2048]{1,0:T(8,128)(2,1)S(1)} %add_convert_fusion), channel_id=1, source_target_pairs={{0,24},{4,28},{8,16},{12,20},{16,8},{20,12},{24,0},{28,4},{1,25},{... | collective-permute-start | bytes 196616 | tf_op jit(solution)/shard_map/ppermute | solution.py:212

commit v4 on v3

--- a/solution.py
+++ b/solution.py
@@ -10,6 +10,8 @@
 SLICES = 8
 CAP = 16
 VMEM_LIMIT = 40 * 1024 * 1024
+WEIGHT_CHUNKS = 4
+TOKEN_CHUNKS = 4
 
 
 def in_hbm(array):
@@ -19,13 +21,14 @@
 def pick_kernel(
     live_ref, ids_hbm, gate_hbm, tokens_hbm, gain_hbm, rows_ref, table_ref, ids_ref, gate_ref, tokens_ref, gain_ref, sems
 ):
-    copies = [
-        pltpu.make_async_copy(source, target, sems.at[i])
+    ids_copy, gate_copy, gain_copy = (
+        pltpu.make_async_copy(source, target, sems.at[TOKEN_CHUNKS + i])
         for i, (source, target) in enumerate(
-            ((ids_hbm, ids_ref), (tokens_hbm, tokens_ref), (gate_hbm, gate_ref), (gain_hbm, gain_ref))
+            ((ids_hbm, ids_ref), (gate_hbm, gate_ref), (gain_hbm, gain_ref))
         )
-    ]
-    for copy in copies:
+    )
+    token_copies = list(chunk_copies(tokens_hbm, tokens_ref, TOKEN_CHUNKS, sems))
+    for copy in (ids_copy, *token_copies, gain_copy, gate_copy):
         copy.start()
     slots, tok_rows = table_ref.shape
     slot = lax.broadcasted_iota(jnp.int32, (slots, tok_rows), 0)
@@ -35,17 +38,18 @@
     before = lax.broadcasted_iota(jnp.int32, (tok_rows, tok_rows), 0)
     after = lax.broadcasted_iota(jnp.int32, (tok_rows, tok_rows), 1)
     earlier = jnp.where(before < after, 1.0, 0.0).astype(jnp.bfloat16)
-    copies[0].wait()
+    ids_copy.wait()
     hits = [(ids_ref[k : k + 1, :] == expert) & live for k in range(ids_ref.shape[0])]
     chosen = jnp.where(functools.reduce(jnp.logical_or, hits), 1.0, 0.0)
     rank = jnp.dot(chosen.astype(jnp.bfloat16), earlier, preferred_element_type=jnp.float32)
     pick = jnp.where((chosen > 0.0) & (rank.astype(jnp.int32) == place), 1.0, 0.0)
-    copies[1].wait()
+    for copy in token_copies:
+        copy.wait()
     values = jnp.dot(pick.astype(jnp.bfloat16), tokens_ref[...], preferred_element_type=jnp.float32)
     mean_sq = jnp.mean(values * values, axis=-1, keepdims=True)
-    copies[2].wait()
-    copies[3].wait()
+    gain_copy.wait()
     rows_ref[...] = (values * lax.rsqrt(mean_sq + 1e-06) * gain_ref[...]).astype(jnp.bfloat16)
+    gate_copy.wait()
     weight = jnp.zeros((slots, tok_rows), jnp.float32)
     for k, hit in enumerate(hits):
         weight = jnp.where(hit, gate_ref[k : k + 1, :], weight)
@@ -68,7 +72,7 @@
             pltpu.VMEM(gate_vals.shape, gate_vals.dtype),
             pltpu.VMEM(tokens.shape, tokens.dtype),
             pltpu.VMEM(gain.shape, gain.dtype),
-            pltpu.SemaphoreType.DMA((4,)),
+            pltpu.SemaphoreType.DMA((TOKEN_CHUNKS + 3,)),
         ],
         compiler_params=pltpu.CompilerParams(vmem_limit_bytes=VMEM_LIMIT),
         name="pick_rows",
@@ -84,66 +88,80 @@
     return partial_out.astype(jnp.bfloat16)
 
 
-def expert_cost(rows, weights):
+def expert_blocks(ins, weights, outs):
+    together = max(1, 128 // ins[0].shape[0])
+    for first in range(0, len(ins), together):
+        some = ins[first : first + together]
+        partial_out = expert_rows(jnp.concatenate([ref[...] for ref in some], axis=0), *weights)
+        at = 0
+        for ref in outs[first : first + together]:
+            ref[...] = partial_out[at : at + ref.shape[0]]
+            at += ref.shape[0]
+
+
+def expert_cost(blocks, weights):
     size = sum(weight.size for weight in weights)
+    rows = sum(block.shape[0] for block in blocks)
     return pl.CostEstimate(flops=2 * rows * size, bytes_accessed=2 * size, transcendentals=0)
 
 
-def first_kernel(rows_ref, gate_hbm, up_hbm, down_hbm, out_ref, gate_ref, up_ref, down_ref, sems):
+def chunk_copies(source, target, chunks, sems):
+    rows = source.shape[0] // chunks
+    for i in range(chunks):
+        at = pl.ds(i * rows, rows)
+        yield pltpu.make_async_copy(source.at[at], target.at[at], sems.at[i])
+
+
+def first_kernel(*refs):
+    *refs, sems = refs
+    count = (len(refs) - 6) // 2
+    ins, sources = refs[:count], refs[count : count + 3]
+    outs, weights = refs[count + 3 : 2 * count + 3], refs[2 * count + 3 :]
     copies = [
-        pltpu.make_async_copy(source, target, sems.at[i])
-        for i, (source, target) in enumerate(
-            ((gate_hbm, gate_ref), (up_hbm, up_ref), (down_hbm, down_ref))
-        )
+        copy
+        for i, pair in enumerate(zip(sources, weights))
+        for copy in chunk_copies(*pair, WEIGHT_CHUNKS, sems.at[i])
     ]
     for copy in copies:
         copy.start()
     for copy in copies:
         copy.wait()
-    out_ref[...] = expert_rows(rows_ref[...], gate_ref, up_ref, down_ref)
-
-
-def first_slice(rows, weights):
+    expert_blocks(ins, weights, outs)
+
+
+def first_slice(blocks, weights):
     vmem = pl.BlockSpec(memory_space=pltpu.VMEM)
     hbm = pl.BlockSpec(memory_space=pltpu.HBM)
-    return pl.pallas_call(
+    count = len(blocks)
+    outs = pl.pallas_call(
         first_kernel,
-        out_shape=[jax.ShapeDtypeStruct(rows.shape, jnp.bfloat16)]
-        + [jax.ShapeDtypeStruct(weight.shape, weight.dtype) for weight in weights],
-        in_specs=[vmem, hbm, hbm, hbm],
-        out_specs=[vmem] * 4,
-        scratch_shapes=[pltpu.SemaphoreType.DMA((3,))],
-        compiler_params=pltpu.CompilerParams(vmem_limit_bytes=VMEM_LIMIT),
-        cost_estimate=expert_cost(rows.shape[0], weights),
+        out_shape=[jax.ShapeDtypeStruct(array.shape, array.dtype) for array in (*blocks, *weights)],
+        in_specs=[vmem] * count + [hbm] * 3,
+        out_specs=[vmem] * (count + 3),
+        scratch_shapes=[pltpu.SemaphoreType.DMA((3, WEIGHT_CHUNKS))],
+        compiler_params=pltpu.CompilerParams(vmem_limit_bytes=VMEM_LIMIT),
+        cost_estimate=expert_cost(blocks, weights),
         name="first_slice",
-    )(rows, *(in_hbm(weight) for weight in weights))
-
-
-def expert_kernel(*refs):
+    )(*blocks, *(in_hbm(weight) for weight in weights))
+    return outs[:count], outs[count:]
+
+
+def last_kernel(*refs):
     count = (len(refs) - 3) // 2
-    weights = refs[count : count + 3]
-    size = refs[0].shape[0]
-    together = max(1, 128 // size)
-    for first in range(0, count, together):
-        last = min(count, first + together)
-        rows = jnp.concatenate([ref[...] for ref in refs[first:last]], axis=0)
-        partial_out = expert_rows(rows, *weights)
-        for i in range(first, last):
-            at = (i - first) * size
-            refs[count + 3 + i][...] = partial_out[at : at + size]
-
-
-def expert_slice(blocks, weights):
+    expert_blocks(refs[:count], refs[count : count + 3], refs[count + 3 :])
+
+
+def last_slice(blocks, weights):
     vmem = pl.BlockSpec(memory_space=pltpu.VMEM)
     count = len(blocks)
     return pl.pallas_call(
-        expert_kernel,
+        last_kernel,
         out_shape=[jax.ShapeDtypeStruct(block.shape, jnp.bfloat16) for block in blocks],
         in_specs=[vmem] * (count + 3),
         out_specs=[vmem] * count,
         compiler_params=pltpu.CompilerParams(vmem_limit_bytes=VMEM_LIMIT),
-        cost_estimate=expert_cost(count * blocks[0].shape[0], weights),
-        name="expert_slice",
+        cost_estimate=expert_cost(blocks, weights),
+        name="last_slice",
     )(*blocks, *weights)
 
 
@@ -221,20 +239,17 @@
         slots, live_counts, expert_ids.T, gate_vals.T, tokens, norm_gain.reshape(1, features)
     )
     own = across_groups(flight, rows)
-    blocks = {0: own}
-    for j in (6, 4, 2, 1):
-        blocks[j] = swap(devices, j, own)
-    for j in (2, 4, 6):
-        blocks[j + 1] = swap(devices, 1, blocks[j])
-    partial_out = {}
-    partial_out[0], *weights = first_slice(own, (w_gate.T, w_up.T, w_down))
-    for group in ((1, 2, 4, 6), (3, 5, 7)):
-        outs = expert_slice([blocks[j] for j in group], weights)
-        partial_out.update(zip(group, outs))
-    level = {}
-    for j in (6, 4, 2, 0):
-        level[j] = add_level(partial_out[j], swap(devices, 1, partial_out[j + 1]))
-    parts = [level[0]] + [swap(devices, j, level[j]) for j in (2, 4, 6)]
+    near, far, farther = (swap(devices, j, own) for j in (2, 4, 6))
+    inner, outer = jnp.concatenate([own, near]), jnp.concatenate([far, farther])
+    inner_y, outer_y = swap(devices, 1, inner), swap(devices, 1, outer)
+    weights = (w_gate.T, w_up.T, w_down)
+    (inner, outer, inner_y), weights = first_slice((inner, outer, inner_y), weights)
+    (outer_y,) = last_slice((outer_y,), weights)
+    inner, outer = (
+        (add_level(kept[:slots], came[:slots]), add_level(kept[slots:], came[slots:]))
+        for kept, came in ((inner, swap(devices, 1, inner_y)), (outer, swap(devices, 1, outer_y)))
+    )
+    parts = [inner[0], swap(devices, 2, inner[1]), swap(devices, 4, outer[0]), swap(devices, 6, outer[1])]
     if flight > 1:
         parts = [across_groups(flight, add_levels(parts))]
     return combine(table, parts)

time: 36.1 us -> 34.4 us (0.953)
  starting transfers between devices: 19.8 us -> 15.9 us
  waiting for transfers between devices: 8.78 us -> 11.5 us
  Pallas kernels: 6.46 us -> 5.97 us
    ppermute x14 -> x10, starting transfers between devices: 19.8 us -> 15.9 us  [swap(): lax.ppermute(block, 'ep', [(i, i ^ distance) for i in range(devices)])]
    ppermute x14 -> x10, waiting for transfers between devices: 8.78 us -> 11.5 us  [swap(): lax.ppermute(block, 'ep', [(i, i ^ distance) for i in range(devices)])]
    pallas_call x3 -> x2, Pallas kernels: 4.03 us -> 3.46 us  [the longest x1 2.66 us: first_slice(): pl.pallas_call(first_kernel, out_shape=[jax.ShapeDtypeStruct(array.shape,...]
  transfers between devices with their start and end apart: 14 -> 10, of which waited for: 4 -> 7; matrix products, arithmetic and copies ran while one was open for 0% -> 0% of each run, Pallas kernels for 11% -> 10%
where the time goes in v4:
time: 34.4 us; the launch traced here: 34.2 us
  starting transfers between devices  15.9 us (46%)
  waiting for transfers between devices  11.5 us (33%)
  Pallas kernels  5.97 us (17%)
  between operations  0.71 us (2%)
    ppermute x10, starting transfers between devices, swap(): lax.ppermute(block, 'ep', [(i, i ^ distance) for i in range(devices)])  15.9 us
    ppermute x10, waiting for transfers between devices, swap(): lax.ppermute(block, 'ep', [(i, i ^ distance) for i in range(devices)])  11.5 us
    pallas_call x1, Pallas kernels, first_slice(): pl.pallas_call(first_kernel, out_shape=[jax.ShapeDtypeStruct(array.shape,...  2.66 us
    pallas_call x1, Pallas kernels, pick_rows(): pl.pallas_call(pick_kernel, out_shape=(jax.ShapeDtypeStruct((slots, token...  1.47 us
    pallas_call x1, Pallas kernels, combine(): pl.pallas_call(combine_kernel, out_shape=jax.ShapeDtypeStruct(shape, jnp....  1.04 us
    pallas_call x1, Pallas kernels, last_slice(): pl.pallas_call(last_kernel, out_shape=[jax.ShapeDtypeStruct(block.shape,...  0.8 us
  transfers between devices with their start and end apart: 10, of which 7 were waited for; matrix products, arithmetic and copies ran while one was open for 0% of the time, Pallas kernels for 10%

profile of v4, /device:TPU:0, one launch (start us, length us, event | category | flops | bytes accessed | tf_op | source)
XLA Modules:
  0.0 34.2 jit_solution(6388068555623605771)
XLA Ops:
  0.7 1.5 %pick_rows.1 = (bf16[16,2048]{1,0:T(8,128)(2,1)S(1)}, f32[16,128]{1,0:T(8,128)S(1)}) custom-call(s32[1]{0:T(128)S(6)} %copy.11.live_ref, s32[8,128]{1,0:T(8,128)} %bitcast.8, f32[8,128]{1,0:T(8,128)} %bitcast.9, bf16[128,2048]{1,0:T(8,128)(2,1)} %tokens_hbm.1, f32[1,2048]{1,0:T(1,128)} %bitcast.7), custom_call_target="tpu_custom_call" | custom-call | tf_op jit(solution)/shard_map/pick_rows/pallas_call | solution.py:62
  2.1 3.1 %collective-permute-start = (bf16[16,2048]{1,0:T(8,128)(2,1)S(1)}, bf16[16,2048]{1,0:T(8,128)(2,1)S(1)}, u32[]{:S(2)}, u32[]{:S(2)}) collective-permute-start(bf16[16,2048]{1,0:T(8,128)(2,1)S(1)} %get-tuple-element.14), channel_id=1, source_target_pairs={{0,8},{4,12},{8,0},{12,4},{16,24},{20,28},{24,16},{28,20},{1,9},{5... | collective-permute-start | bytes 196616 | tf_op jit(solution)/shard_map/ppermute | solution.py:230
  5.2 2.6 %collective-permute-start.1 = (bf16[16,2048]{1,0:T(8,128)(2,1)S(1)}, bf16[16,2048]{1,0:T(8,128)(2,1)S(1)}, u32[]{:S(2)}, u32[]{:S(2)}) collective-permute-start(bf16[16,2048]{1,0:T(8,128)(2,1)S(1)} %get-tuple-element.14), channel_id=1, source_target_pairs={{0,16},{4,20},{8,24},{12,28},{16,0},{20,4},{24,8},{28,12},{1,17},{... | collective-permute-start | bytes 196616 | tf_op jit(solution)/shard_map/ppermute | solution.py:230
  7.8 0.0 collective-permute-start.2
  7.8 0.0 collective-permute-done
  7.8 1.8 %collective-permute-start.3 = (bf16[32,2048]{1,0:T(8,128)(2,1)S(1)}, bf16[32,2048]{1,0:T(8,128)(2,1)S(1)}, u32[]{:S(2)}, u32[]{:S(2)}) collective-permute-start(bf16[32,2048]{1,0:T(8,128)(2,1)S(1)} %constant_dynamic-update-slice_fusion.refs_0_), channel_id=1, source_target_pairs={{0,4},{4,0},{8,12},{12,8},{16,20},{20,16},{24,28},{28,24},{1,5},{5... | collective-permute-start | bytes 393224 | tf_op jit(solution)/shard_map/ppermute | solution.py:230
  9.6 2.8 %collective-permute-done.1 = bf16[16,2048]{1,0:T(8,128)(2,1)S(1)} collective-permute-done((bf16[16,2048]{1,0:T(8,128)(2,1)S(1)}, bf16[16,2048]{1,0:T(8,128)(2,1)S(1)}, u32[]{:S(2)}, u32[]{:S(2)}) %collective-permute-start.1) | collective-permute-done | bytes 65568 | tf_op jit(solution)/shard_map/ppermute | solution.py:230
  12.5 1.4 %collective-permute-done.2 = bf16[16,2048]{1,0:T(8,128)(2,1)S(1)} collective-permute-done((bf16[16,2048]{1,0:T(8,128)(2,1)S(1)}, bf16[16,2048]{1,0:T(8,128)(2,1)S(1)}, u32[]{:S(2)}, u32[]{:S(2)}) %collective-permute-start.2) | collective-permute-done | bytes 65568 | tf_op jit(solution)/shard_map/ppermute | solution.py:230
  13.9 1.5 %collective-permute-start.6 = (bf16[32,2048]{1,0:T(8,128)(2,1)S(1)}, bf16[32,2048]{1,0:T(8,128)(2,1)S(1)}, u32[]{:S(2)}, u32[]{:S(2)}) collective-permute-start(bf16[32,2048]{1,0:T(8,128)(2,1)S(1)} %constant_dynamic-update-slice_fusion.2.refs_1_), channel_id=1, source_target_pairs={{0,4},{4,0},{8,12},{12,8},{16,20},{20,16},{24,28},{28,24},{1,5},{5... | collective-permute-start | bytes 393224 | tf_op jit(solution)/shard_map/ppermute | solution.py:230
  15.4 0.0 collective-permute-done.3.refs_2_
  15.4 2.7 %first_slice.1 = (bf16[32,2048]{1,0:T(8,128)(2,1)S(1)}, bf16[32,2048]{1,0:T(8,128)(2,1)S(1)}, bf16[32,2048]{1,0:T(8,128)(2,1)S(1)}, bf16[192,2048]{1,0:T(8,128)(...) custom-call(bf16[32,2048]{1,0:T(8,128)(2,1)S(1)} %constant_dynamic-update-slice_fusion.refs_0_, ...), custom_call_target="tpu_custom_call" | custom-call | flops 226492416 | bytes 2359296 | tf_op jit(solution)/shard_map/first_slice/pallas_call | solution.py:136
  18.1 0.6 %collective-permute-start.4 = (bf16[32,2048]{1,0:T(8,128)(2,1)S(1)}, bf16[32,2048]{1,0:T(8,128)(2,1)S(1)}, u32[]{:S(2)}, u32[]{:S(2)}) collective-permute-start(bf16[32,2048]{1,0:T(8,128)(2,1)S(1)} %get-tuple-element.16), channel_id=1, source_target_pairs={{0,4},{4,0},{8,12},{12,8},{16,20},{20,16},{24,28},{28,24},{1,5},{5... | collective-permute-start | bytes 393224 | tf_op jit(solution)/shard_map/ppermute | solution.py:230
  18.7 0.4 %collective-permute-done.6.refs_0_ = bf16[32,2048]{1,0:T(8,128)(2,1)S(1)} collective-permute-done((bf16[32,2048]{1,0:T(8,128)(2,1)S(1)}, bf16[32,2048]{1,0:T(8,128)(2,1)S(1)}, u32[]{:S(2)}, u32[]{:S(2)}) %collective-permute-start.6) | collective-permute-done | bytes 131104 | tf_op jit(solution)/shard_map/ppermute | solution.py:230
  19.1 0.8 %last_slice.1 = bf16[32,2048]{1,0:T(8,128)(2,1)S(1)} custom-call(bf16[32,2048]{1,0:T(8,128)(2,1)S(1)} %collective-permute-done.6.refs_0_, bf16[192,2048]{1,0:T(8,128)(2,1)S(1)} %get-tuple-element.18.refs_1_, bf16[192,2048]{1,0:T(8,128)(2,1)S(1)} %get-tuple-element.19.refs_2_, bf16[192,2048]{1,0:T(8,128)(2,1)S(1)} %get-tuple-element.20.refs_3_), custom_call_target="tpu_custom_call" | custom-call | flops 75497472 | bytes 2359296 | tf_op jit(solution)/shard_map/last_slice/pallas_call | solution.py:157
  19.9 2.5 %collective-permute-start.7 = (bf16[32,2048]{1,0:T(8,128)(2,1)S(1)}, bf16[32,2048]{1,0:T(8,128)(2,1)S(1)}, u32[]{:S(2)}, u32[]{:S(2)}) collective-permute-start(bf16[32,2048]{1,0:T(8,128)(2,1)S(1)} %last_slice.1), channel_id=1, source_target_pairs={{0,4},{4,0},{8,12},{12,8},{16,20},{20,16},{24,28},{28,24},{1,5},{5... | collective-permute-start | bytes 393224 | tf_op jit(solution)/shard_map/ppermute | solution.py:230
  22.4 0.7 %collective-permute-done.4 = bf16[32,2048]{1,0:T(8,128)(2,1)S(1)} collective-permute-done((bf16[32,2048]{1,0:T(8,128)(2,1)S(1)}, bf16[32,2048]{1,0:T(8,128)(2,1)S(1)}, u32[]{:S(2)}, u32[]{:S(2)}) %collective-permute-start.4) | collective-permute-done | bytes 131104 | tf_op jit(solution)/shard_map/ppermute | solution.py:230
  23.2 0.5 %collective-permute-start.5 = (bf16[16,2048]{1,0:T(8,128)(2,1)S(1)}, bf16[16,2048]{1,0:T(8,128)(2,1)S(1)}, u32[]{:S(2)}, u32[]{:S(2)}) collective-permute-start(bf16[16,2048]{1,0:T(8,128)(2,1)S(1)} %get-tuple-element.23), channel_id=1, source_target_pairs={{0,8},{4,12},{8,0},{12,4},{16,24},{20,28},{24,16},{28,20},{1,9},{5... | collective-permute-start | bytes 196616 | tf_op jit(solution)/shard_map/ppermute | solution.py:230
  23.6 1.7 %collective-permute-done.7 = bf16[32,2048]{1,0:T(8,128)(2,1)S(1)} collective-permute-done((bf16[32,2048]{1,0:T(8,128)(2,1)S(1)}, bf16[32,2048]{1,0:T(8,128)(2,1)S(1)}, u32[]{:S(2)}, u32[]{:S(2)}) %collective-permute-start.7) | collective-permute-done | bytes 131104 | tf_op jit(solution)/shard_map/ppermute | solution.py:230
  25.4 1.5 %collective-permute-start.8 = (bf16[16,2048]{1,0:T(8,128)(2,1)S(1)}, bf16[16,2048]{1,0:T(8,128)(2,1)S(1)}, u32[]{:S(2)}, u32[]{:S(2)}) collective-permute-start(bf16[16,2048]{1,0:T(8,128)(2,1)S(1)} %get-tuple-element.22), channel_id=1, source_target_pairs={{0,16},{4,20},{8,24},{12,28},{16,0},{20,4},{24,8},{28,12},{1,17},{... | collective-permute-start | bytes 196616 | tf_op jit(solution)/shard_map/ppermute | solution.py:230
  27.0 1.8 %collective-permute-start.9 = (bf16[16,2048]{1,0:T(8,128)(2,1)S(1)}, bf16[16,2048]{1,0:T(8,128)(2,1)S(1)}, u32[]{:S(2)}, u32[]{:S(2)}) collective-permute-start(bf16[16,2048]{1,0:T(8,128)(2,1)S(1)} %get-tuple-element.21), channel_id=1, source_target_pairs={{0,24},{4,28},{8,16},{12,20},{16,8},{20,12},{24,0},{28,4},{1,25},{... | collective-permute-start | bytes 196616 | tf_op jit(solution)/shard_map/ppermute | solution.py:230
  28.8 0.0 collective-permute-done.5.refs_1_
  28.8 2.6 %collective-permute-done.8.refs_2_ = bf16[16,2048]{1,0:T(8,128)(2,1)S(1)} collective-permute-done((bf16[16,2048]{1,0:T(8,128)(2,1)S(1)}, bf16[16,2048]{1,0:T(8,128)(2,1)S(1)}, u32[]{:S(2)}, u32[]{:S(2)}) %collective-permute-start.8) | collective-permute-done | bytes 65568 | tf_op jit(solution)/shard_map/ppermute | solution.py:230
  31.4 1.8 %collective-permute-done.9.refs_3_ = bf16[16,2048]{1,0:T(8,128)(2,1)S(1)} collective-permute-done((bf16[16,2048]{1,0:T(8,128)(2,1)S(1)}, bf16[16,2048]{1,0:T(8,128)(2,1)S(1)}, u32[]{:S(2)}, u32[]{:S(2)}) %collective-permute-start.9) | collective-permute-done | bytes 65568 | tf_op jit(solution)/shard_map/ppermute | solution.py:230
  33.1 1.0 %combine.1 = bf16[128,2048]{1,0:T(8,128)(2,1)} custom-call(f32[16,128]{1,0:T(8,128)S(1)} %get-tuple-element.13.table_ref, bf16[16,2048]{1,0:T(8,128)(2,1)S(1)} %get-tuple-element.24.refs_0_, bf16[16,2048]{1,0:T(8,128)(2,1)S(1)} %collective-permute-done.5.refs_1_, bf16[16,2048]{1,0:T(8,128)(2,1)S(1)} %collective-permute-done.8.refs_2_, ...), custom_call_target="tpu_custom_call" | custom-call | tf_op jit(solution)/shard_map/combine/pallas_call | solution.py:209
  (6 shorter events, 0.1 us)
Async XLA Ops:
  2.1 5.7 %collective-permute-start = (bf16[16,2048]{1,0:T(8,128)(2,1)S(1)}, bf16[16,2048]{1,0:T(8,128)(2,1)S(1)}, u32[]{:S(2)}, u32[]{:S(2)}) collective-permute-start(bf16[16,2048]{1,0:T(8,128)(2,1)S(1)} %get-tuple-element.14), channel_id=1, source_target_pairs={{0,8},{4,12},{8,0},{12,4},{16,24},{20,28},{24,16},{28,20},{1,9},{5... | collective-permute-start | bytes 196616 | tf_op jit(solution)/shard_map/ppermute | solution.py:230
  5.2 7.3 %collective-permute-start.1 = (bf16[16,2048]{1,0:T(8,128)(2,1)S(1)}, bf16[16,2048]{1,0:T(8,128)(2,1)S(1)}, u32[]{:S(2)}, u32[]{:S(2)}) collective-permute-start(bf16[16,2048]{1,0:T(8,128)(2,1)S(1)} %get-tuple-element.14), channel_id=1, source_target_pairs={{0,16},{4,20},{8,24},{12,28},{16,0},{20,4},{24,8},{28,12},{1,17},{... | collective-permute-start | bytes 196616 | tf_op jit(solution)/shard_map/ppermute | solution.py:230
  7.8 6.1 %collective-permute-start.2 = (bf16[16,2048]{1,0:T(8,128)(2,1)S(1)}, bf16[16,2048]{1,0:T(8,128)(2,1)S(1)}, u32[]{:S(2)}, u32[]{:S(2)}) collective-permute-start(bf16[16,2048]{1,0:T(8,128)(2,1)S(1)} %get-tuple-element.14), channel_id=1, source_target_pairs={{0,24},{4,28},{8,16},{12,20},{16,8},{20,12},{24,0},{28,4},{1,25},{... | collective-permute-start | bytes 196616 | tf_op jit(solution)/shard_map/ppermute | solution.py:230
  7.8 7.6 %collective-permute-start.3 = (bf16[32,2048]{1,0:T(8,128)(2,1)S(1)}, bf16[32,2048]{1,0:T(8,128)(2,1)S(1)}, u32[]{:S(2)}, u32[]{:S(2)}) collective-permute-start(bf16[32,2048]{1,0:T(8,128)(2,1)S(1)} %constant_dynamic-update-slice_fusion.refs_0_), channel_id=1, source_target_pairs={{0,4},{4,0},{8,12},{12,8},{16,20},{20,16},{24,28},{28,24},{1,5},{5... | collective-permute-start | bytes 393224 | tf_op jit(solution)/shard_map/ppermute | solution.py:230
  13.9 5.2 %collective-permute-start.6 = (bf16[32,2048]{1,0:T(8,128)(2,1)S(1)}, bf16[32,2048]{1,0:T(8,128)(2,1)S(1)}, u32[]{:S(2)}, u32[]{:S(2)}) collective-permute-start(bf16[32,2048]{1,0:T(8,128)(2,1)S(1)} %constant_dynamic-update-slice_fusion.2.refs_1_), channel_id=1, source_target_pairs={{0,4},{4,0},{8,12},{12,8},{16,20},{20,16},{24,28},{28,24},{1,5},{5... | collective-permute-start | bytes 393224 | tf_op jit(solution)/shard_map/ppermute | solution.py:230
  18.1 5.0 %collective-permute-start.4 = (bf16[32,2048]{1,0:T(8,128)(2,1)S(1)}, bf16[32,2048]{1,0:T(8,128)(2,1)S(1)}, u32[]{:S(2)}, u32[]{:S(2)}) collective-permute-start(bf16[32,2048]{1,0:T(8,128)(2,1)S(1)} %get-tuple-element.16), channel_id=1, source_target_pairs={{0,4},{4,0},{8,12},{12,8},{16,20},{20,16},{24,28},{28,24},{1,5},{5... | collective-permute-start | bytes 393224 | tf_op jit(solution)/shard_map/ppermute | solution.py:230
  19.9 5.5 %collective-permute-start.7 = (bf16[32,2048]{1,0:T(8,128)(2,1)S(1)}, bf16[32,2048]{1,0:T(8,128)(2,1)S(1)}, u32[]{:S(2)}, u32[]{:S(2)}) collective-permute-start(bf16[32,2048]{1,0:T(8,128)(2,1)S(1)} %last_slice.1), channel_id=1, source_target_pairs={{0,4},{4,0},{8,12},{12,8},{16,20},{20,16},{24,28},{28,24},{1,5},{5... | collective-permute-start | bytes 393224 | tf_op jit(solution)/shard_map/ppermute | solution.py:230
  23.2 5.6 %collective-permute-start.5 = (bf16[16,2048]{1,0:T(8,128)(2,1)S(1)}, bf16[16,2048]{1,0:T(8,128)(2,1)S(1)}, u32[]{:S(2)}, u32[]{:S(2)}) collective-permute-start(bf16[16,2048]{1,0:T(8,128)(2,1)S(1)} %get-tuple-element.23), channel_id=1, source_target_pairs={{0,8},{4,12},{8,0},{12,4},{16,24},{20,28},{24,16},{28,20},{1,9},{5... | collective-permute-start | bytes 196616 | tf_op jit(solution)/shard_map/ppermute | solution.py:230
  25.4 5.9 %collective-permute-start.8 = (bf16[16,2048]{1,0:T(8,128)(2,1)S(1)}, bf16[16,2048]{1,0:T(8,128)(2,1)S(1)}, u32[]{:S(2)}, u32[]{:S(2)}) collective-permute-start(bf16[16,2048]{1,0:T(8,128)(2,1)S(1)} %get-tuple-element.22), channel_id=1, source_target_pairs={{0,16},{4,20},{8,24},{12,28},{16,0},{20,4},{24,8},{28,12},{1,17},{... | collective-permute-start | bytes 196616 | tf_op jit(solution)/shard_map/ppermute | solution.py:230
  27.0 6.2 %collective-permute-start.9 = (bf16[16,2048]{1,0:T(8,128)(2,1)S(1)}, bf16[16,2048]{1,0:T(8,128)(2,1)S(1)}, u32[]{:S(2)}, u32[]{:S(2)}) collective-permute-start(bf16[16,2048]{1,0:T(8,128)(2,1)S(1)} %get-tuple-element.21), channel_id=1, source_target_pairs={{0,24},{4,28},{8,16},{12,20},{16,8},{20,12},{24,0},{28,4},{1,25},{... | collective-permute-start | bytes 196616 | tf_op jit(solution)/shard_map/ppermute | solution.py:230

commit v5 on v4

--- a/solution.py
+++ b/solution.py
@@ -112,11 +112,9 @@
         yield pltpu.make_async_copy(source.at[at], target.at[at], sems.at[i])
 
 
-def first_kernel(*refs):
+def stage_kernel(rows_ref, *refs):
     *refs, sems = refs
-    count = (len(refs) - 6) // 2
-    ins, sources = refs[:count], refs[count : count + 3]
-    outs, weights = refs[count + 3 : 2 * count + 3], refs[2 * count + 3 :]
+    sources, out_ref, weights = refs[:3], refs[3], refs[4:]
     copies = [
         copy
         for i, pair in enumerate(zip(sources, weights))
@@ -124,55 +122,48 @@
     ]
     for copy in copies:
         copy.start()
+    out_ref[...] = rows_ref[...]
     for copy in copies:
         copy.wait()
-    expert_blocks(ins, weights, outs)
-
-
-def first_slice(blocks, weights):
+
+
+def stage_weights(rows, weights):
     vmem = pl.BlockSpec(memory_space=pltpu.VMEM)
     hbm = pl.BlockSpec(memory_space=pltpu.HBM)
-    count = len(blocks)
-    outs = pl.pallas_call(
-        first_kernel,
-        out_shape=[jax.ShapeDtypeStruct(array.shape, array.dtype) for array in (*blocks, *weights)],
-        in_specs=[vmem] * count + [hbm] * 3,
-        out_specs=[vmem] * (count + 3),
+    rows, *weights = pl.pallas_call(
+        stage_kernel,
+        out_shape=[jax.ShapeDtypeStruct(array.shape, array.dtype) for array in (rows, *weights)],
+        in_specs=[vmem] + [hbm] * 3,
+        out_specs=[vmem] * 4,
         scratch_shapes=[pltpu.SemaphoreType.DMA((3, WEIGHT_CHUNKS))],
         compiler_params=pltpu.CompilerParams(vmem_limit_bytes=VMEM_LIMIT),
-        cost_estimate=expert_cost(blocks, weights),
-        name="first_slice",
-    )(*blocks, *(in_hbm(weight) for weight in weights))
-    return outs[:count], outs[count:]
-
-
-def last_kernel(*refs):
+        cost_estimate=expert_cost([rows], weights),
+        name="stage_weights",
+    )(rows, *(in_hbm(weight) for weight in weights))
+    return rows, weights
+
+
+def slice_kernel(*refs):
     count = (len(refs) - 3) // 2
     expert_blocks(refs[:count], refs[count : count + 3], refs[count + 3 :])
 
 
-def last_slice(blocks, weights):
+def expert_slice(blocks, weights):
     vmem = pl.BlockSpec(memory_space=pltpu.VMEM)
     count = len(blocks)
     return pl.pallas_call(
-        last_kernel,
+        slice_kernel,
         out_shape=[jax.ShapeDtypeStruct(block.shape, jnp.bfloat16) for block in blocks],
         in_specs=[vmem] * (count + 3),
         out_specs=[vmem] * count,
         compiler_params=pltpu.CompilerParams(vmem_limit_bytes=VMEM_LIMIT),
         cost_estimate=expert_cost(blocks, weights),
-        name="last_slice",
+        name="expert_slice",
     )(*blocks, *weights)
 
 
 def add_level(kept, came):
     return (kept.astype(jnp.float32) + came.astype(jnp.float32)).astype(jnp.bfloat16)
-
-
-def add_levels(parts):
-    while len(parts) > 1:
-        parts = [add_level(*pair) for pair in zip(parts[::2], parts[1::2])]
-    return parts[0]
 
 
 def combine_kernel(table_ref, *refs):
@@ -188,7 +179,7 @@
     copies = []
     for i in range(4):
         columns = pl.ds(i * width, width)
-        summed = add_levels([part[:, columns] for part in parts])
+        summed = functools.reduce(add_level, [part[:, columns] for part in parts])
         out_ref[:, columns] = lax.dot_general(
             pieces,
             jnp.concatenate([summed] * 3, axis=0),
@@ -239,19 +230,22 @@
         slots, live_counts, expert_ids.T, gate_vals.T, tokens, norm_gain.reshape(1, features)
     )
     own = across_groups(flight, rows)
-    near, far, farther = (swap(devices, j, own) for j in (2, 4, 6))
+    far = swap(devices, 4, own)
+    own, weights = stage_weights(own, (w_gate.T, w_up.T, w_down))
+    near = swap(devices, 2, own)
+    farther = swap(devices, 2, far)
     inner, outer = jnp.concatenate([own, near]), jnp.concatenate([far, farther])
     inner_y, outer_y = swap(devices, 1, inner), swap(devices, 1, outer)
-    weights = (w_gate.T, w_up.T, w_down)
-    (inner, outer, inner_y), weights = first_slice((inner, outer, inner_y), weights)
-    (outer_y,) = last_slice((outer_y,), weights)
-    inner, outer = (
-        (add_level(kept[:slots], came[:slots]), add_level(kept[slots:], came[slots:]))
-        for kept, came in ((inner, swap(devices, 1, inner_y)), (outer, swap(devices, 1, outer_y)))
-    )
-    parts = [inner[0], swap(devices, 2, inner[1]), swap(devices, 4, outer[0]), swap(devices, 6, outer[1])]
+    inner, outer, inner_y = expert_slice((inner, outer, inner_y), weights)
+    (outer_y,) = expert_slice((outer_y,), weights)
+    inner_y, outer_y = swap(devices, 1, inner_y), swap(devices, 1, outer_y)
+    own, near = (add_level(inner[at], inner_y[at]) for at in (slice(slots), slice(slots, None)))
+    far, farther = (add_level(outer[at], outer_y[at]) for at in (slice(slots), slice(slots, None)))
+    near = swap(devices, 2, near)
+    far = swap(devices, 4, add_level(far, swap(devices, 2, farther)))
+    parts = [own, near, far]
     if flight > 1:
-        parts = [across_groups(flight, add_levels(parts))]
+        parts = [across_groups(flight, functools.reduce(add_level, parts))]
     return combine(table, parts)
 
 

time: 34.4 us -> 37.7 us (1.096)
  waiting for transfers between devices: 11.5 us -> 17 us
  starting transfers between devices: 15.9 us -> 13.7 us
    ppermute x10, waiting for transfers between devices: 11.5 us -> 17 us  [swap(): lax.ppermute(block, 'ep', [(i, i ^ distance) for i in range(devices)])]
    ppermute x10, starting transfers between devices: 15.9 us -> 13.7 us  [swap(): lax.ppermute(block, 'ep', [(i, i ^ distance) for i in range(devices)])]
    pallas_call x2 -> x3, Pallas kernels: 3.46 us -> 3.46 us  [the longest x1 1.8 us: stage_weights(): pl.pallas_call(stage_kernel, out_shape=[jax.ShapeDtypeStruct(array.shape,...]
  transfers between devices with their start and end apart: 10 -> 10, of which waited for: 7 -> 8; matrix products, arithmetic and copies ran while one was open for 0% -> 0% of each run, Pallas kernels for 10% -> 9%
where the time goes in v5:
time: 37.7 us; the launch traced here: 37.5 us
  waiting for transfers between devices  17 us (45%)
  starting transfers between devices  13.7 us (36%)
  Pallas kernels  5.96 us (16%)
  between operations  0.7 us (2%)
    ppermute x10, waiting for transfers between devices, swap(): lax.ppermute(block, 'ep', [(i, i ^ distance) for i in range(devices)])  17 us
    ppermute x10, starting transfers between devices, swap(): lax.ppermute(block, 'ep', [(i, i ^ distance) for i in range(devices)])  13.7 us
    pallas_call x1, Pallas kernels, stage_weights(): pl.pallas_call(stage_kernel, out_shape=[jax.ShapeDtypeStruct(array.shape,...  1.8 us
    pallas_call x2, Pallas kernels, expert_slice(): pl.pallas_call(slice_kernel, out_shape=[jax.ShapeDtypeStruct(block.shape,...  1.66 us
    pallas_call x1, Pallas kernels, pick_rows(): pl.pallas_call(pick_kernel, out_shape=(jax.ShapeDtypeStruct((slots, token...  1.47 us
    pallas_call x1, Pallas kernels, combine(): pl.pallas_call(combine_kernel, out_shape=jax.ShapeDtypeStruct(shape, jnp....  1.04 us
  transfers between devices with their start and end apart: 10, of which 8 were waited for; matrix products, arithmetic and copies ran while one was open for 0% of the time, Pallas kernels for 9%

profile of v5, /device:TPU:0, one launch (start us, length us, event | category | flops | bytes accessed | tf_op | source)
XLA Modules:
  0.0 37.5 jit_solution(2180382259928079575)
XLA Ops:
  0.7 1.5 %pick_rows.1 = (bf16[16,2048]{1,0:T(8,128)(2,1)S(1)}, f32[16,128]{1,0:T(8,128)S(1)}) custom-call(s32[1]{0:T(128)S(6)} %copy.11.live_ref, s32[8,128]{1,0:T(8,128)} %bitcast.8, f32[8,128]{1,0:T(8,128)} %bitcast.9, bf16[128,2048]{1,0:T(8,128)(2,1)} %tokens_hbm.1, f32[1,2048]{1,0:T(1,128)} %bitcast.7), custom_call_target="tpu_custom_call" | custom-call | tf_op jit(solution)/shard_map/pick_rows/pallas_call | solution.py:62
  2.1 4.1 %collective-permute-start.1 = (bf16[16,2048]{1,0:T(8,128)(2,1)S(1)}, bf16[16,2048]{1,0:T(8,128)(2,1)S(1)}, u32[]{:S(2)}, u32[]{:S(2)}) collective-permute-start(bf16[16,2048]{1,0:T(8,128)(2,1)S(1)} %get-tuple-element.15.rows_ref), channel_id=1, source_target_pairs={{0,16},{4,20},{8,24},{12,28},{16,0},{20,4},{24,8},{28,12},{1,17},{... | collective-permute-start | bytes 196616 | tf_op jit(solution)/shard_map/ppermute | solution.py:221
  6.2 1.8 %stage_weights.1 = (bf16[16,2048]{1,0:T(8,128)(2,1)S(1)}, bf16[192,2048]{1,0:T(8,128)(2,1)S(1)}, bf16[192,2048]{1,0:T(8,128)(2,1)S(1)}, bf16[192,2048]{1,0:T(8,128)(2,1)S(1)}) custom-call(bf16[16,2048]{1,0:T(8,128)(2,1)S(1)} %get-tuple-element.15.rows_ref, bf16[192,2048]{1,0:T(8,128)(2,1)} %bitcast.5, bf16[192,2048]{1,0:T(8,128)(2,1)} %bitcast.6, ...), custom_call_target="tpu_custom_call" | custom-call | flops 37748736 | bytes 2359296 | tf_op jit(solution)/shard_map/stage_weights/pallas_call | solution.py:133
  8.0 1.6 %collective-permute-start = (bf16[16,2048]{1,0:T(8,128)(2,1)S(1)}, bf16[16,2048]{1,0:T(8,128)(2,1)S(1)}, u32[]{:S(2)}, u32[]{:S(2)}) collective-permute-start(bf16[16,2048]{1,0:T(8,128)(2,1)S(1)} %get-tuple-element.16), channel_id=1, source_target_pairs={{0,8},{4,12},{8,0},{12,4},{16,24},{20,28},{24,16},{28,20},{1,9},{5... | collective-permute-start | bytes 196616 | tf_op jit(solution)/shard_map/ppermute | solution.py:221
  9.7 0.2 collective-permute-done.1
  9.9 0.6 %collective-permute-start.2 = (bf16[16,2048]{1,0:T(8,128)(2,1)S(1)}, bf16[16,2048]{1,0:T(8,128)(2,1)S(1)}, u32[]{:S(2)}, u32[]{:S(2)}) collective-permute-start(bf16[16,2048]{1,0:T(8,128)(2,1)S(1)} %collective-permute-done.1), channel_id=1, source_target_pairs={{0,8},{4,12},{8,0},{12,4},{16,24},{20,28},{24,16},{28,20},{1,9},{5... | collective-permute-start | bytes 196616 | tf_op jit(solution)/shard_map/ppermute | solution.py:221
  10.5 3.7 %collective-permute-done.2 = bf16[16,2048]{1,0:T(8,128)(2,1)S(1)} collective-permute-done((bf16[16,2048]{1,0:T(8,128)(2,1)S(1)}, bf16[16,2048]{1,0:T(8,128)(2,1)S(1)}, u32[]{:S(2)}, u32[]{:S(2)}) %collective-permute-start.2) | collective-permute-done | bytes 65568 | tf_op jit(solution)/shard_map/ppermute | solution.py:221
  14.2 1.7 %collective-permute-start.6 = (bf16[32,2048]{1,0:T(8,128)(2,1)S(1)}, bf16[32,2048]{1,0:T(8,128)(2,1)S(1)}, u32[]{:S(2)}, u32[]{:S(2)}) collective-permute-start(bf16[32,2048]{1,0:T(8,128)(2,1)S(1)} %constant_dynamic-update-slice_fusion.2.refs_1_), channel_id=1, source_target_pairs={{0,4},{4,0},{8,12},{12,8},{16,20},{20,16},{24,28},{28,24},{1,5},{5... | collective-permute-start | bytes 393224 | tf_op jit(solution)/shard_map/ppermute | solution.py:221
  15.9 0.0 collective-permute-done
  15.9 0.4 collective-permute-start.3
  16.3 3.7 %collective-permute-done.6.refs_0_ = bf16[32,2048]{1,0:T(8,128)(2,1)S(1)} collective-permute-done((bf16[32,2048]{1,0:T(8,128)(2,1)S(1)}, bf16[32,2048]{1,0:T(8,128)(2,1)S(1)}, u32[]{:S(2)}, u32[]{:S(2)}) %collective-permute-start.6) | collective-permute-done | bytes 131104 | tf_op jit(solution)/shard_map/ppermute | solution.py:221
  19.9 0.8 %expert_slice.3 = bf16[32,2048]{1,0:T(8,128)(2,1)S(1)} custom-call(bf16[32,2048]{1,0:T(8,128)(2,1)S(1)} %collective-permute-done.6.refs_0_, bf16[192,2048]{1,0:T(8,128)(2,1)S(1)} %get-tuple-element.17.refs_3_.refs_1_, bf16[192,2048]{1,0:T(8,128)(2,1)S(1)} %get-tuple-element.18.refs_4_.refs_2_, bf16[192,2048]{1,0:T(8,128)(2,1)S(1)} %get-tuple-element.19.refs_5_.refs_3_), custom_call_target="tpu_custom_call" | custom-call | flops 75497472 | bytes 2359296 | tf_op jit(solution)/shard_map/expert_slice/pallas_call | solution.py:154
  20.7 1.6 %collective-permute-start.7 = (bf16[32,2048]{1,0:T(8,128)(2,1)S(1)}, bf16[32,2048]{1,0:T(8,128)(2,1)S(1)}, u32[]{:S(2)}, u32[]{:S(2)}) collective-permute-start(bf16[32,2048]{1,0:T(8,128)(2,1)S(1)} %expert_slice.3), channel_id=1, source_target_pairs={{0,4},{4,0},{8,12},{12,8},{16,20},{20,16},{24,28},{28,24},{1,5},{5... | collective-permute-start | bytes 393224 | tf_op jit(solution)/shard_map/ppermute | solution.py:221
  22.3 0.0 collective-permute-done.3.refs_2_
  22.3 0.9 %expert_slice.2 = (bf16[32,2048]{1,0:T(8,128)(2,1)S(1)}, bf16[32,2048]{1,0:T(8,128)(2,1)S(1)}, bf16[32,2048]{1,0:T(8,128)(2,1)S(1)}) custom-call(bf16[32,2048]{1,0:T(8,128)(2,1)S(1)} %constant_dynamic-update-slice_fusion.refs_0_, bf16[32,2048]{1,0:T(8,128)(2,1)S(1)} %constant_dynamic-update-slice_fusion.2.refs_1_, ...), custom_call_target="tpu_custom_call" | custom-call | flops 226492416 | bytes 2359296 | tf_op jit(solution)/shard_map/expert_slice/pallas_call | solution.py:154
  23.2 1.5 %collective-permute-start.4 = (bf16[32,2048]{1,0:T(8,128)(2,1)S(1)}, bf16[32,2048]{1,0:T(8,128)(2,1)S(1)}, u32[]{:S(2)}, u32[]{:S(2)}) collective-permute-start(bf16[32,2048]{1,0:T(8,128)(2,1)S(1)} %get-tuple-element.21), channel_id=1, source_target_pairs={{0,4},{4,0},{8,12},{12,8},{16,20},{20,16},{24,28},{28,24},{1,5},{5... | collective-permute-start | bytes 393224 | tf_op jit(solution)/shard_map/ppermute | solution.py:221
  24.6 1.1 %collective-permute-done.7 = bf16[32,2048]{1,0:T(8,128)(2,1)S(1)} collective-permute-done((bf16[32,2048]{1,0:T(8,128)(2,1)S(1)}, bf16[32,2048]{1,0:T(8,128)(2,1)S(1)}, u32[]{:S(2)}, u32[]{:S(2)}) %collective-permute-start.7) | collective-permute-done | bytes 131104 | tf_op jit(solution)/shard_map/ppermute | solution.py:221
  25.8 0.4 %collective-permute-start.8 = (bf16[16,2048]{1,0:T(8,128)(2,1)S(1)}, bf16[16,2048]{1,0:T(8,128)(2,1)S(1)}, u32[]{:S(2)}, u32[]{:S(2)}) collective-permute-start(bf16[16,2048]{1,0:T(8,128)(2,1)S(1)} %add_convert_fusion.1), channel_id=1, source_target_pairs={{0,8},{4,12},{8,0},{12,4},{16,24},{20,28},{24,16},{28,20},{1,9},{5... | collective-permute-start | bytes 196616 | tf_op jit(solution)/shard_map/ppermute | solution.py:221
  26.2 2.0 %collective-permute-done.4 = bf16[32,2048]{1,0:T(8,128)(2,1)S(1)} collective-permute-done((bf16[32,2048]{1,0:T(8,128)(2,1)S(1)}, bf16[32,2048]{1,0:T(8,128)(2,1)S(1)}, u32[]{:S(2)}, u32[]{:S(2)}) %collective-permute-start.4) | collective-permute-done | bytes 131104 | tf_op jit(solution)/shard_map/ppermute | solution.py:221
  28.2 0.4 %collective-permute-start.5 = (bf16[16,2048]{1,0:T(8,128)(2,1)S(1)}, bf16[16,2048]{1,0:T(8,128)(2,1)S(1)}, u32[]{:S(2)}, u32[]{:S(2)}) collective-permute-start(bf16[16,2048]{1,0:T(8,128)(2,1)S(1)} %get-tuple-element.23), channel_id=1, source_target_pairs={{0,8},{4,12},{8,0},{12,4},{16,24},{20,28},{24,16},{28,20},{1,9},{5... | collective-permute-start | bytes 196616 | tf_op jit(solution)/shard_map/ppermute | solution.py:221
  28.7 1.8 %collective-permute-done.8 = bf16[16,2048]{1,0:T(8,128)(2,1)S(1)} collective-permute-done((bf16[16,2048]{1,0:T(8,128)(2,1)S(1)}, bf16[16,2048]{1,0:T(8,128)(2,1)S(1)}, u32[]{:S(2)}, u32[]{:S(2)}) %collective-permute-start.8) | collective-permute-done | bytes 65568 | tf_op jit(solution)/shard_map/ppermute | solution.py:221
  30.5 1.4 %collective-permute-start.9 = (bf16[16,2048]{1,0:T(8,128)(2,1)S(1)}, bf16[16,2048]{1,0:T(8,128)(2,1)S(1)}, u32[]{:S(2)}, u32[]{:S(2)}) collective-permute-start(bf16[16,2048]{1,0:T(8,128)(2,1)S(1)} %add_convert_fusion), channel_id=1, source_target_pairs={{0,16},{4,20},{8,24},{12,28},{16,0},{20,4},{24,8},{28,12},{1,17},{... | collective-permute-start | bytes 196616 | tf_op jit(solution)/shard_map/ppermute | solution.py:221
  32.0 0.6 %collective-permute-done.5.refs_1_ = bf16[16,2048]{1,0:T(8,128)(2,1)S(1)} collective-permute-done((bf16[16,2048]{1,0:T(8,128)(2,1)S(1)}, bf16[16,2048]{1,0:T(8,128)(2,1)S(1)}, u32[]{:S(2)}, u32[]{:S(2)}) %collective-permute-start.5) | collective-permute-done | bytes 65568 | tf_op jit(solution)/shard_map/ppermute | solution.py:221
  32.6 3.9 %collective-permute-done.9.refs_2_ = bf16[16,2048]{1,0:T(8,128)(2,1)S(1)} collective-permute-done((bf16[16,2048]{1,0:T(8,128)(2,1)S(1)}, bf16[16,2048]{1,0:T(8,128)(2,1)S(1)}, u32[]{:S(2)}, u32[]{:S(2)}) %collective-permute-start.9) | collective-permute-done | bytes 65568 | tf_op jit(solution)/shard_map/ppermute | solution.py:221
  36.5 1.0 %combine.1 = bf16[128,2048]{1,0:T(8,128)(2,1)} custom-call(f32[16,128]{1,0:T(8,128)S(1)} %get-tuple-element.14.table_ref, bf16[16,2048]{1,0:T(8,128)(2,1)S(1)} %get-tuple-element.24.refs_0_, bf16[16,2048]{1,0:T(8,128)(2,1)S(1)} %collective-permute-done.5.refs_1_, bf16[16,2048]{1,0:T(8,128)(2,1)S(1)} %collective-permute-done.9.refs_2_), custom_call_target="tpu_custom_call" | custom-call | tf_op jit(solution)/shard_map/combine/pallas_call | solution.py:200
  (7 shorter events, 0.1 us)
Async XLA Ops:
  2.1 7.8 %collective-permute-start.1 = (bf16[16,2048]{1,0:T(8,128)(2,1)S(1)}, bf16[16,2048]{1,0:T(8,128)(2,1)S(1)}, u32[]{:S(2)}, u32[]{:S(2)}) collective-permute-start(bf16[16,2048]{1,0:T(8,128)(2,1)S(1)} %get-tuple-element.15.rows_ref), channel_id=1, source_target_pairs={{0,16},{4,20},{8,24},{12,28},{16,0},{20,4},{24,8},{28,12},{1,17},{... | collective-permute-start | bytes 196616 | tf_op jit(solution)/shard_map/ppermute | solution.py:221
  8.0 7.8 %collective-permute-start = (bf16[16,2048]{1,0:T(8,128)(2,1)S(1)}, bf16[16,2048]{1,0:T(8,128)(2,1)S(1)}, u32[]{:S(2)}, u32[]{:S(2)}) collective-permute-start(bf16[16,2048]{1,0:T(8,128)(2,1)S(1)} %get-tuple-element.16), channel_id=1, source_target_pairs={{0,8},{4,12},{8,0},{12,4},{16,24},{20,28},{24,16},{28,20},{1,9},{5... | collective-permute-start | bytes 196616 | tf_op jit(solution)/shard_map/ppermute | solution.py:221
  9.9 4.3 %collective-permute-start.2 = (bf16[16,2048]{1,0:T(8,128)(2,1)S(1)}, bf16[16,2048]{1,0:T(8,128)(2,1)S(1)}, u32[]{:S(2)}, u32[]{:S(2)}) collective-permute-start(bf16[16,2048]{1,0:T(8,128)(2,1)S(1)} %collective-permute-done.1), channel_id=1, source_target_pairs={{0,8},{4,12},{8,0},{12,4},{16,24},{20,28},{24,16},{28,20},{1,9},{5... | collective-permute-start | bytes 196616 | tf_op jit(solution)/shard_map/ppermute | solution.py:221
  14.2 5.8 %collective-permute-start.6 = (bf16[32,2048]{1,0:T(8,128)(2,1)S(1)}, bf16[32,2048]{1,0:T(8,128)(2,1)S(1)}, u32[]{:S(2)}, u32[]{:S(2)}) collective-permute-start(bf16[32,2048]{1,0:T(8,128)(2,1)S(1)} %constant_dynamic-update-slice_fusion.2.refs_1_), channel_id=1, source_target_pairs={{0,4},{4,0},{8,12},{12,8},{16,20},{20,16},{24,28},{28,24},{1,5},{5... | collective-permute-start | bytes 393224 | tf_op jit(solution)/shard_map/ppermute | solution.py:221
  15.9 6.4 %collective-permute-start.3 = (bf16[32,2048]{1,0:T(8,128)(2,1)S(1)}, bf16[32,2048]{1,0:T(8,128)(2,1)S(1)}, u32[]{:S(2)}, u32[]{:S(2)}) collective-permute-start(bf16[32,2048]{1,0:T(8,128)(2,1)S(1)} %constant_dynamic-update-slice_fusion.refs_0_), channel_id=1, source_target_pairs={{0,4},{4,0},{8,12},{12,8},{16,20},{20,16},{24,28},{28,24},{1,5},{5... | collective-permute-start | bytes 393224 | tf_op jit(solution)/shard_map/ppermute | solution.py:221
  20.7 5.0 %collective-permute-start.7 = (bf16[32,2048]{1,0:T(8,128)(2,1)S(1)}, bf16[32,2048]{1,0:T(8,128)(2,1)S(1)}, u32[]{:S(2)}, u32[]{:S(2)}) collective-permute-start(bf16[32,2048]{1,0:T(8,128)(2,1)S(1)} %expert_slice.3), channel_id=1, source_target_pairs={{0,4},{4,0},{8,12},{12,8},{16,20},{20,16},{24,28},{28,24},{1,5},{5... | collective-permute-start | bytes 393224 | tf_op jit(solution)/shard_map/ppermute | solution.py:221
  23.2 5.0 %collective-permute-start.4 = (bf16[32,2048]{1,0:T(8,128)(2,1)S(1)}, bf16[32,2048]{1,0:T(8,128)(2,1)S(1)}, u32[]{:S(2)}, u32[]{:S(2)}) collective-permute-start(bf16[32,2048]{1,0:T(8,128)(2,1)S(1)} %get-tuple-element.21), channel_id=1, source_target_pairs={{0,4},{4,0},{8,12},{12,8},{16,20},{20,16},{24,28},{28,24},{1,5},{5... | collective-permute-start | bytes 393224 | tf_op jit(solution)/shard_map/ppermute | solution.py:221
  25.8 4.7 %collective-permute-start.8 = (bf16[16,2048]{1,0:T(8,128)(2,1)S(1)}, bf16[16,2048]{1,0:T(8,128)(2,1)S(1)}, u32[]{:S(2)}, u32[]{:S(2)}) collective-permute-start(bf16[16,2048]{1,0:T(8,128)(2,1)S(1)} %add_convert_fusion.1), channel_id=1, source_target_pairs={{0,8},{4,12},{8,0},{12,4},{16,24},{20,28},{24,16},{28,20},{1,9},{5... | collective-permute-start | bytes 196616 | tf_op jit(solution)/shard_map/ppermute | solution.py:221
  28.2 4.3 %collective-permute-start.5 = (bf16[16,2048]{1,0:T(8,128)(2,1)S(1)}, bf16[16,2048]{1,0:T(8,128)(2,1)S(1)}, u32[]{:S(2)}, u32[]{:S(2)}) collective-permute-start(bf16[16,2048]{1,0:T(8,128)(2,1)S(1)} %get-tuple-element.23), channel_id=1, source_target_pairs={{0,8},{4,12},{8,0},{12,4},{16,24},{20,28},{24,16},{28,20},{1,9},{5... | collective-permute-start | bytes 196616 | tf_op jit(solution)/shard_map/ppermute | solution.py:221
  30.5 5.9 %collective-permute-start.9 = (bf16[16,2048]{1,0:T(8,128)(2,1)S(1)}, bf16[16,2048]{1,0:T(8,128)(2,1)S(1)}, u32[]{:S(2)}, u32[]{:S(2)}) collective-permute-start(bf16[16,2048]{1,0:T(8,128)(2,1)S(1)} %add_convert_fusion), channel_id=1, source_target_pairs={{0,16},{4,20},{8,24},{12,28},{16,0},{20,4},{24,8},{28,12},{1,17},{... | collective-permute-start | bytes 196616 | tf_op jit(solution)/shard_map/ppermute | solution.py:221

commit v6 on v5

--- a/solution.py
+++ b/solution.py
@@ -143,23 +143,23 @@
     return rows, weights
 
 
-def slice_kernel(*refs):
-    count = (len(refs) - 3) // 2
-    expert_blocks(refs[:count], refs[count : count + 3], refs[count + 3 :])
-
-
-def expert_slice(blocks, weights):
+def slice_kernel(count, *refs):
+    outs = refs[len(refs) - count :]
+    expert_blocks(refs[:count], refs[count : count + 3], outs)
+
+
+def expert_slice(blocks, weights, after=()):
     vmem = pl.BlockSpec(memory_space=pltpu.VMEM)
     count = len(blocks)
     return pl.pallas_call(
-        slice_kernel,
+        functools.partial(slice_kernel, count),
         out_shape=[jax.ShapeDtypeStruct(block.shape, jnp.bfloat16) for block in blocks],
-        in_specs=[vmem] * (count + 3),
+        in_specs=[vmem] * (count + 3) + [pl.BlockSpec(memory_space=pl.ANY)] * len(after),
         out_specs=[vmem] * count,
         compiler_params=pltpu.CompilerParams(vmem_limit_bytes=VMEM_LIMIT),
         cost_estimate=expert_cost(blocks, weights),
         name="expert_slice",
-    )(*blocks, *weights)
+    )(*blocks, *weights, *after)
 
 
 def add_level(kept, came):
@@ -230,20 +230,18 @@
         slots, live_counts, expert_ids.T, gate_vals.T, tokens, norm_gain.reshape(1, features)
     )
     own = across_groups(flight, rows)
-    far = swap(devices, 4, own)
+    farther, far = swap(devices, 6, own), swap(devices, 4, own)
     own, weights = stage_weights(own, (w_gate.T, w_up.T, w_down))
     near = swap(devices, 2, own)
-    farther = swap(devices, 2, far)
-    inner, outer = jnp.concatenate([own, near]), jnp.concatenate([far, farther])
-    inner_y, outer_y = swap(devices, 1, inner), swap(devices, 1, outer)
-    inner, outer, inner_y = expert_slice((inner, outer, inner_y), weights)
+    outer, inner = jnp.concatenate([far, farther]), jnp.concatenate([own, near])
+    outer_y, inner_y = swap(devices, 1, outer), swap(devices, 1, inner)
     (outer_y,) = expert_slice((outer_y,), weights)
-    inner_y, outer_y = swap(devices, 1, inner_y), swap(devices, 1, outer_y)
+    outer, inner, inner_y = expert_slice((outer, inner, inner_y), weights, (outer_y,))
+    outer_y, inner_y = swap(devices, 1, outer_y), swap(devices, 1, inner_y)
+    far, farther = (add_level(outer[at], outer_y[at]) for at in (slice(slots), slice(slots, None)))
     own, near = (add_level(inner[at], inner_y[at]) for at in (slice(slots), slice(slots, None)))
-    far, farther = (add_level(outer[at], outer_y[at]) for at in (slice(slots), slice(slots, None)))
-    near = swap(devices, 2, near)
-    far = swap(devices, 4, add_level(far, swap(devices, 2, farther)))
-    parts = [own, near, far]
+    farther, far = swap(devices, 6, farther), swap(devices, 4, far)
+    parts = [own, swap(devices, 2, near), add_level(far, farther)]
     if flight > 1:
         parts = [across_groups(flight, functools.reduce(add_level, parts))]
     return combine(table, parts)

time: 37.7 us -> 34 us (0.902)
  waiting for transfers between devices: 17 us -> 12.5 us
  starting transfers between devices: 13.7 us -> 14.5 us
    ppermute x10, waiting for transfers between devices: 17 us -> 12.5 us  [swap(): lax.ppermute(block, 'ep', [(i, i ^ distance) for i in range(devices)])]
    ppermute x10, starting transfers between devices: 13.7 us -> 14.5 us  [swap(): lax.ppermute(block, 'ep', [(i, i ^ distance) for i in range(devices)])]
  transfers between devices with their start and end apart: 10 -> 10, of which waited for: 8 -> 7; matrix products, arithmetic and copies ran while one was open for 0% -> 0% of each run, Pallas kernels for 9% -> 10%
where the time goes in v6:
time: 34 us; the launch traced here: 33.8 us
  starting transfers between devices  14.5 us (43%)
  waiting for transfers between devices  12.5 us (37%)
  Pallas kernels  5.97 us (18%)
  between operations  0.72 us (2%)
    ppermute x10, starting transfers between devices, swap(): lax.ppermute(block, 'ep', [(i, i ^ distance) for i in range(devices)])  14.5 us
    ppermute x10, waiting for transfers between devices, swap(): lax.ppermute(block, 'ep', [(i, i ^ distance) for i in range(devices)])  12.5 us
    pallas_call x1, Pallas kernels, stage_weights(): pl.pallas_call(stage_kernel, out_shape=[jax.ShapeDtypeStruct(array.shape,...  1.8 us
    pallas_call x2, Pallas kernels, expert_slice(): pl.pallas_call(functools.partial(slice_kernel, count), out_shape=[jax.Sha...  1.66 us
    pallas_call x1, Pallas kernels, pick_rows(): pl.pallas_call(pick_kernel, out_shape=(jax.ShapeDtypeStruct((slots, token...  1.47 us
    pallas_call x1, Pallas kernels, combine(): pl.pallas_call(combine_kernel, out_shape=jax.ShapeDtypeStruct(shape, jnp....  1.04 us
  transfers between devices with their start and end apart: 10, of which 7 were waited for; matrix products, arithmetic and copies ran while one was open for 0% of the time, Pallas kernels for 10%

profile of v6, /device:TPU:0, one launch (start us, length us, event | category | flops | bytes accessed | tf_op | source)
XLA Modules:
  0.0 33.8 jit_solution(17885498455066788495)
XLA Ops:
  0.7 1.5 %pick_rows.1 = (bf16[16,2048]{1,0:T(8,128)(2,1)S(1)}, f32[16,128]{1,0:T(8,128)S(1)}) custom-call(s32[1]{0:T(128)S(6)} %copy.11.live_ref, s32[8,128]{1,0:T(8,128)} %bitcast.8, f32[8,128]{1,0:T(8,128)} %bitcast.9, bf16[128,2048]{1,0:T(8,128)(2,1)} %tokens_hbm.1, f32[1,2048]{1,0:T(1,128)} %bitcast.7), custom_call_target="tpu_custom_call" | custom-call | tf_op jit(solution)/shard_map/pick_rows/pallas_call | solution.py:62
  2.1 5.1 %collective-permute-start.1 = (bf16[16,2048]{1,0:T(8,128)(2,1)S(1)}, bf16[16,2048]{1,0:T(8,128)(2,1)S(1)}, u32[]{:S(2)}, u32[]{:S(2)}) collective-permute-start(bf16[16,2048]{1,0:T(8,128)(2,1)S(1)} %get-tuple-element.15.rows_ref), channel_id=1, source_target_pairs={{0,24},{4,28},{8,16},{12,20},{16,8},{20,12},{24,0},{28,4},{1,25},{... | collective-permute-start | bytes 196616 | tf_op jit(solution)/shard_map/ppermute | solution.py:221
  7.2 0.0 collective-permute-start
  7.2 1.8 %stage_weights.1 = (bf16[16,2048]{1,0:T(8,128)(2,1)S(1)}, bf16[192,2048]{1,0:T(8,128)(2,1)S(1)}, bf16[192,2048]{1,0:T(8,128)(2,1)S(1)}, bf16[192,2048]{1,0:T(8,128)(2,1)S(1)}) custom-call(bf16[16,2048]{1,0:T(8,128)(2,1)S(1)} %get-tuple-element.15.rows_ref, bf16[192,2048]{1,0:T(8,128)(2,1)} %bitcast.5, bf16[192,2048]{1,0:T(8,128)(2,1)} %bitcast.6, ...), custom_call_target="tpu_custom_call" | custom-call | flops 37748736 | bytes 2359296 | tf_op jit(solution)/shard_map/stage_weights/pallas_call | solution.py:133
  9.1 0.7 %collective-permute-start.2 = (bf16[16,2048]{1,0:T(8,128)(2,1)S(1)}, bf16[16,2048]{1,0:T(8,128)(2,1)S(1)}, u32[]{:S(2)}, u32[]{:S(2)}) collective-permute-start(bf16[16,2048]{1,0:T(8,128)(2,1)S(1)} %get-tuple-element.16), channel_id=1, source_target_pairs={{0,8},{4,12},{8,0},{12,4},{16,24},{20,28},{24,16},{28,20},{1,9},{5... | collective-permute-start | bytes 196616 | tf_op jit(solution)/shard_map/ppermute | solution.py:221
  9.8 3.2 %collective-permute-done = bf16[16,2048]{1,0:T(8,128)(2,1)S(1)} collective-permute-done((bf16[16,2048]{1,0:T(8,128)(2,1)S(1)}, bf16[16,2048]{1,0:T(8,128)(2,1)S(1)}, u32[]{:S(2)}, u32[]{:S(2)}) %collective-permute-start) | collective-permute-done | bytes 65568 | tf_op jit(solution)/shard_map/ppermute | solution.py:221
  13.0 0.0 collective-permute-done.1
  13.0 1.6 %collective-permute-start.4 = (bf16[32,2048]{1,0:T(8,128)(2,1)S(1)}, bf16[32,2048]{1,0:T(8,128)(2,1)S(1)}, u32[]{:S(2)}, u32[]{:S(2)}) collective-permute-start(bf16[32,2048]{1,0:T(8,128)(2,1)S(1)} %constant_dynamic-update-slice_fusion.refs_0_), channel_id=1, source_target_pairs={{0,4},{4,0},{8,12},{12,8},{16,20},{20,16},{24,28},{28,24},{1,5},{5... | collective-permute-start | bytes 393224 | tf_op jit(solution)/shard_map/ppermute | solution.py:221
  14.6 0.0 collective-permute-done.2
  14.6 0.9 %collective-permute-start.3 = (bf16[32,2048]{1,0:T(8,128)(2,1)S(1)}, bf16[32,2048]{1,0:T(8,128)(2,1)S(1)}, u32[]{:S(2)}, u32[]{:S(2)}) collective-permute-start(bf16[32,2048]{1,0:T(8,128)(2,1)S(1)} %constant_dynamic-update-slice_fusion.2.refs_1_), channel_id=1, source_target_pairs={{0,4},{4,0},{8,12},{12,8},{16,20},{20,16},{24,28},{28,24},{1,5},{5... | collective-permute-start | bytes 393224 | tf_op jit(solution)/shard_map/ppermute | solution.py:221
  15.5 3.8 %collective-permute-done.4.refs_0_ = bf16[32,2048]{1,0:T(8,128)(2,1)S(1)} collective-permute-done((bf16[32,2048]{1,0:T(8,128)(2,1)S(1)}, bf16[32,2048]{1,0:T(8,128)(2,1)S(1)}, u32[]{:S(2)}, u32[]{:S(2)}) %collective-permute-start.4) | collective-permute-done | bytes 131104 | tf_op jit(solution)/shard_map/ppermute | solution.py:221
  19.3 0.8 %expert_slice.2.refs_6_ = bf16[32,2048]{1,0:T(8,128)(2,1)S(1)} custom-call(bf16[32,2048]{1,0:T(8,128)(2,1)S(1)} %collective-permute-done.4.refs_0_, bf16[192,2048]{1,0:T(8,128)(2,1)S(1)} %get-tuple-element.17.refs_1_.refs_3_, bf16[192,2048]{1,0:T(8,128)(2,1)S(1)} %get-tuple-element.18.refs_2_.refs_4_, bf16[192,2048]{1,0:T(8,128)(2,1)S(1)} %get-tuple-element.19.refs_3_.refs_5_), custom_call_target="tpu_custom_call" | custom-call | flops 75497472 | bytes 2359296 | tf_op jit(solution)/shard_map/expert_slice/pallas_call | solution.py:154
  20.1 1.7 %collective-permute-start.7 = (bf16[32,2048]{1,0:T(8,128)(2,1)S(1)}, bf16[32,2048]{1,0:T(8,128)(2,1)S(1)}, u32[]{:S(2)}, u32[]{:S(2)}) collective-permute-start(bf16[32,2048]{1,0:T(8,128)(2,1)S(1)} %expert_slice.2.refs_6_), channel_id=1, source_target_pairs={{0,4},{4,0},{8,12},{12,8},{16,20},{20,16},{24,28},{28,24},{1,5},{5... | collective-permute-start | bytes 393224 | tf_op jit(solution)/shard_map/ppermute | solution.py:221
  21.8 0.0 collective-permute-done.3.refs_2_
  21.8 0.9 %expert_slice.3 = (bf16[32,2048]{1,0:T(8,128)(2,1)S(1)}, bf16[32,2048]{1,0:T(8,128)(2,1)S(1)}, bf16[32,2048]{1,0:T(8,128)(2,1)S(1)}) custom-call(bf16[32,2048]{1,0:T(8,128)(2,1)S(1)} %constant_dynamic-update-slice_fusion.refs_0_, bf16[32,2048]{1,0:T(8,128)(2,1)S(1)} %constant_dynamic-update-slice_fusion.2.refs_1_, ...), custom_call_target="tpu_custom_call" | custom-call | flops 226492416 | bytes 2359296 | tf_op jit(solution)/shard_map/expert_slice/pallas_call | solution.py:154
  22.7 1.2 %collective-permute-start.5 = (bf16[32,2048]{1,0:T(8,128)(2,1)S(1)}, bf16[32,2048]{1,0:T(8,128)(2,1)S(1)}, u32[]{:S(2)}, u32[]{:S(2)}) collective-permute-start(bf16[32,2048]{1,0:T(8,128)(2,1)S(1)} %get-tuple-element.21), channel_id=1, source_target_pairs={{0,4},{4,0},{8,12},{12,8},{16,20},{20,16},{24,28},{28,24},{1,5},{5... | collective-permute-start | bytes 393224 | tf_op jit(solution)/shard_map/ppermute | solution.py:221
  23.9 2.1 %collective-permute-done.7 = bf16[32,2048]{1,0:T(8,128)(2,1)S(1)} collective-permute-done((bf16[32,2048]{1,0:T(8,128)(2,1)S(1)}, bf16[32,2048]{1,0:T(8,128)(2,1)S(1)}, u32[]{:S(2)}, u32[]{:S(2)}) %collective-permute-start.7) | collective-permute-done | bytes 131104 | tf_op jit(solution)/shard_map/ppermute | solution.py:221
  26.0 0.1 collective-permute-start.8
  26.1 1.4 %collective-permute-start.9 = (bf16[16,2048]{1,0:T(8,128)(2,1)S(1)}, bf16[16,2048]{1,0:T(8,128)(2,1)S(1)}, u32[]{:S(2)}, u32[]{:S(2)}) collective-permute-start(bf16[16,2048]{1,0:T(8,128)(2,1)S(1)} %get-tuple-element.24), channel_id=1, source_target_pairs={{0,24},{4,28},{8,16},{12,20},{16,8},{20,12},{24,0},{28,4},{1,25},{... | collective-permute-start | bytes 196616 | tf_op jit(solution)/shard_map/ppermute | solution.py:221
  27.4 0.3 collective-permute-done.5
  27.8 1.9 %collective-permute-start.6 = (bf16[16,2048]{1,0:T(8,128)(2,1)S(1)}, bf16[16,2048]{1,0:T(8,128)(2,1)S(1)}, u32[]{:S(2)}, u32[]{:S(2)}) collective-permute-start(bf16[16,2048]{1,0:T(8,128)(2,1)S(1)} %get-tuple-element.25), channel_id=1, source_target_pairs={{0,8},{4,12},{8,0},{12,4},{16,24},{20,28},{24,16},{28,20},{1,9},{5... | collective-permute-start | bytes 196616 | tf_op jit(solution)/shard_map/ppermute | solution.py:221
  29.7 1.6 %collective-permute-done.8 = bf16[16,2048]{1,0:T(8,128)(2,1)S(1)} collective-permute-done((bf16[16,2048]{1,0:T(8,128)(2,1)S(1)}, bf16[16,2048]{1,0:T(8,128)(2,1)S(1)}, u32[]{:S(2)}, u32[]{:S(2)}) %collective-permute-start.8) | collective-permute-done | bytes 65568 | tf_op jit(solution)/shard_map/ppermute | solution.py:221
  31.2 1.1 %collective-permute-done.9 = bf16[16,2048]{1,0:T(8,128)(2,1)S(1)} collective-permute-done((bf16[16,2048]{1,0:T(8,128)(2,1)S(1)}, bf16[16,2048]{1,0:T(8,128)(2,1)S(1)}, u32[]{:S(2)}, u32[]{:S(2)}) %collective-permute-start.9) | collective-permute-done | bytes 65568 | tf_op jit(solution)/shard_map/ppermute | solution.py:221
  32.4 0.4 %collective-permute-done.6.refs_1_ = bf16[16,2048]{1,0:T(8,128)(2,1)S(1)} collective-permute-done((bf16[16,2048]{1,0:T(8,128)(2,1)S(1)}, bf16[16,2048]{1,0:T(8,128)(2,1)S(1)}, u32[]{:S(2)}, u32[]{:S(2)}) %collective-permute-start.6) | collective-permute-done | bytes 65568 | tf_op jit(solution)/shard_map/ppermute | solution.py:221
  32.8 1.0 %combine.1 = bf16[128,2048]{1,0:T(8,128)(2,1)} custom-call(f32[16,128]{1,0:T(8,128)S(1)} %get-tuple-element.14.table_ref, bf16[16,2048]{1,0:T(8,128)(2,1)S(1)} %get-tuple-element.26.refs_0_, bf16[16,2048]{1,0:T(8,128)(2,1)S(1)} %collective-permute-done.6.refs_1_, bf16[16,2048]{1,0:T(8,128)(2,1)S(1)} %add_convert_fusion.refs_2_), custom_call_target="tpu_custom_call" | custom-call | tf_op jit(solution)/shard_map/combine/pallas_call | solution.py:200
  (7 shorter events, 0.1 us)
Async XLA Ops:
  2.1 10.8 %collective-permute-start.1 = (bf16[16,2048]{1,0:T(8,128)(2,1)S(1)}, bf16[16,2048]{1,0:T(8,128)(2,1)S(1)}, u32[]{:S(2)}, u32[]{:S(2)}) collective-permute-start(bf16[16,2048]{1,0:T(8,128)(2,1)S(1)} %get-tuple-element.15.rows_ref), channel_id=1, source_target_pairs={{0,24},{4,28},{8,16},{12,20},{16,8},{20,12},{24,0},{28,4},{1,25},{... | collective-permute-start | bytes 196616 | tf_op jit(solution)/shard_map/ppermute | solution.py:221
  7.2 5.7 %collective-permute-start = (bf16[16,2048]{1,0:T(8,128)(2,1)S(1)}, bf16[16,2048]{1,0:T(8,128)(2,1)S(1)}, u32[]{:S(2)}, u32[]{:S(2)}) collective-permute-start(bf16[16,2048]{1,0:T(8,128)(2,1)S(1)} %get-tuple-element.15.rows_ref), channel_id=1, source_target_pairs={{0,16},{4,20},{8,24},{12,28},{16,0},{20,4},{24,8},{28,12},{1,17},{... | collective-permute-start | bytes 196616 | tf_op jit(solution)/shard_map/ppermute | solution.py:221
  9.1 5.5 %collective-permute-start.2 = (bf16[16,2048]{1,0:T(8,128)(2,1)S(1)}, bf16[16,2048]{1,0:T(8,128)(2,1)S(1)}, u32[]{:S(2)}, u32[]{:S(2)}) collective-permute-start(bf16[16,2048]{1,0:T(8,128)(2,1)S(1)} %get-tuple-element.16), channel_id=1, source_target_pairs={{0,8},{4,12},{8,0},{12,4},{16,24},{20,28},{24,16},{28,20},{1,9},{5... | collective-permute-start | bytes 196616 | tf_op jit(solution)/shard_map/ppermute | solution.py:221
  13.0 6.3 %collective-permute-start.4 = (bf16[32,2048]{1,0:T(8,128)(2,1)S(1)}, bf16[32,2048]{1,0:T(8,128)(2,1)S(1)}, u32[]{:S(2)}, u32[]{:S(2)}) collective-permute-start(bf16[32,2048]{1,0:T(8,128)(2,1)S(1)} %constant_dynamic-update-slice_fusion.refs_0_), channel_id=1, source_target_pairs={{0,4},{4,0},{8,12},{12,8},{16,20},{20,16},{24,28},{28,24},{1,5},{5... | collective-permute-start | bytes 393224 | tf_op jit(solution)/shard_map/ppermute | solution.py:221
  14.6 7.3 %collective-permute-start.3 = (bf16[32,2048]{1,0:T(8,128)(2,1)S(1)}, bf16[32,2048]{1,0:T(8,128)(2,1)S(1)}, u32[]{:S(2)}, u32[]{:S(2)}) collective-permute-start(bf16[32,2048]{1,0:T(8,128)(2,1)S(1)} %constant_dynamic-update-slice_fusion.2.refs_1_), channel_id=1, source_target_pairs={{0,4},{4,0},{8,12},{12,8},{16,20},{20,16},{24,28},{28,24},{1,5},{5... | collective-permute-start | bytes 393224 | tf_op jit(solution)/shard_map/ppermute | solution.py:221
  20.1 5.8 %collective-permute-start.7 = (bf16[32,2048]{1,0:T(8,128)(2,1)S(1)}, bf16[32,2048]{1,0:T(8,128)(2,1)S(1)}, u32[]{:S(2)}, u32[]{:S(2)}) collective-permute-start(bf16[32,2048]{1,0:T(8,128)(2,1)S(1)} %expert_slice.2.refs_6_), channel_id=1, source_target_pairs={{0,4},{4,0},{8,12},{12,8},{16,20},{20,16},{24,28},{28,24},{1,5},{5... | collective-permute-start | bytes 393224 | tf_op jit(solution)/shard_map/ppermute | solution.py:221
  22.7 5.0 %collective-permute-start.5 = (bf16[32,2048]{1,0:T(8,128)(2,1)S(1)}, bf16[32,2048]{1,0:T(8,128)(2,1)S(1)}, u32[]{:S(2)}, u32[]{:S(2)}) collective-permute-start(bf16[32,2048]{1,0:T(8,128)(2,1)S(1)} %get-tuple-element.21), channel_id=1, source_target_pairs={{0,4},{4,0},{8,12},{12,8},{16,20},{20,16},{24,28},{28,24},{1,5},{5... | collective-permute-start | bytes 393224 | tf_op jit(solution)/shard_map/ppermute | solution.py:221
  26.0 5.2 %collective-permute-start.8 = (bf16[16,2048]{1,0:T(8,128)(2,1)S(1)}, bf16[16,2048]{1,0:T(8,128)(2,1)S(1)}, u32[]{:S(2)}, u32[]{:S(2)}) collective-permute-start(bf16[16,2048]{1,0:T(8,128)(2,1)S(1)} %get-tuple-element.23), channel_id=1, source_target_pairs={{0,16},{4,20},{8,24},{12,28},{16,0},{20,4},{24,8},{28,12},{1,17},{... | collective-permute-start | bytes 196616 | tf_op jit(solution)/shard_map/ppermute | solution.py:221
  26.1 6.3 %collective-permute-start.9 = (bf16[16,2048]{1,0:T(8,128)(2,1)S(1)}, bf16[16,2048]{1,0:T(8,128)(2,1)S(1)}, u32[]{:S(2)}, u32[]{:S(2)}) collective-permute-start(bf16[16,2048]{1,0:T(8,128)(2,1)S(1)} %get-tuple-element.24), channel_id=1, source_target_pairs={{0,24},{4,28},{8,16},{12,20},{16,8},{20,12},{24,0},{28,4},{1,25},{... | collective-permute-start | bytes 196616 | tf_op jit(solution)/shard_map/ppermute | solution.py:221
  27.8 5.0 %collective-permute-start.6 = (bf16[16,2048]{1,0:T(8,128)(2,1)S(1)}, bf16[16,2048]{1,0:T(8,128)(2,1)S(1)}, u32[]{:S(2)}, u32[]{:S(2)}) collective-permute-start(bf16[16,2048]{1,0:T(8,128)(2,1)S(1)} %get-tuple-element.25), channel_id=1, source_target_pairs={{0,8},{4,12},{8,0},{12,4},{16,24},{20,28},{24,16},{28,20},{1,9},{5... | collective-permute-start | bytes 196616 | tf_op jit(solution)/shard_map/ppermute | solution.py:221

commit v7 on v6

--- a/solution.py
+++ b/solution.py
@@ -230,20 +230,16 @@
         slots, live_counts, expert_ids.T, gate_vals.T, tokens, norm_gain.reshape(1, features)
     )
     own = across_groups(flight, rows)
-    farther, far = swap(devices, 6, own), swap(devices, 4, own)
-    own, weights = stage_weights(own, (w_gate.T, w_up.T, w_down))
-    near = swap(devices, 2, own)
-    outer, inner = jnp.concatenate([far, farther]), jnp.concatenate([own, near])
-    outer_y, inner_y = swap(devices, 1, outer), swap(devices, 1, inner)
-    (outer_y,) = expert_slice((outer_y,), weights)
-    outer, inner, inner_y = expert_slice((outer, inner, inner_y), weights, (outer_y,))
-    outer_y, inner_y = swap(devices, 1, outer_y), swap(devices, 1, inner_y)
-    far, farther = (add_level(outer[at], outer_y[at]) for at in (slice(slots), slice(slots, None)))
-    own, near = (add_level(inner[at], inner_y[at]) for at in (slice(slots), slice(slots, None)))
-    farther, far = swap(devices, 6, farther), swap(devices, 4, far)
-    parts = [own, swap(devices, 2, near), add_level(far, farther)]
-    if flight > 1:
-        parts = [across_groups(flight, functools.reduce(add_level, parts))]
+    weights = (w_gate.T, w_up.T, w_down)
+    own, weights = stage_weights(own, weights)
+    groups = [[g * SLICES + m for m in range(SLICES)] for g in range(flight)]
+    groups = None if flight == 1 else groups
+    arrived = lax.all_gather(own, "ep", axis_index_groups=groups, tiled=True)
+    (partial_out,) = expert_slice((arrived,), weights)
+    summed = lax.psum_scatter(
+        partial_out, "ep", scatter_dimension=0, axis_index_groups=groups, tiled=True
+    )
+    parts = [across_groups(flight, summed)]
     return combine(table, parts)
 
 

time: 34 us -> 118 us (3.47)
  waiting for transfers between devices: 12.5 us -> 63.7 us
  blocking collectives: 0 us -> 33 us
  starting transfers between devices: 14.5 us -> 0.01 us
  between operations: 0.72 us -> 14.1 us
    reduce_scatter x0 -> x1, waiting for transfers between devices: none -> 63.6 us  [on_device(): lax.psum_scatter(partial_out, 'ep', scatter_dimension=0, axis_index_group...]
    all_gather x0 -> x1, blocking collectives: none -> 33 us  [on_device(): arrived = lax.all_gather(own, 'ep', axis_index_groups=groups, tiled=True)]
    ppermute x10 -> x0, starting transfers between devices: 14.5 us -> none  [swap(): lax.ppermute(block, 'ep', [(i, i ^ distance) for i in range(devices)])]
    ppermute x10 -> x0, waiting for transfers between devices: 12.5 us -> none  [swap(): lax.ppermute(block, 'ep', [(i, i ^ distance) for i in range(devices)])]
  transfers between devices with their start and end apart: 10 -> 1, of which waited for: 7 -> 1; matrix products, arithmetic and copies ran while one was open for 0% -> 0% of each run, Pallas kernels for 10% -> 0%
where the time goes in v7:
time: 118 us
  waiting for transfers between devices  63.7 us (54%)
  blocking collectives  33 us (28%)
  between operations  14.1 us (12%)
  Pallas kernels  6.01 us (5%)
    reduce_scatter x1, waiting for transfers between devices, on_device(): lax.psum_scatter(partial_out, 'ep', scatter_dimension=0, axis_index_group...  63.6 us
    all_gather x1, blocking collectives, on_device(): arrived = lax.all_gather(own, 'ep', axis_index_groups=groups, tiled=True)  33 us
  transfers between devices with their start and end apart: 1, of which 1 were waited for; matrix products, arithmetic and copies ran while one was open for 0% of the time, Pallas kernels for 0%

profile of v7, /device:TPU:0, one launch (start us, length us, event | category | flops | bytes accessed | tf_op | source)
XLA Modules:
  0.0 117.6 jit_solution(2187279506185607808)
XLA Ops:
  6.5 0.0 reduce-scatter.2.cloned.1.call-start
  7.2 1.5 %pick_rows.1 = (bf16[16,2048]{1,0:T(8,128)(2,1)S(1)}, f32[16,128]{1,0:T(8,128)S(1)}) custom-call(s32[1]{0:T(128)S(6)} %copy.9.live_ref, s32[8,128]{1,0:T(8,128)} %bitcast.8, f32[8,128]{1,0:T(8,128)} %bitcast.9, bf16[128,2048]{1,0:T(8,128)(2,1)} %tokens_hbm.1, f32[1,2048]{1,0:T(1,128)} %bitcast.7), custom_call_target="tpu_custom_call" | custom-call | tf_op jit(solution)/shard_map/pick_rows/pallas_call | solution.py:62
  8.7 1.8 %stage_weights.1 = (bf16[16,2048]{1,0:T(8,128)(2,1)S(1)}, bf16[192,2048]{1,0:T(8,128)(2,1)S(1)}, bf16[192,2048]{1,0:T(8,128)(2,1)S(1)}, bf16[192,2048]{1,0:T(8,128)(2,1)S(1)}) custom-call(bf16[16,2048]{1,0:T(8,128)(2,1)S(1)} %get-tuple-element.12.rows_ref, bf16[192,2048]{1,0:T(8,128)(2,1)} %bitcast.5, bf16[192,2048]{1,0:T(8,128)(2,1)} %bitcast.6, ...), custom_call_target="tpu_custom_call" | custom-call | flops 37748736 | bytes 2359296 | tf_op jit(solution)/shard_map/stage_weights/pallas_call | solution.py:133
  10.5 33.0 %all_gather.3.refs_0_ = bf16[128,2048]{1,0:T(8,128)(2,1)S(1)} all-gather(bf16[16,2048]{1,0:T(8,128)(2,1)S(1)} %get-tuple-element.13), channel_id=1, replica_groups=mesh['ep'=8,'sp'=4] {'ep'}, dimensions={0}, use_global_device_ids=true | all-gather | bytes 589824 | tf_op jit(solution)/shard_map/all_gather | solution.py:237
  43.5 1.7 %expert_slice.1 = bf16[128,2048]{1,0:T(8,128)(2,1)} custom-call(bf16[128,2048]{1,0:T(8,128)(2,1)S(1)} %all_gather.3.refs_0_, bf16[192,2048]{1,0:T(8,128)(2,1)S(1)} %get-tuple-element.14.refs_1_, bf16[192,2048]{1,0:T(8,128)(2,1)S(1)} %get-tuple-element.15.refs_2_, bf16[192,2048]{1,0:T(8,128)(2,1)S(1)} %get-tuple-element.16.refs_3_), custom_call_target="tpu_custom_call" | custom-call | flops 301989888 | bytes 2359296 | tf_op jit(solution)/shard_map/expert_slice/pallas_call | solution.py:154
  45.2 0.0 reduce-scatter.2.cloned.1.call-update
  45.2 63.6 %reduce-scatter.2.cloned.1.call-done.refs_0_ = bf16[16,2048]{1,0:T(8,128)(2,1)} async-done(((bf16[128,2048]{1,0:T(8,128)(2,1)}), bf16[16,2048]{1,0:T(8,128)(2,1)}) %reduce-scatter.2.cloned.1.call-update) | async-done | bytes 65552 | tf_op jit(solution)/shard_map/reduce_scatter | solution.py:239
  108.8 0.0 copy-start
  108.8 0.8 copy-done
  109.7 1.0 combine.1
Async XLA Ops:
  6.5 102.3 %reduce-scatter.2.cloned.1.call-start = ((), (), s32[]{:S(2)}) async-start(), calls=%async_computation.1 | async-start | bytes 589824 | tf_op jit(solution)/shard_map/reduce_scatter | solution.py:239
  108.8 0.8 copy-start
Sparse Core Ops, SparseCore 0:
  45.3 63.4 reduce-scatter.1

commit v8 on v7

--- a/solution.py
+++ b/solution.py
@@ -112,9 +112,9 @@
         yield pltpu.make_async_copy(source.at[at], target.at[at], sems.at[i])
 
 
-def stage_kernel(rows_ref, *refs):
+def stage_kernel(count, *refs):
     *refs, sems = refs
-    sources, out_ref, weights = refs[:3], refs[3], refs[4:]
+    blocks, sources, out_ref, weights = refs[:count], refs[count : count + 3], refs[-4], refs[-3:]
     copies = [
         copy
         for i, pair in enumerate(zip(sources, weights))
@@ -122,25 +122,30 @@
     ]
     for copy in copies:
         copy.start()
-    out_ref[...] = rows_ref[...]
+    at = 0
+    for ref in blocks:
+        out_ref[at : at + ref.shape[0]] = ref[...]
+        at += ref.shape[0]
     for copy in copies:
         copy.wait()
 
 
-def stage_weights(rows, weights):
+def stage_weights(blocks, weights, after=()):
     vmem = pl.BlockSpec(memory_space=pltpu.VMEM)
     hbm = pl.BlockSpec(memory_space=pltpu.HBM)
-    rows, *weights = pl.pallas_call(
-        stage_kernel,
-        out_shape=[jax.ShapeDtypeStruct(array.shape, array.dtype) for array in (rows, *weights)],
-        in_specs=[vmem] + [hbm] * 3,
+    rows = sum(block.shape[0] for block in blocks)
+    joined = jax.ShapeDtypeStruct((rows, blocks[0].shape[1]), jnp.bfloat16)
+    joined, *weights = pl.pallas_call(
+        functools.partial(stage_kernel, len(blocks)),
+        out_shape=[joined] + [jax.ShapeDtypeStruct(array.shape, array.dtype) for array in weights],
+        in_specs=[vmem] * len(blocks) + [hbm] * 3 + [pl.BlockSpec(memory_space=pl.ANY)] * len(after),
         out_specs=[vmem] * 4,
         scratch_shapes=[pltpu.SemaphoreType.DMA((3, WEIGHT_CHUNKS))],
         compiler_params=pltpu.CompilerParams(vmem_limit_bytes=VMEM_LIMIT),
-        cost_estimate=expert_cost([rows], weights),
+        cost_estimate=expert_cost(blocks, weights),
         name="stage_weights",
-    )(rows, *(in_hbm(weight) for weight in weights))
-    return rows, weights
+    )(*blocks, *(in_hbm(weight) for weight in weights), *after)
+    return joined, weights
 
 
 def slice_kernel(count, *refs):
@@ -231,15 +236,25 @@
     )
     own = across_groups(flight, rows)
     weights = (w_gate.T, w_up.T, w_down)
-    own, weights = stage_weights(own, weights)
-    groups = [[g * SLICES + m for m in range(SLICES)] for g in range(flight)]
-    groups = None if flight == 1 else groups
-    arrived = lax.all_gather(own, "ep", axis_index_groups=groups, tiled=True)
-    (partial_out,) = expert_slice((arrived,), weights)
-    summed = lax.psum_scatter(
-        partial_out, "ep", scatter_dimension=0, axis_index_groups=groups, tiled=True
-    )
-    parts = [across_groups(flight, summed)]
+    far = swap(devices, 4, own)
+    farther = swap(devices, 6, own)
+    near = swap(devices, 2, own)
+    own_staged, weights = stage_weights((own,), weights, ())
+    inner = jnp.concatenate([own, near])
+    farther_y, far_y = swap(devices, 1, farther), swap(devices, 1, far)
+    inner_y = swap(devices, 1, inner)
+    r_farther_y, r_farther = expert_slice((farther_y, farther), weights, ())
+    r_far_y, r_far = expert_slice((far_y, far), weights, (near,))
+    r_inner_y, r_inner = expert_slice((inner_y, inner), weights, (r_farther_y,))
+    c_inner = swap(devices, 1, r_inner_y)
+    s_own, s_near = (add_level(r_inner[at], c_inner[at]) for at in (slice(slots), slice(slots, None)))
+    w_near = swap(devices, 2, s_near)
+    c_outer = swap(devices, 1, jnp.concatenate([r_far_y, r_farther_y]))
+    s_far, s_farther = add_level(r_far, c_outer[:slots]), add_level(r_farther, c_outer[slots:])
+    w_farther, w_far = swap(devices, 6, s_farther), swap(devices, 4, s_far)
+    parts = [s_own, w_near, add_level(w_far, w_farther)]
+    if flight > 1:
+        parts = [across_groups(flight, functools.reduce(add_level, parts))]
     return combine(table, parts)
 
 

time: 118 us -> 34 us (0.29)
  waiting for transfers between devices: 63.7 us -> 10.3 us
  blocking collectives: 33 us -> 0 us
  starting transfers between devices: 0.01 us -> 15.3 us
  between operations: 14.1 us -> 0.74 us
  Pallas kernels: 6.01 us -> 7.39 us
    reduce_scatter x1 -> x0, waiting for transfers between devices: 63.6 us -> none  [on_device(): lax.psum_scatter(partial_out, 'ep', scatter_dimension=0, axis_index_group...]
    all_gather x1 -> x0, blocking collectives: 33 us -> none  [on_device(): arrived = lax.all_gather(own, 'ep', axis_index_groups=groups, tiled=True)]
    ppermute x0 -> x11, starting transfers between devices: none -> 15.3 us  [swap(): lax.ppermute(block, 'ep', [(i, i ^ distance) for i in range(devices)])]
    ppermute x0 -> x11, waiting for transfers between devices: none -> 10.3 us  [swap(): lax.ppermute(block, 'ep', [(i, i ^ distance) for i in range(devices)])]
    pallas_call x1 -> x3, Pallas kernels: 1.69 us -> 2.45 us  [expert_slice(): pl.pallas_call(functools.partial(slice_kernel, count), out_shape=[jax.Sha...]
  transfers between devices with their start and end apart: 1 -> 11, of which waited for: 1 -> 7; matrix products, arithmetic and copies ran while one was open for 0% -> 0% of each run, Pallas kernels for 0% -> 14%
where the time goes in v8:
time: 34 us; the launch traced here: 33.8 us
  starting transfers between devices  15.3 us (45%)
  waiting for transfers between devices  10.3 us (30%)
  Pallas kernels  7.39 us (22%)
  between operations  0.74 us (2%)
    ppermute x11, starting transfers between devices, swap(): lax.ppermute(block, 'ep', [(i, i ^ distance) for i in range(devices)])  15.3 us
    ppermute x11, waiting for transfers between devices, swap(): lax.ppermute(block, 'ep', [(i, i ^ distance) for i in range(devices)])  10.3 us
    pallas_call x3, Pallas kernels, expert_slice(): pl.pallas_call(functools.partial(slice_kernel, count), out_shape=[jax.Sha...  2.45 us
    pallas_call x1, Pallas kernels, stage_weights(): pl.pallas_call(functools.partial(stage_kernel, len(blocks)), out_shape=[j...  2.43 us
    pallas_call x1, Pallas kernels, pick_rows(): pl.pallas_call(pick_kernel, out_shape=(jax.ShapeDtypeStruct((slots, token...  1.47 us
    pallas_call x1, Pallas kernels, combine(): pl.pallas_call(combine_kernel, out_shape=jax.ShapeDtypeStruct(shape, jnp....  1.04 us
  transfers between devices with their start and end apart: 11, of which 7 were waited for; matrix products, arithmetic and copies ran while one was open for 0% of the time, Pallas kernels for 14%

profile of v8, /device:TPU:0, one launch (start us, length us, event | category | flops | bytes accessed | tf_op | source)
XLA Modules:
  0.0 33.8 jit_solution(10323922434536373192)
XLA Ops:
  0.7 1.5 %pick_rows.1 = (bf16[16,2048]{1,0:T(8,128)(2,1)S(1)}, f32[16,128]{1,0:T(8,128)S(1)}) custom-call(s32[1]{0:T(128)S(6)} %copy.10.live_ref, s32[8,128]{1,0:T(8,128)} %bitcast.8, f32[8,128]{1,0:T(8,128)} %bitcast.9, bf16[128,2048]{1,0:T(8,128)(2,1)} %tokens_hbm.1, f32[1,2048]{1,0:T(1,128)} %bitcast.7), custom_call_target="tpu_custom_call" | custom-call | tf_op jit(solution)/shard_map/pick_rows/pallas_call | solution.py:62
  2.1 4.1 %collective-permute-start.6 = (bf16[16,2048]{1,0:T(8,128)(2,1)S(1)}, bf16[16,2048]{1,0:T(8,128)(2,1)S(1)}, u32[]{:S(2)}, u32[]{:S(2)}) collective-permute-start(bf16[16,2048]{1,0:T(8,128)(2,1)S(1)} %get-tuple-element.17.refs_0_), channel_id=1, source_target_pairs={{0,16},{4,20},{8,24},{12,28},{16,0},{20,4},{24,8},{28,12},{1,17},{... | collective-permute-start | bytes 196616 | tf_op jit(solution)/shard_map/ppermute | solution.py:226
  6.2 1.6 %collective-permute-start = (bf16[16,2048]{1,0:T(8,128)(2,1)S(1)}, bf16[16,2048]{1,0:T(8,128)(2,1)S(1)}, u32[]{:S(2)}, u32[]{:S(2)}) collective-permute-start(bf16[16,2048]{1,0:T(8,128)(2,1)S(1)} %get-tuple-element.17.refs_0_), channel_id=1, source_target_pairs={{0,8},{4,12},{8,0},{12,4},{16,24},{20,28},{24,16},{28,20},{1,9},{5... | collective-permute-start | bytes 196616 | tf_op jit(solution)/shard_map/ppermute | solution.py:226
  7.8 0.0 collective-permute-start.2
  7.8 2.4 %stage_weights.1 = (bf16[16,2048]{1,0:T(8,128)(2,1)}, bf16[192,2048]{1,0:T(8,128)(2,1)S(1)}, bf16[192,2048]{1,0:T(8,128)(2,1)S(1)}, bf16[192,2048]{1,0:T(8,128)(2,1)S(1)}) custom-call(bf16[16,2048]{1,0:T(8,128)(2,1)S(1)} %get-tuple-element.17.refs_0_, bf16[192,2048]{1,0:T(8,128)(2,1)} %bitcast.5, bf16[192,2048]{1,0:T(8,128)(2,1)} %bitcast.6, ...), custom_call_target="tpu_custom_call" | custom-call | flops 37748736 | bytes 2359296 | tf_op jit(solution)/shard_map/stage_weights/pallas_call | solution.py:138
  10.3 0.0 collective-permute-done.6.refs_1_
  10.3 1.8 %collective-permute-start.7 = (bf16[16,2048]{1,0:T(8,128)(2,1)S(1)}, bf16[16,2048]{1,0:T(8,128)(2,1)S(1)}, u32[]{:S(2)}, u32[]{:S(2)}) collective-permute-start(bf16[16,2048]{1,0:T(8,128)(2,1)S(1)} %collective-permute-done.6.refs_1_), channel_id=1, source_target_pairs={{0,4},{4,0},{8,12},{12,8},{16,20},{20,16},{24,28},{28,24},{1,5},{5... | collective-permute-start | bytes 196616 | tf_op jit(solution)/shard_map/ppermute | solution.py:226
  12.1 1.8 %collective-permute-done.2.refs_1_ = bf16[16,2048]{1,0:T(8,128)(2,1)S(1)} collective-permute-done((bf16[16,2048]{1,0:T(8,128)(2,1)S(1)}, bf16[16,2048]{1,0:T(8,128)(2,1)S(1)}, u32[]{:S(2)}, u32[]{:S(2)}) %collective-permute-start.2) | collective-permute-done | bytes 65568 | tf_op jit(solution)/shard_map/ppermute | solution.py:226
  13.9 1.5 %collective-permute-start.3 = (bf16[16,2048]{1,0:T(8,128)(2,1)S(1)}, bf16[16,2048]{1,0:T(8,128)(2,1)S(1)}, u32[]{:S(2)}, u32[]{:S(2)}) collective-permute-start(bf16[16,2048]{1,0:T(8,128)(2,1)S(1)} %collective-permute-done.2.refs_1_), channel_id=1, source_target_pairs={{0,4},{4,0},{8,12},{12,8},{16,20},{20,16},{24,28},{28,24},{1,5},{5... | collective-permute-start | bytes 196616 | tf_op jit(solution)/shard_map/ppermute | solution.py:226
  15.4 0.0 collective-permute-done.refs_5_
  15.4 0.6 %collective-permute-start.1 = (bf16[32,2048]{1,0:T(8,128)(2,1)S(1)}, bf16[32,2048]{1,0:T(8,128)(2,1)S(1)}, u32[]{:S(2)}, u32[]{:S(2)}) collective-permute-start(bf16[32,2048]{1,0:T(8,128)(2,1)S(1)} %constant_dynamic-update-slice_fusion.refs_1_), channel_id=1, source_target_pairs={{0,4},{4,0},{8,12},{12,8},{16,20},{20,16},{24,28},{28,24},{1,5},{5... | collective-permute-start | bytes 393224 | tf_op jit(solution)/shard_map/ppermute | solution.py:226
  16.0 0.0 collective-permute-done.7.refs_0_
  16.0 0.8 %expert_slice.5 = (bf16[16,2048]{1,0:T(8,128)(2,1)S(1)}, bf16[16,2048]{1,0:T(8,128)(2,1)S(1)}) custom-call(bf16[16,2048]{1,0:T(8,128)(2,1)S(1)} %collective-permute-done.7.refs_0_, bf16[16,2048]{1,0:T(8,128)(2,1)S(1)} %collective-permute-done.6.refs_1_, bf16[192,2048]{1,0:T(8,128)(2,1)S(1)} %get-tuple-element.18.refs_2_, ...), custom_call_target="tpu_custom_call" | custom-call | flops 75497472 | bytes 2359296 | tf_op jit(solution)/shard_map/expert_slice/pallas_call | solution.py:159
  16.8 1.4 %collective-permute-done.3.refs_0_ = bf16[16,2048]{1,0:T(8,128)(2,1)S(1)} collective-permute-done((bf16[16,2048]{1,0:T(8,128)(2,1)S(1)}, bf16[16,2048]{1,0:T(8,128)(2,1)S(1)}, u32[]{:S(2)}, u32[]{:S(2)}) %collective-permute-start.3) | collective-permute-done | bytes 65568 | tf_op jit(solution)/shard_map/ppermute | solution.py:226
  18.1 0.8 %expert_slice.3 = (bf16[16,2048]{1,0:T(8,128)(2,1)S(1)}, bf16[16,2048]{1,0:T(8,128)(2,1)S(1)}) custom-call(bf16[16,2048]{1,0:T(8,128)(2,1)S(1)} %collective-permute-done.3.refs_0_, bf16[16,2048]{1,0:T(8,128)(2,1)S(1)} %collective-permute-done.2.refs_1_, bf16[192,2048]{1,0:T(8,128)(2,1)S(1)} %get-tuple-element.18.refs_2_, ...), custom_call_target="tpu_custom_call" | custom-call | flops 75497472 | bytes 2359296 | tf_op jit(solution)/shard_map/expert_slice/pallas_call | solution.py:159
  19.0 1.6 %collective-permute-start.8 = (bf16[32,2048]{1,0:T(8,128)(2,1)S(1)}, bf16[32,2048]{1,0:T(8,128)(2,1)S(1)}, u32[]{:S(2)}, u32[]{:S(2)}) collective-permute-start(bf16[32,2048]{1,0:T(8,128)(2,1)S(1)} %pad_maximum_fusion), channel_id=1, source_target_pairs={{0,4},{4,0},{8,12},{12,8},{16,20},{20,16},{24,28},{28,24},{1,5},{5... | collective-permute-start | bytes 393224 | tf_op jit(solution)/shard_map/ppermute | solution.py:226
  20.6 1.3 %collective-permute-done.1.refs_0_ = bf16[32,2048]{1,0:T(8,128)(2,1)S(1)} collective-permute-done((bf16[32,2048]{1,0:T(8,128)(2,1)S(1)}, bf16[32,2048]{1,0:T(8,128)(2,1)S(1)}, u32[]{:S(2)}, u32[]{:S(2)}) %collective-permute-start.1) | collective-permute-done | bytes 131104 | tf_op jit(solution)/shard_map/ppermute | solution.py:226
  21.8 0.8 %expert_slice.4 = (bf16[32,2048]{1,0:T(8,128)(2,1)S(1)}, bf16[32,2048]{1,0:T(8,128)(2,1)S(1)}) custom-call(bf16[32,2048]{1,0:T(8,128)(2,1)S(1)} %collective-permute-done.1.refs_0_, bf16[32,2048]{1,0:T(8,128)(2,1)S(1)} %constant_dynamic-update-slice_fusion.refs_1_, bf16[192,2048]{1,0:T(8,128)(2,1)S(1)} %get-tuple-element.18.refs_2_, ...), custom_call_target="tpu_custom_call" | custom-call | flops 150994944 | bytes 2359296 | tf_op jit(solution)/shard_map/expert_slice/pallas_call | solution.py:159
  22.7 0.1 collective-permute-start.4
  22.8 1.6 %collective-permute-done.8 = bf16[32,2048]{1,0:T(8,128)(2,1)S(1)} collective-permute-done((bf16[32,2048]{1,0:T(8,128)(2,1)S(1)}, bf16[32,2048]{1,0:T(8,128)(2,1)S(1)}, u32[]{:S(2)}, u32[]{:S(2)}) %collective-permute-start.8) | collective-permute-done | bytes 131104 | tf_op jit(solution)/shard_map/ppermute | solution.py:226
  24.4 2.5 %collective-permute-start.10 = (bf16[16,2048]{1,0:T(8,128)(2,1)S(1)}, bf16[16,2048]{1,0:T(8,128)(2,1)S(1)}, u32[]{:S(2)}, u32[]{:S(2)}) collective-permute-start(bf16[16,2048]{1,0:T(8,128)(2,1)S(1)} %get-tuple-element.30), channel_id=1, source_target_pairs={{0,24},{4,28},{8,16},{12,20},{16,8},{20,12},{24,0},{28,4},{1,25},{... | collective-permute-start | bytes 196616 | tf_op jit(solution)/shard_map/ppermute | solution.py:226
  26.9 0.4 %collective-permute-start.9 = (bf16[16,2048]{1,0:T(8,128)(2,1)S(1)}, bf16[16,2048]{1,0:T(8,128)(2,1)S(1)}, u32[]{:S(2)}, u32[]{:S(2)}) collective-permute-start(bf16[16,2048]{1,0:T(8,128)(2,1)S(1)} %get-tuple-element.29), channel_id=1, source_target_pairs={{0,16},{4,20},{8,24},{12,28},{16,0},{20,4},{24,8},{28,12},{1,17},{... | collective-permute-start | bytes 196616 | tf_op jit(solution)/shard_map/ppermute | solution.py:226
  27.3 0.5 %collective-permute-done.4 = bf16[32,2048]{1,0:T(8,128)(2,1)S(1)} collective-permute-done((bf16[32,2048]{1,0:T(8,128)(2,1)S(1)}, bf16[32,2048]{1,0:T(8,128)(2,1)S(1)}, u32[]{:S(2)}, u32[]{:S(2)}) %collective-permute-start.4) | collective-permute-done | bytes 131104 | tf_op jit(solution)/shard_map/ppermute | solution.py:226
  27.8 1.2 %collective-permute-start.5 = (bf16[16,2048]{1,0:T(8,128)(2,1)S(1)}, bf16[16,2048]{1,0:T(8,128)(2,1)S(1)}, u32[]{:S(2)}, u32[]{:S(2)}) collective-permute-start(bf16[16,2048]{1,0:T(8,128)(2,1)S(1)} %get-tuple-element.27), channel_id=1, source_target_pairs={{0,8},{4,12},{8,0},{12,4},{16,24},{20,28},{24,16},{28,20},{1,9},{5... | collective-permute-start | bytes 196616 | tf_op jit(solution)/shard_map/ppermute | solution.py:226
  28.9 1.8 %collective-permute-done.10 = bf16[16,2048]{1,0:T(8,128)(2,1)S(1)} collective-permute-done((bf16[16,2048]{1,0:T(8,128)(2,1)S(1)}, bf16[16,2048]{1,0:T(8,128)(2,1)S(1)}, u32[]{:S(2)}, u32[]{:S(2)}) %collective-permute-start.10) | collective-permute-done | bytes 65568 | tf_op jit(solution)/shard_map/ppermute | solution.py:226
  30.8 2.0 %collective-permute-done.9 = bf16[16,2048]{1,0:T(8,128)(2,1)S(1)} collective-permute-done((bf16[16,2048]{1,0:T(8,128)(2,1)S(1)}, bf16[16,2048]{1,0:T(8,128)(2,1)S(1)}, u32[]{:S(2)}, u32[]{:S(2)}) %collective-permute-start.9) | collective-permute-done | bytes 65568 | tf_op jit(solution)/shard_map/ppermute | solution.py:226
  32.8 0.0 collective-permute-done.5.refs_1_
  32.8 1.0 %combine.1 = bf16[128,2048]{1,0:T(8,128)(2,1)} custom-call(f32[16,128]{1,0:T(8,128)S(1)} %get-tuple-element.16.table_ref, bf16[16,2048]{1,0:T(8,128)(2,1)S(1)} %get-tuple-element.28.refs_0_, bf16[16,2048]{1,0:T(8,128)(2,1)S(1)} %collective-permute-done.5.refs_1_, bf16[16,2048]{1,0:T(8,128)(2,1)S(1)} %add_convert_fusion.refs_2_), custom_call_target="tpu_custom_call" | custom-call | tf_op jit(solution)/shard_map/combine/pallas_call | solution.py:205
  (6 shorter events, 0.1 us)
Async XLA Ops:
  2.1 8.1 %collective-permute-start.6 = (bf16[16,2048]{1,0:T(8,128)(2,1)S(1)}, bf16[16,2048]{1,0:T(8,128)(2,1)S(1)}, u32[]{:S(2)}, u32[]{:S(2)}) collective-permute-start(bf16[16,2048]{1,0:T(8,128)(2,1)S(1)} %get-tuple-element.17.refs_0_), channel_id=1, source_target_pairs={{0,16},{4,20},{8,24},{12,28},{16,0},{20,4},{24,8},{28,12},{1,17},{... | collective-permute-start | bytes 196616 | tf_op jit(solution)/shard_map/ppermute | solution.py:226
  6.2 9.2 %collective-permute-start = (bf16[16,2048]{1,0:T(8,128)(2,1)S(1)}, bf16[16,2048]{1,0:T(8,128)(2,1)S(1)}, u32[]{:S(2)}, u32[]{:S(2)}) collective-permute-start(bf16[16,2048]{1,0:T(8,128)(2,1)S(1)} %get-tuple-element.17.refs_0_), channel_id=1, source_target_pairs={{0,8},{4,12},{8,0},{12,4},{16,24},{20,28},{24,16},{28,20},{1,9},{5... | collective-permute-start | bytes 196616 | tf_op jit(solution)/shard_map/ppermute | solution.py:226
  7.8 6.1 %collective-permute-start.2 = (bf16[16,2048]{1,0:T(8,128)(2,1)S(1)}, bf16[16,2048]{1,0:T(8,128)(2,1)S(1)}, u32[]{:S(2)}, u32[]{:S(2)}) collective-permute-start(bf16[16,2048]{1,0:T(8,128)(2,1)S(1)} %get-tuple-element.17.refs_0_), channel_id=1, source_target_pairs={{0,24},{4,28},{8,16},{12,20},{16,8},{20,12},{24,0},{28,4},{1,25},{... | collective-permute-start | bytes 196616 | tf_op jit(solution)/shard_map/ppermute | solution.py:226
  10.3 5.7 %collective-permute-start.7 = (bf16[16,2048]{1,0:T(8,128)(2,1)S(1)}, bf16[16,2048]{1,0:T(8,128)(2,1)S(1)}, u32[]{:S(2)}, u32[]{:S(2)}) collective-permute-start(bf16[16,2048]{1,0:T(8,128)(2,1)S(1)} %collective-permute-done.6.refs_1_), channel_id=1, source_target_pairs={{0,4},{4,0},{8,12},{12,8},{16,20},{20,16},{24,28},{28,24},{1,5},{5... | collective-permute-start | bytes 196616 | tf_op jit(solution)/shard_map/ppermute | solution.py:226
  13.9 4.3 %collective-permute-start.3 = (bf16[16,2048]{1,0:T(8,128)(2,1)S(1)}, bf16[16,2048]{1,0:T(8,128)(2,1)S(1)}, u32[]{:S(2)}, u32[]{:S(2)}) collective-permute-start(bf16[16,2048]{1,0:T(8,128)(2,1)S(1)} %collective-permute-done.2.refs_1_), channel_id=1, source_target_pairs={{0,4},{4,0},{8,12},{12,8},{16,20},{20,16},{24,28},{28,24},{1,5},{5... | collective-permute-start | bytes 196616 | tf_op jit(solution)/shard_map/ppermute | solution.py:226
  15.4 6.4 %collective-permute-start.1 = (bf16[32,2048]{1,0:T(8,128)(2,1)S(1)}, bf16[32,2048]{1,0:T(8,128)(2,1)S(1)}, u32[]{:S(2)}, u32[]{:S(2)}) collective-permute-start(bf16[32,2048]{1,0:T(8,128)(2,1)S(1)} %constant_dynamic-update-slice_fusion.refs_1_), channel_id=1, source_target_pairs={{0,4},{4,0},{8,12},{12,8},{16,20},{20,16},{24,28},{28,24},{1,5},{5... | collective-permute-start | bytes 393224 | tf_op jit(solution)/shard_map/ppermute | solution.py:226
  19.0 5.4 %collective-permute-start.8 = (bf16[32,2048]{1,0:T(8,128)(2,1)S(1)}, bf16[32,2048]{1,0:T(8,128)(2,1)S(1)}, u32[]{:S(2)}, u32[]{:S(2)}) collective-permute-start(bf16[32,2048]{1,0:T(8,128)(2,1)S(1)} %pad_maximum_fusion), channel_id=1, source_target_pairs={{0,4},{4,0},{8,12},{12,8},{16,20},{20,16},{24,28},{28,24},{1,5},{5... | collective-permute-start | bytes 393224 | tf_op jit(solution)/shard_map/ppermute | solution.py:226
  22.7 5.0 %collective-permute-start.4 = (bf16[32,2048]{1,0:T(8,128)(2,1)S(1)}, bf16[32,2048]{1,0:T(8,128)(2,1)S(1)}, u32[]{:S(2)}, u32[]{:S(2)}) collective-permute-start(bf16[32,2048]{1,0:T(8,128)(2,1)S(1)} %get-tuple-element.23), channel_id=1, source_target_pairs={{0,4},{4,0},{8,12},{12,8},{16,20},{20,16},{24,28},{28,24},{1,5},{5... | collective-permute-start | bytes 393224 | tf_op jit(solution)/shard_map/ppermute | solution.py:226
  24.4 6.4 %collective-permute-start.10 = (bf16[16,2048]{1,0:T(8,128)(2,1)S(1)}, bf16[16,2048]{1,0:T(8,128)(2,1)S(1)}, u32[]{:S(2)}, u32[]{:S(2)}) collective-permute-start(bf16[16,2048]{1,0:T(8,128)(2,1)S(1)} %get-tuple-element.30), channel_id=1, source_target_pairs={{0,24},{4,28},{8,16},{12,20},{16,8},{20,12},{24,0},{28,4},{1,25},{... | collective-permute-start | bytes 196616 | tf_op jit(solution)/shard_map/ppermute | solution.py:226
  26.9 5.9 %collective-permute-start.9 = (bf16[16,2048]{1,0:T(8,128)(2,1)S(1)}, bf16[16,2048]{1,0:T(8,128)(2,1)S(1)}, u32[]{:S(2)}, u32[]{:S(2)}) collective-permute-start(bf16[16,2048]{1,0:T(8,128)(2,1)S(1)} %get-tuple-element.29), channel_id=1, source_target_pairs={{0,16},{4,20},{8,24},{12,28},{16,0},{20,4},{24,8},{28,12},{1,17},{... | collective-permute-start | bytes 196616 | tf_op jit(solution)/shard_map/ppermute | solution.py:226
  27.8 5.0 %collective-permute-start.5 = (bf16[16,2048]{1,0:T(8,128)(2,1)S(1)}, bf16[16,2048]{1,0:T(8,128)(2,1)S(1)}, u32[]{:S(2)}, u32[]{:S(2)}) collective-permute-start(bf16[16,2048]{1,0:T(8,128)(2,1)S(1)} %get-tuple-element.27), channel_id=1, source_target_pairs={{0,8},{4,12},{8,0},{12,4},{16,24},{20,28},{24,16},{28,20},{1,9},{5... | collective-permute-start | bytes 196616 | tf_op jit(solution)/shard_map/ppermute | solution.py:226

commit v9 on v6

--- a/solution.py
+++ b/solution.py
@@ -12,6 +12,7 @@
 VMEM_LIMIT = 40 * 1024 * 1024
 WEIGHT_CHUNKS = 4
 TOKEN_CHUNKS = 4
+OUT_CHUNKS = 8
 
 
 def in_hbm(array):
@@ -89,14 +90,17 @@
 
 
 def expert_blocks(ins, weights, outs):
-    together = max(1, 128 // ins[0].shape[0])
-    for first in range(0, len(ins), together):
-        some = ins[first : first + together]
-        partial_out = expert_rows(jnp.concatenate([ref[...] for ref in some], axis=0), *weights)
-        at = 0
-        for ref in outs[first : first + together]:
-            ref[...] = partial_out[at : at + ref.shape[0]]
-            at += ref.shape[0]
+    size = ins[0].shape[0]
+    together = max(1, 128 // size)
+    targets = [(ref, at) for ref in outs for at in range(0, ref.shape[0], size)]
+    first = 0
+    while first < len(ins):
+        some = [ref for ref in ins[first : first + together]]
+        rows = jnp.concatenate([ref[...] for ref in some], axis=0)
+        partial_out = expert_rows(rows, *weights)
+        for i, (ref, at) in enumerate(targets[first : first + len(some)]):
+            ref[at : at + size] = partial_out[i * size : (i + 1) * size]
+        first += together
 
 
 def expert_cost(blocks, weights):
@@ -112,50 +116,49 @@
         yield pltpu.make_async_copy(source.at[at], target.at[at], sems.at[i])
 
 
-def stage_kernel(rows_ref, *refs):
+def stage_kernel(*refs):
     *refs, sems = refs
-    sources, out_ref, weights = refs[:3], refs[3], refs[4:]
     copies = [
         copy
-        for i, pair in enumerate(zip(sources, weights))
+        for i, pair in enumerate(zip(refs[:3], refs[-3:]))
         for copy in chunk_copies(*pair, WEIGHT_CHUNKS, sems.at[i])
     ]
     for copy in copies:
         copy.start()
-    out_ref[...] = rows_ref[...]
     for copy in copies:
         copy.wait()
 
 
-def stage_weights(rows, weights):
+def stage_weights(weights, after):
     vmem = pl.BlockSpec(memory_space=pltpu.VMEM)
     hbm = pl.BlockSpec(memory_space=pltpu.HBM)
-    rows, *weights = pl.pallas_call(
+    return pl.pallas_call(
         stage_kernel,
-        out_shape=[jax.ShapeDtypeStruct(array.shape, array.dtype) for array in (rows, *weights)],
-        in_specs=[vmem] + [hbm] * 3,
-        out_specs=[vmem] * 4,
+        out_shape=[jax.ShapeDtypeStruct(array.shape, array.dtype) for array in weights],
+        in_specs=[hbm] * 3 + [pl.BlockSpec(memory_space=pl.ANY)] * len(after),
+        out_specs=[vmem] * 3,
         scratch_shapes=[pltpu.SemaphoreType.DMA((3, WEIGHT_CHUNKS))],
         compiler_params=pltpu.CompilerParams(vmem_limit_bytes=VMEM_LIMIT),
-        cost_estimate=expert_cost([rows], weights),
+        cost_estimate=expert_cost(after, weights),
         name="stage_weights",
-    )(rows, *(in_hbm(weight) for weight in weights))
-    return rows, weights
-
-
-def slice_kernel(count, *refs):
-    outs = refs[len(refs) - count :]
-    expert_blocks(refs[:count], refs[count : count + 3], outs)
-
-
-def expert_slice(blocks, weights, after=()):
-    vmem = pl.BlockSpec(memory_space=pltpu.VMEM)
-    count = len(blocks)
-    return pl.pallas_call(
-        functools.partial(slice_kernel, count),
-        out_shape=[jax.ShapeDtypeStruct(block.shape, jnp.bfloat16) for block in blocks],
-        in_specs=[vmem] * (count + 3) + [pl.BlockSpec(memory_space=pl.ANY)] * len(after),
-        out_specs=[vmem] * count,
+    )(*(in_hbm(weight) for weight in weights), *after)
+
+
+def slice_kernel(count, made, *refs):
+    expert_blocks(refs[:count], refs[count : count + 3], refs[len(refs) - made :])
+
+
+def expert_slice(groups, weights, after=()):
+    vmem = pl.BlockSpec(memory_space=pltpu.VMEM)
+    blocks = [block for group in groups for block in group]
+    rows, features = blocks[0].shape
+    return pl.pallas_call(
+        functools.partial(slice_kernel, len(blocks), len(groups)),
+        out_shape=[
+            jax.ShapeDtypeStruct((rows * len(group), features), jnp.bfloat16) for group in groups
+        ],
+        in_specs=[vmem] * (len(blocks) + 3) + [pl.BlockSpec(memory_space=pl.ANY)] * len(after),
+        out_specs=[vmem] * len(groups),
         compiler_params=pltpu.CompilerParams(vmem_limit_bytes=VMEM_LIMIT),
         cost_estimate=expert_cost(blocks, weights),
         name="expert_slice",
@@ -175,9 +178,9 @@
         table = table - pieces[-1].astype(jnp.float32)
     pieces = jnp.concatenate(pieces, axis=0)
     features = out_ref.shape[1]
-    width = features // 4
+    width = features // OUT_CHUNKS
     copies = []
-    for i in range(4):
+    for i in range(OUT_CHUNKS):
         columns = pl.ds(i * width, width)
         summed = functools.reduce(add_level, [part[:, columns] for part in parts])
         out_ref[:, columns] = lax.dot_general(
@@ -202,7 +205,7 @@
         out_shape=jax.ShapeDtypeStruct(shape, jnp.bfloat16),
         in_specs=[vmem] * (1 + len(parts)),
         out_specs=pl.BlockSpec(memory_space=pltpu.HBM),
-        scratch_shapes=[pltpu.VMEM(shape, jnp.bfloat16), pltpu.SemaphoreType.DMA((4,))],
+        scratch_shapes=[pltpu.VMEM(shape, jnp.bfloat16), pltpu.SemaphoreType.DMA((OUT_CHUNKS,))],
         compiler_params=pltpu.CompilerParams(vmem_limit_bytes=VMEM_LIMIT),
         name="combine",
     )(table, *parts)
@@ -230,16 +233,19 @@
         slots, live_counts, expert_ids.T, gate_vals.T, tokens, norm_gain.reshape(1, features)
     )
     own = across_groups(flight, rows)
-    farther, far = swap(devices, 6, own), swap(devices, 4, own)
-    own, weights = stage_weights(own, (w_gate.T, w_up.T, w_down))
+    far = swap(devices, 4, own)
     near = swap(devices, 2, own)
-    outer, inner = jnp.concatenate([far, farther]), jnp.concatenate([own, near])
-    outer_y, inner_y = swap(devices, 1, outer), swap(devices, 1, inner)
-    (outer_y,) = expert_slice((outer_y,), weights)
-    outer, inner, inner_y = expert_slice((outer, inner, inner_y), weights, (outer_y,))
-    outer_y, inner_y = swap(devices, 1, outer_y), swap(devices, 1, inner_y)
-    far, farther = (add_level(outer[at], outer_y[at]) for at in (slice(slots), slice(slots, None)))
-    own, near = (add_level(inner[at], inner_y[at]) for at in (slice(slots), slice(slots, None)))
+    farther = swap(devices, 6, own)
+    weights = stage_weights((w_gate.T, w_up.T, w_down), (own,))
+    inner = jnp.concatenate([own, near])
+    farther_y, far_y = swap(devices, 1, farther), swap(devices, 1, far)
+    inner_y = swap(devices, 1, inner)
+    outer_y, far, farther = expert_slice(((far_y, farther_y), (far,), (farther,)), weights)
+    inner_y, inner = expert_slice(((inner_y,), (inner,)), weights, (outer_y,))
+    halves = (slice(slots), slice(slots, None))
+    outer_c, inner_c = swap(devices, 1, outer_y), swap(devices, 1, inner_y)
+    far, farther = (add_level(kept, outer_c[at]) for kept, at in zip((far, farther), halves))
+    own, near = (add_level(inner[at], inner_c[at]) for at in halves)
     farther, far = swap(devices, 6, farther), swap(devices, 4, far)
     parts = [own, swap(devices, 2, near), add_level(far, farther)]
     if flight > 1:

time: 34 us -> 34.7 us (1.021)
  starting transfers between devices: 14.5 us -> 18 us
  waiting for transfers between devices: 12.5 us -> 9.64 us
    ppermute x10 -> x11, starting transfers between devices: 14.5 us -> 18 us  [swap(): lax.ppermute(block, 'ep', [(i, i ^ distance) for i in range(devices)])]
    ppermute x10 -> x11, waiting for transfers between devices: 12.5 us -> 9.64 us  [swap(): lax.ppermute(block, 'ep', [(i, i ^ distance) for i in range(devices)])]
  transfers between devices with their start and end apart: 10 -> 11, of which waited for: 7 -> 7; matrix products, arithmetic and copies ran while one was open for 0% -> 0% of each run, Pallas kernels for 10% -> 10%
where the time goes in v9:
time: 34.7 us; the launch traced here: 34.5 us
  starting transfers between devices  18 us (52%)
  waiting for transfers between devices  9.64 us (28%)
  Pallas kernels  6.04 us (17%)
  between operations  0.72 us (2%)
    ppermute x11, starting transfers between devices, swap(): lax.ppermute(block, 'ep', [(i, i ^ distance) for i in range(devices)])  18 us
    ppermute x11, waiting for transfers between devices, swap(): lax.ppermute(block, 'ep', [(i, i ^ distance) for i in range(devices)])  9.64 us
    pallas_call x1, Pallas kernels, stage_weights(): pl.pallas_call(stage_kernel, out_shape=[jax.ShapeDtypeStruct(array.shape,...  1.8 us
    pallas_call x2, Pallas kernels, expert_slice(): pl.pallas_call(functools.partial(slice_kernel, len(blocks), len(groups)),...  1.69 us
    pallas_call x1, Pallas kernels, pick_rows(): pl.pallas_call(pick_kernel, out_shape=(jax.ShapeDtypeStruct((slots, token...  1.47 us
    pallas_call x1, Pallas kernels, combine(): pl.pallas_call(combine_kernel, out_shape=jax.ShapeDtypeStruct(shape, jnp....  1.08 us
  transfers between devices with their start and end apart: 11, of which 7 were waited for; matrix products, arithmetic and copies ran while one was open for 0% of the time, Pallas kernels for 10%

profile of v9, /device:TPU:0, one launch (start us, length us, event | category | flops | bytes accessed | tf_op | source)
XLA Modules:
  0.0 34.5 jit_solution(14825682959608529009)
XLA Ops:
  0.7 1.5 %pick_rows.1 = (bf16[16,2048]{1,0:T(8,128)(2,1)S(1)}, f32[16,128]{1,0:T(8,128)S(1)}) custom-call(s32[1]{0:T(128)S(6)} %copy.10.live_ref, s32[8,128]{1,0:T(8,128)} %bitcast.8, f32[8,128]{1,0:T(8,128)} %bitcast.9, bf16[128,2048]{1,0:T(8,128)(2,1)} %tokens_hbm.1, f32[1,2048]{1,0:T(1,128)} %bitcast.7), custom_call_target="tpu_custom_call" | custom-call | tf_op jit(solution)/shard_map/pick_rows/pallas_call | solution.py:63
  2.1 4.1 %collective-permute-start.2 = (bf16[16,2048]{1,0:T(8,128)(2,1)S(1)}, bf16[16,2048]{1,0:T(8,128)(2,1)S(1)}, u32[]{:S(2)}, u32[]{:S(2)}) collective-permute-start(bf16[16,2048]{1,0:T(8,128)(2,1)S(1)} %get-tuple-element.16.refs_3_), channel_id=1, source_target_pairs={{0,16},{4,20},{8,24},{12,28},{16,0},{20,4},{24,8},{28,12},{1,17},{... | collective-permute-start | bytes 196616 | tf_op jit(solution)/shard_map/ppermute | solution.py:224
  6.2 1.3 %collective-permute-start.4 = (bf16[16,2048]{1,0:T(8,128)(2,1)S(1)}, bf16[16,2048]{1,0:T(8,128)(2,1)S(1)}, u32[]{:S(2)}, u32[]{:S(2)}) collective-permute-start(bf16[16,2048]{1,0:T(8,128)(2,1)S(1)} %get-tuple-element.16.refs_3_), channel_id=1, source_target_pairs={{0,24},{4,28},{8,16},{12,20},{16,8},{20,12},{24,0},{28,4},{1,25},{... | collective-permute-start | bytes 196616 | tf_op jit(solution)/shard_map/ppermute | solution.py:224
  7.6 0.2 collective-permute-start
  7.8 1.8 %stage_weights.1 = (bf16[192,2048]{1,0:T(8,128)(2,1)S(1)}, bf16[192,2048]{1,0:T(8,128)(2,1)S(1)}, bf16[192,2048]{1,0:T(8,128)(2,1)S(1)}) custom-call(bf16[192,2048]{1,0:T(8,128)(2,1)} %bitcast.5, bf16[192,2048]{1,0:T(8,128)(2,1)} %bitcast.6, bf16[192,2048]{1,0:T(8,128)(2,1)} %refs_2_.1, bf16[16,2048]{1,0:T(8,128)(2,1)S(1)} %get-tuple-element.16.refs_3_), custom_call_target="tpu_custom_call" | custom-call | flops 37748736 | bytes 2359296 | tf_op jit(solution)/shard_map/stage_weights/pallas_call | solution.py:135
  9.6 0.4 %collective-permute-done.2.refs_2_ = bf16[16,2048]{1,0:T(8,128)(2,1)S(1)} collective-permute-done((bf16[16,2048]{1,0:T(8,128)(2,1)S(1)}, bf16[16,2048]{1,0:T(8,128)(2,1)S(1)}, u32[]{:S(2)}, u32[]{:S(2)}) %collective-permute-start.2) | collective-permute-done | bytes 65568 | tf_op jit(solution)/shard_map/ppermute | solution.py:224
  10.0 2.6 %collective-permute-start.3 = (bf16[16,2048]{1,0:T(8,128)(2,1)S(1)}, bf16[16,2048]{1,0:T(8,128)(2,1)S(1)}, u32[]{:S(2)}, u32[]{:S(2)}) collective-permute-start(bf16[16,2048]{1,0:T(8,128)(2,1)S(1)} %collective-permute-done.2.refs_2_), channel_id=1, source_target_pairs={{0,4},{4,0},{8,12},{12,8},{16,20},{20,16},{24,28},{28,24},{1,5},{5... | collective-permute-start | bytes 196616 | tf_op jit(solution)/shard_map/ppermute | solution.py:224
  12.5 0.0 collective-permute-done.4.refs_3_
  12.5 1.4 %collective-permute-start.5 = (bf16[16,2048]{1,0:T(8,128)(2,1)S(1)}, bf16[16,2048]{1,0:T(8,128)(2,1)S(1)}, u32[]{:S(2)}, u32[]{:S(2)}) collective-permute-start(bf16[16,2048]{1,0:T(8,128)(2,1)S(1)} %collective-permute-done.4.refs_3_), channel_id=1, source_target_pairs={{0,4},{4,0},{8,12},{12,8},{16,20},{20,16},{24,28},{28,24},{1,5},{5... | collective-permute-start | bytes 196616 | tf_op jit(solution)/shard_map/ppermute | solution.py:224
  14.0 0.0 collective-permute-done
  14.0 0.7 %collective-permute-start.1 = (bf16[32,2048]{1,0:T(8,128)(2,1)S(1)}, bf16[32,2048]{1,0:T(8,128)(2,1)S(1)}, u32[]{:S(2)}, u32[]{:S(2)}) collective-permute-start(bf16[32,2048]{1,0:T(8,128)(2,1)S(1)} %constant_dynamic-update-slice_fusion.refs_1_), channel_id=1, source_target_pairs={{0,4},{4,0},{8,12},{12,8},{16,20},{20,16},{24,28},{28,24},{1,5},{5... | collective-permute-start | bytes 393224 | tf_op jit(solution)/shard_map/ppermute | solution.py:224
  14.7 0.4 %collective-permute-done.3.refs_0_ = bf16[16,2048]{1,0:T(8,128)(2,1)S(1)} collective-permute-done((bf16[16,2048]{1,0:T(8,128)(2,1)S(1)}, bf16[16,2048]{1,0:T(8,128)(2,1)S(1)}, u32[]{:S(2)}, u32[]{:S(2)}) %collective-permute-start.3) | collective-permute-done | bytes 65568 | tf_op jit(solution)/shard_map/ppermute | solution.py:224
  15.1 1.8 %collective-permute-done.5.refs_1_ = bf16[16,2048]{1,0:T(8,128)(2,1)S(1)} collective-permute-done((bf16[16,2048]{1,0:T(8,128)(2,1)S(1)}, bf16[16,2048]{1,0:T(8,128)(2,1)S(1)}, u32[]{:S(2)}, u32[]{:S(2)}) %collective-permute-start.5) | collective-permute-done | bytes 65568 | tf_op jit(solution)/shard_map/ppermute | solution.py:224
  16.9 0.8 %expert_slice.2 = (bf16[32,2048]{1,0:T(8,128)(2,1)S(1)}, bf16[16,2048]{1,0:T(8,128)(2,1)S(1)}, bf16[16,2048]{1,0:T(8,128)(2,1)S(1)}) custom-call(bf16[16,2048]{1,0:T(8,128)(2,1)S(1)} %collective-permute-done.3.refs_0_, bf16[16,2048]{1,0:T(8,128)(2,1)S(1)} %collective-permute-done.5.refs_1_, bf16[16,2048]{1,0:T(8,128)(2,1)S(1)} %collective-permute-done.2.refs_2_, ...), custom_call_target="tpu_custom_call" | custom-call | flops 150994944 | bytes 2359296 | tf_op jit(solution)/shard_map/expert_slice/pallas_call | solution.py:155
  17.7 1.6 %collective-permute-start.8 = (bf16[32,2048]{1,0:T(8,128)(2,1)S(1)}, bf16[32,2048]{1,0:T(8,128)(2,1)S(1)}, u32[]{:S(2)}, u32[]{:S(2)}) collective-permute-start(bf16[32,2048]{1,0:T(8,128)(2,1)S(1)} %get-tuple-element.20.refs_5_), channel_id=1, source_target_pairs={{0,4},{4,0},{8,12},{12,8},{16,20},{20,16},{24,28},{28,24},{1,5},{5... | collective-permute-start | bytes 393224 | tf_op jit(solution)/shard_map/ppermute | solution.py:224
  19.3 1.1 %collective-permute-done.1.refs_0_ = bf16[32,2048]{1,0:T(8,128)(2,1)S(1)} collective-permute-done((bf16[32,2048]{1,0:T(8,128)(2,1)S(1)}, bf16[32,2048]{1,0:T(8,128)(2,1)S(1)}, u32[]{:S(2)}, u32[]{:S(2)}) %collective-permute-start.1) | collective-permute-done | bytes 131104 | tf_op jit(solution)/shard_map/ppermute | solution.py:224
  20.4 0.8 %expert_slice.3 = (bf16[32,2048]{1,0:T(8,128)(2,1)S(1)}, bf16[32,2048]{1,0:T(8,128)(2,1)S(1)}) custom-call(bf16[32,2048]{1,0:T(8,128)(2,1)S(1)} %collective-permute-done.1.refs_0_, bf16[32,2048]{1,0:T(8,128)(2,1)S(1)} %constant_dynamic-update-slice_fusion.refs_1_, bf16[192,2048]{1,0:T(8,128)(2,1)S(1)} %get-tuple-element.17.refs_4_.refs_2_, ...), custom_call_target="tpu_custom_call" | custom-call | flops 150994944 | bytes 2359296 | tf_op jit(solution)/shard_map/expert_slice/pallas_call | solution.py:155
  21.3 0.2 collective-permute-start.6
  21.5 1.5 %collective-permute-done.8 = bf16[32,2048]{1,0:T(8,128)(2,1)S(1)} collective-permute-done((bf16[32,2048]{1,0:T(8,128)(2,1)S(1)}, bf16[32,2048]{1,0:T(8,128)(2,1)S(1)}, u32[]{:S(2)}, u32[]{:S(2)}) %collective-permute-start.8) | collective-permute-done | bytes 131104 | tf_op jit(solution)/shard_map/ppermute | solution.py:224
  23.0 5.2 %collective-permute-start.10 = (bf16[16,2048]{1,0:T(8,128)(2,1)S(1)}, bf16[16,2048]{1,0:T(8,128)(2,1)S(1)}, u32[]{:S(2)}, u32[]{:S(2)}) collective-permute-start(bf16[16,2048]{1,0:T(8,128)(2,1)S(1)} %get-tuple-element.28), channel_id=1, source_target_pairs={{0,24},{4,28},{8,16},{12,20},{16,8},{20,12},{24,0},{28,4},{1,25},{... | collective-permute-start | bytes 196616 | tf_op jit(solution)/shard_map/ppermute | solution.py:224
  28.2 0.0 collective-permute-start.9
  28.2 0.0 collective-permute-done.6
  28.3 0.7 %collective-permute-start.7 = (bf16[16,2048]{1,0:T(8,128)(2,1)S(1)}, bf16[16,2048]{1,0:T(8,128)(2,1)S(1)}, u32[]{:S(2)}, u32[]{:S(2)}) collective-permute-start(bf16[16,2048]{1,0:T(8,128)(2,1)S(1)} %get-tuple-element.25), channel_id=1, source_target_pairs={{0,8},{4,12},{8,0},{12,4},{16,24},{20,28},{24,16},{28,20},{1,9},{5... | collective-permute-start | bytes 196616 | tf_op jit(solution)/shard_map/ppermute | solution.py:224
  29.0 1.8 %collective-permute-done.10 = bf16[16,2048]{1,0:T(8,128)(2,1)S(1)} collective-permute-done((bf16[16,2048]{1,0:T(8,128)(2,1)S(1)}, bf16[16,2048]{1,0:T(8,128)(2,1)S(1)}, u32[]{:S(2)}, u32[]{:S(2)}) %collective-permute-start.10) | collective-permute-done | bytes 65568 | tf_op jit(solution)/shard_map/ppermute | solution.py:224
  30.8 2.6 %collective-permute-done.9 = bf16[16,2048]{1,0:T(8,128)(2,1)S(1)} collective-permute-done((bf16[16,2048]{1,0:T(8,128)(2,1)S(1)}, bf16[16,2048]{1,0:T(8,128)(2,1)S(1)}, u32[]{:S(2)}, u32[]{:S(2)}) %collective-permute-start.9) | collective-permute-done | bytes 65568 | tf_op jit(solution)/shard_map/ppermute | solution.py:224
  33.4 0.0 collective-permute-done.7.refs_1_
  33.4 1.1 %combine.1 = bf16[128,2048]{1,0:T(8,128)(2,1)} custom-call(f32[16,128]{1,0:T(8,128)S(1)} %get-tuple-element.15.table_ref, bf16[16,2048]{1,0:T(8,128)(2,1)S(1)} %get-tuple-element.26.refs_0_, bf16[16,2048]{1,0:T(8,128)(2,1)S(1)} %collective-permute-done.7.refs_1_, bf16[16,2048]{1,0:T(8,128)(2,1)S(1)} %add_convert_fusion.refs_2_), custom_call_target="tpu_custom_call" | custom-call | tf_op jit(solution)/shard_map/combine/pallas_call | solution.py:203
  (5 shorter events, 0.1 us)
Async XLA Ops:
  2.1 7.9 %collective-permute-start.2 = (bf16[16,2048]{1,0:T(8,128)(2,1)S(1)}, bf16[16,2048]{1,0:T(8,128)(2,1)S(1)}, u32[]{:S(2)}, u32[]{:S(2)}) collective-permute-start(bf16[16,2048]{1,0:T(8,128)(2,1)S(1)} %get-tuple-element.16.refs_3_), channel_id=1, source_target_pairs={{0,16},{4,20},{8,24},{12,28},{16,0},{20,4},{24,8},{28,12},{1,17},{... | collective-permute-start | bytes 196616 | tf_op jit(solution)/shard_map/ppermute | solution.py:224
  6.2 6.3 %collective-permute-start.4 = (bf16[16,2048]{1,0:T(8,128)(2,1)S(1)}, bf16[16,2048]{1,0:T(8,128)(2,1)S(1)}, u32[]{:S(2)}, u32[]{:S(2)}) collective-permute-start(bf16[16,2048]{1,0:T(8,128)(2,1)S(1)} %get-tuple-element.16.refs_3_), channel_id=1, source_target_pairs={{0,24},{4,28},{8,16},{12,20},{16,8},{20,12},{24,0},{28,4},{1,25},{... | collective-permute-start | bytes 196616 | tf_op jit(solution)/shard_map/ppermute | solution.py:224
  7.6 6.4 %collective-permute-start = (bf16[16,2048]{1,0:T(8,128)(2,1)S(1)}, bf16[16,2048]{1,0:T(8,128)(2,1)S(1)}, u32[]{:S(2)}, u32[]{:S(2)}) collective-permute-start(bf16[16,2048]{1,0:T(8,128)(2,1)S(1)} %get-tuple-element.16.refs_3_), channel_id=1, source_target_pairs={{0,8},{4,12},{8,0},{12,4},{16,24},{20,28},{24,16},{28,20},{1,9},{5... | collective-permute-start | bytes 196616 | tf_op jit(solution)/shard_map/ppermute | solution.py:224
  10.0 5.1 %collective-permute-start.3 = (bf16[16,2048]{1,0:T(8,128)(2,1)S(1)}, bf16[16,2048]{1,0:T(8,128)(2,1)S(1)}, u32[]{:S(2)}, u32[]{:S(2)}) collective-permute-start(bf16[16,2048]{1,0:T(8,128)(2,1)S(1)} %collective-permute-done.2.refs_2_), channel_id=1, source_target_pairs={{0,4},{4,0},{8,12},{12,8},{16,20},{20,16},{24,28},{28,24},{1,5},{5... | collective-permute-start | bytes 196616 | tf_op jit(solution)/shard_map/ppermute | solution.py:224
  12.5 4.3 %collective-permute-start.5 = (bf16[16,2048]{1,0:T(8,128)(2,1)S(1)}, bf16[16,2048]{1,0:T(8,128)(2,1)S(1)}, u32[]{:S(2)}, u32[]{:S(2)}) collective-permute-start(bf16[16,2048]{1,0:T(8,128)(2,1)S(1)} %collective-permute-done.4.refs_3_), channel_id=1, source_target_pairs={{0,4},{4,0},{8,12},{12,8},{16,20},{20,16},{24,28},{28,24},{1,5},{5... | collective-permute-start | bytes 196616 | tf_op jit(solution)/shard_map/ppermute | solution.py:224
  14.0 6.4 %collective-permute-start.1 = (bf16[32,2048]{1,0:T(8,128)(2,1)S(1)}, bf16[32,2048]{1,0:T(8,128)(2,1)S(1)}, u32[]{:S(2)}, u32[]{:S(2)}) collective-permute-start(bf16[32,2048]{1,0:T(8,128)(2,1)S(1)} %constant_dynamic-update-slice_fusion.refs_1_), channel_id=1, source_target_pairs={{0,4},{4,0},{8,12},{12,8},{16,20},{20,16},{24,28},{28,24},{1,5},{5... | collective-permute-start | bytes 393224 | tf_op jit(solution)/shard_map/ppermute | solution.py:224
  17.7 5.3 %collective-permute-start.8 = (bf16[32,2048]{1,0:T(8,128)(2,1)S(1)}, bf16[32,2048]{1,0:T(8,128)(2,1)S(1)}, u32[]{:S(2)}, u32[]{:S(2)}) collective-permute-start(bf16[32,2048]{1,0:T(8,128)(2,1)S(1)} %get-tuple-element.20.refs_5_), channel_id=1, source_target_pairs={{0,4},{4,0},{8,12},{12,8},{16,20},{20,16},{24,28},{28,24},{1,5},{5... | collective-permute-start | bytes 393224 | tf_op jit(solution)/shard_map/ppermute | solution.py:224
  21.3 7.0 %collective-permute-start.6 = (bf16[32,2048]{1,0:T(8,128)(2,1)S(1)}, bf16[32,2048]{1,0:T(8,128)(2,1)S(1)}, u32[]{:S(2)}, u32[]{:S(2)}) collective-permute-start(bf16[32,2048]{1,0:T(8,128)(2,1)S(1)} %get-tuple-element.22), channel_id=1, source_target_pairs={{0,4},{4,0},{8,12},{12,8},{16,20},{20,16},{24,28},{28,24},{1,5},{5... | collective-permute-start | bytes 393224 | tf_op jit(solution)/shard_map/ppermute | solution.py:224
  23.0 7.8 %collective-permute-start.10 = (bf16[16,2048]{1,0:T(8,128)(2,1)S(1)}, bf16[16,2048]{1,0:T(8,128)(2,1)S(1)}, u32[]{:S(2)}, u32[]{:S(2)}) collective-permute-start(bf16[16,2048]{1,0:T(8,128)(2,1)S(1)} %get-tuple-element.28), channel_id=1, source_target_pairs={{0,24},{4,28},{8,16},{12,20},{16,8},{20,12},{24,0},{28,4},{1,25},{... | collective-permute-start | bytes 196616 | tf_op jit(solution)/shard_map/ppermute | solution.py:224
  28.2 5.2 %collective-permute-start.9 = (bf16[16,2048]{1,0:T(8,128)(2,1)S(1)}, bf16[16,2048]{1,0:T(8,128)(2,1)S(1)}, u32[]{:S(2)}, u32[]{:S(2)}) collective-permute-start(bf16[16,2048]{1,0:T(8,128)(2,1)S(1)} %get-tuple-element.27), channel_id=1, source_target_pairs={{0,16},{4,20},{8,24},{12,28},{16,0},{20,4},{24,8},{28,12},{1,17},{... | collective-permute-start | bytes 196616 | tf_op jit(solution)/shard_map/ppermute | solution.py:224
  28.3 5.1 %collective-permute-start.7 = (bf16[16,2048]{1,0:T(8,128)(2,1)S(1)}, bf16[16,2048]{1,0:T(8,128)(2,1)S(1)}, u32[]{:S(2)}, u32[]{:S(2)}) collective-permute-start(bf16[16,2048]{1,0:T(8,128)(2,1)S(1)} %get-tuple-element.25), channel_id=1, source_target_pairs={{0,8},{4,12},{8,0},{12,4},{16,24},{20,28},{24,16},{28,20},{1,9},{5... | collective-permute-start | bytes 196616 | tf_op jit(solution)/shard_map/ppermute | solution.py:224

commit v10 on v6

--- a/solution.py
+++ b/solution.py
@@ -19,7 +19,7 @@
 
 
 def pick_kernel(
-    live_ref, ids_hbm, gate_hbm, tokens_hbm, gain_hbm, rows_ref, table_ref, ids_ref, gate_ref, tokens_ref, gain_ref, sems
+    ids_hbm, gate_hbm, tokens_hbm, gain_hbm, rows_ref, table_ref, ids_ref, gate_ref, tokens_ref, gain_ref, sems
 ):
     ids_copy, gate_copy, gain_copy = (
         pltpu.make_async_copy(source, target, sems.at[TOKEN_CHUNKS + i])
@@ -27,28 +27,36 @@
             ((ids_hbm, ids_ref), (gate_hbm, gate_ref), (gain_hbm, gain_ref))
         )
     )
-    token_copies = list(chunk_copies(tokens_hbm, tokens_ref, TOKEN_CHUNKS, sems))
+    features = tokens_ref.shape[1]
+    width = features // TOKEN_CHUNKS
+    columns = [pl.ds(i * width, width) for i in range(TOKEN_CHUNKS)]
+    token_copies = [
+        pltpu.make_async_copy(tokens_hbm.at[:, some], tokens_ref.at[:, some], sems.at[i])
+        for i, some in enumerate(columns)
+    ]
     for copy in (ids_copy, *token_copies, gain_copy, gate_copy):
         copy.start()
     slots, tok_rows = table_ref.shape
     slot = lax.broadcasted_iota(jnp.int32, (slots, tok_rows), 0)
-    token = lax.broadcasted_iota(jnp.int32, (slots, tok_rows), 1)
     expert, place = slot // CAP, slot % CAP
-    live = token < live_ref[0]
     before = lax.broadcasted_iota(jnp.int32, (tok_rows, tok_rows), 0)
     after = lax.broadcasted_iota(jnp.int32, (tok_rows, tok_rows), 1)
     earlier = jnp.where(before < after, 1.0, 0.0).astype(jnp.bfloat16)
     ids_copy.wait()
-    hits = [(ids_ref[k : k + 1, :] == expert) & live for k in range(ids_ref.shape[0])]
+    hits = [ids_ref[k : k + 1, :] == expert for k in range(ids_ref.shape[0])]
     chosen = jnp.where(functools.reduce(jnp.logical_or, hits), 1.0, 0.0)
     rank = jnp.dot(chosen.astype(jnp.bfloat16), earlier, preferred_element_type=jnp.float32)
     pick = jnp.where((chosen > 0.0) & (rank.astype(jnp.int32) == place), 1.0, 0.0)
-    for copy in token_copies:
+    pick_rows = pick.astype(jnp.bfloat16)
+    values, square = [], 0.0
+    for copy, some in zip(token_copies, columns):
         copy.wait()
-    values = jnp.dot(pick.astype(jnp.bfloat16), tokens_ref[...], preferred_element_type=jnp.float32)
-    mean_sq = jnp.mean(values * values, axis=-1, keepdims=True)
+        values.append(jnp.dot(pick_rows, tokens_ref[:, some], preferred_element_type=jnp.float32))
+        square = square + jnp.sum(values[-1] * values[-1], axis=-1, keepdims=True)
+    scale = lax.rsqrt(square / features + 1e-06)
     gain_copy.wait()
-    rows_ref[...] = (values * lax.rsqrt(mean_sq + 1e-06) * gain_ref[...]).astype(jnp.bfloat16)
+    for part, some in zip(values, columns):
+        rows_ref[:, some] = (part * scale * gain_ref[:, some]).astype(jnp.bfloat16)
     gate_copy.wait()
     weight = jnp.zeros((slots, tok_rows), jnp.float32)
     for k, hit in enumerate(hits):
@@ -56,7 +64,7 @@
     table_ref[...] = pick * weight
 
 
-def pick_rows(slots, live_counts, ids, gate_vals, tokens, gain):
+def pick_rows(slots, ids, gate_vals, tokens, gain):
     vmem = pl.BlockSpec(memory_space=pltpu.VMEM)
     hbm = pl.BlockSpec(memory_space=pltpu.HBM)
     return pl.pallas_call(
@@ -65,7 +73,7 @@
             jax.ShapeDtypeStruct((slots, tokens.shape[1]), jnp.bfloat16),
             jax.ShapeDtypeStruct((slots, tokens.shape[0]), jnp.float32),
         ),
-        in_specs=[pl.BlockSpec(memory_space=pltpu.SMEM), hbm, hbm, hbm, hbm],
+        in_specs=[hbm] * 4,
         out_specs=(vmem, vmem),
         scratch_shapes=[
             pltpu.VMEM(ids.shape, ids.dtype),
@@ -76,7 +84,7 @@
         ],
         compiler_params=pltpu.CompilerParams(vmem_limit_bytes=VMEM_LIMIT),
         name="pick_rows",
-    )(live_counts, *(in_hbm(array) for array in (ids, gate_vals, tokens, gain)))
+    )(*(in_hbm(array) for array in (ids, gate_vals, tokens, gain)))
 
 
 def expert_rows(rows, gate_ref, up_ref, down_ref):
@@ -112,9 +120,9 @@
         yield pltpu.make_async_copy(source.at[at], target.at[at], sems.at[i])
 
 
-def stage_kernel(rows_ref, *refs):
+def stage_kernel(live_ref, rows_ref, table_ref, *refs):
     *refs, sems = refs
-    sources, out_ref, weights = refs[:3], refs[3], refs[4:]
+    sources, (rows_out, table_out), weights = refs[:3], refs[3:5], refs[5:]
     copies = [
         copy
         for i, pair in enumerate(zip(sources, weights))
@@ -122,25 +130,28 @@
     ]
     for copy in copies:
         copy.start()
-    out_ref[...] = rows_ref[...]
+    rows_out[...] = rows_ref[...]
+    token = lax.broadcasted_iota(jnp.int32, table_ref.shape, 1)
+    table_out[...] = jnp.where(token < live_ref[0], table_ref[...], 0.0)
     for copy in copies:
         copy.wait()
 
 
-def stage_weights(rows, weights):
+def stage_weights(live_counts, rows, table, weights):
     vmem = pl.BlockSpec(memory_space=pltpu.VMEM)
     hbm = pl.BlockSpec(memory_space=pltpu.HBM)
-    rows, *weights = pl.pallas_call(
+    arrays = (rows, table, *weights)
+    rows, table, *weights = pl.pallas_call(
         stage_kernel,
-        out_shape=[jax.ShapeDtypeStruct(array.shape, array.dtype) for array in (rows, *weights)],
-        in_specs=[vmem] + [hbm] * 3,
-        out_specs=[vmem] * 4,
+        out_shape=[jax.ShapeDtypeStruct(array.shape, array.dtype) for array in arrays],
+        in_specs=[pl.BlockSpec(memory_space=pltpu.SMEM), vmem, vmem] + [hbm] * 3,
+        out_specs=[vmem] * 5,
         scratch_shapes=[pltpu.SemaphoreType.DMA((3, WEIGHT_CHUNKS))],
         compiler_params=pltpu.CompilerParams(vmem_limit_bytes=VMEM_LIMIT),
         cost_estimate=expert_cost([rows], weights),
         name="stage_weights",
-    )(rows, *(in_hbm(weight) for weight in weights))
-    return rows, weights
+    )(live_counts, rows, table, *(in_hbm(weight) for weight in weights))
+    return rows, table, weights
 
 
 def slice_kernel(count, *refs):
@@ -227,11 +238,11 @@
     flight = devices // SLICES
     slots = flight * CAP
     rows, table = pick_rows(
-        slots, live_counts, expert_ids.T, gate_vals.T, tokens, norm_gain.reshape(1, features)
+        slots, expert_ids.T, gate_vals.T, tokens, norm_gain.reshape(1, features)
     )
     own = across_groups(flight, rows)
     farther, far = swap(devices, 6, own), swap(devices, 4, own)
-    own, weights = stage_weights(own, (w_gate.T, w_up.T, w_down))
+    own, table, weights = stage_weights(live_counts, own, table, (w_gate.T, w_up.T, w_down))
     near = swap(devices, 2, own)
     outer, inner = jnp.concatenate([far, farther]), jnp.concatenate([own, near])
     outer_y, inner_y = swap(devices, 1, outer), swap(devices, 1, inner)

time: 34 us -> 33.8 us (level)
  waiting for transfers between devices: 12.5 us -> 11.4 us
  starting transfers between devices: 14.5 us -> 15.1 us
  Pallas kernels: 5.97 us -> 6.38 us
    ppermute x10, waiting for transfers between devices: 12.5 us -> 11.4 us  [swap(): lax.ppermute(block, 'ep', [(i, i ^ distance) for i in range(devices)])]
    ppermute x10, starting transfers between devices: 14.5 us -> 15.1 us  [swap(): lax.ppermute(block, 'ep', [(i, i ^ distance) for i in range(devices)])]
    pallas_call x1, Pallas kernels: 1.47 us -> 1.87 us  [pick_rows(): pl.pallas_call(pick_kernel, out_shape=(jax.ShapeDtypeStruct((slots, token...]
  transfers between devices with their start and end apart: 10 -> 10, of which waited for: 7 -> 5; matrix products, arithmetic and copies ran while one was open for 0% -> 0% of each run, Pallas kernels for 10% -> 10%
where the time goes in v10:
time: 33.8 us; the launch traced here: 33.7 us
  starting transfers between devices  15.1 us (45%)
  waiting for transfers between devices  11.4 us (34%)
  Pallas kernels  6.38 us (19%)
  between operations  0.72 us (2%)
    ppermute x10, starting transfers between devices, swap(): lax.ppermute(block, 'ep', [(i, i ^ distance) for i in range(devices)])  15.1 us
    ppermute x10, waiting for transfers between devices, swap(): lax.ppermute(block, 'ep', [(i, i ^ distance) for i in range(devices)])  11.4 us
    pallas_call x1, Pallas kernels, pick_rows(): pl.pallas_call(pick_kernel, out_shape=(jax.ShapeDtypeStruct((slots, token...  1.87 us
    pallas_call x1, Pallas kernels, stage_weights(): pl.pallas_call(stage_kernel, out_shape=[jax.ShapeDtypeStruct(array.shape,...  1.8 us
    pallas_call x2, Pallas kernels, expert_slice(): pl.pallas_call(functools.partial(slice_kernel, count), out_shape=[jax.Sha...  1.66 us
    pallas_call x1, Pallas kernels, combine(): pl.pallas_call(combine_kernel, out_shape=jax.ShapeDtypeStruct(shape, jnp....  1.04 us
  transfers between devices with their start and end apart: 10, of which 5 were waited for; matrix products, arithmetic and copies ran while one was open for 0% of the time, Pallas kernels for 10%

profile of v10, /device:TPU:0, one launch (start us, length us, event | category | flops | bytes accessed | tf_op | source)
XLA Modules:
  0.0 33.7 jit_solution(15687979807327202432)
XLA Ops:
  0.0 1.9 %pick_rows.1 = (bf16[16,2048]{1,0:T(8,128)(2,1)S(1)}, f32[16,128]{1,0:T(8,128)S(1)}) custom-call(s32[8,128]{1,0:T(8,128)} %bitcast.8, f32[8,128]{1,0:T(8,128)} %bitcast.9, bf16[128,2048]{1,0:T(8,128)(2,1)} %tokens_hbm.1, f32[1,2048]{1,0:T(1,128)} %bitcast.7), custom_call_target="tpu_custom_call" | custom-call | tf_op jit(solution)/shard_map/pick_rows/pallas_call | solution.py:70
  1.9 5.1 %collective-permute-start.1 = (bf16[16,2048]{1,0:T(8,128)(2,1)S(1)}, bf16[16,2048]{1,0:T(8,128)(2,1)S(1)}, u32[]{:S(2)}, u32[]{:S(2)}) collective-permute-start(bf16[16,2048]{1,0:T(8,128)(2,1)S(1)} %get-tuple-element.15.rows_ref), channel_id=1, source_target_pairs={{0,24},{4,28},{8,16},{12,20},{16,8},{20,12},{24,0},{28,4},{1,25},{... | collective-permute-start | bytes 196616 | tf_op jit(solution)/shard_map/ppermute | solution.py:232
  7.0 0.0 collective-permute-start
  7.6 1.8 %stage_weights.1 = (bf16[16,2048]{1,0:T(8,128)(2,1)S(1)}, f32[16,128]{1,0:T(8,128)S(1)}, bf16[192,2048]{1,0:T(8,128)(2,1)S(1)}, bf16[192,2048]{1,0:T(8,128)(2,1)S(1)}, bf16[192,2048]{1,0:T(8,128)(2,1)S(1)}) custom-call(s32[1]{0:T(128)S(6)} %copy.11.live_ref, bf16[16,2048]{1,0:T(8,128)(2,1)S(1)} %get-tuple-element.15.rows_ref, ...), custom_call_target="tpu_custom_call" | custom-call | flops 37748736 | bytes 2359296 | tf_op jit(solution)/shard_map/stage_weights/pallas_call | solution.py:144
  9.5 0.7 %collective-permute-start.2 = (bf16[16,2048]{1,0:T(8,128)(2,1)S(1)}, bf16[16,2048]{1,0:T(8,128)(2,1)S(1)}, u32[]{:S(2)}, u32[]{:S(2)}) collective-permute-start(bf16[16,2048]{1,0:T(8,128)(2,1)S(1)} %get-tuple-element.18), channel_id=1, source_target_pairs={{0,8},{4,12},{8,0},{12,4},{16,24},{20,28},{24,16},{28,20},{1,9},{5... | collective-permute-start | bytes 196616 | tf_op jit(solution)/shard_map/ppermute | solution.py:232
  10.2 2.5 %collective-permute-done = bf16[16,2048]{1,0:T(8,128)(2,1)S(1)} collective-permute-done((bf16[16,2048]{1,0:T(8,128)(2,1)S(1)}, bf16[16,2048]{1,0:T(8,128)(2,1)S(1)}, u32[]{:S(2)}, u32[]{:S(2)}) %collective-permute-start) | collective-permute-done | bytes 65568 | tf_op jit(solution)/shard_map/ppermute | solution.py:232
  12.7 0.0 collective-permute-done.1
  12.7 1.6 %collective-permute-start.4 = (bf16[32,2048]{1,0:T(8,128)(2,1)S(1)}, bf16[32,2048]{1,0:T(8,128)(2,1)S(1)}, u32[]{:S(2)}, u32[]{:S(2)}) collective-permute-start(bf16[32,2048]{1,0:T(8,128)(2,1)S(1)} %constant_dynamic-update-slice_fusion.refs_0_), channel_id=1, source_target_pairs={{0,4},{4,0},{8,12},{12,8},{16,20},{20,16},{24,28},{28,24},{1,5},{5... | collective-permute-start | bytes 393224 | tf_op jit(solution)/shard_map/ppermute | solution.py:232
  14.3 0.0 collective-permute-done.2
  14.3 1.2 %collective-permute-start.3 = (bf16[32,2048]{1,0:T(8,128)(2,1)S(1)}, bf16[32,2048]{1,0:T(8,128)(2,1)S(1)}, u32[]{:S(2)}, u32[]{:S(2)}) collective-permute-start(bf16[32,2048]{1,0:T(8,128)(2,1)S(1)} %constant_dynamic-update-slice_fusion.2.refs_1_), channel_id=1, source_target_pairs={{0,4},{4,0},{8,12},{12,8},{16,20},{20,16},{24,28},{28,24},{1,5},{5... | collective-permute-start | bytes 393224 | tf_op jit(solution)/shard_map/ppermute | solution.py:232
  15.5 3.5 %collective-permute-done.4.refs_0_ = bf16[32,2048]{1,0:T(8,128)(2,1)S(1)} collective-permute-done((bf16[32,2048]{1,0:T(8,128)(2,1)S(1)}, bf16[32,2048]{1,0:T(8,128)(2,1)S(1)}, u32[]{:S(2)}, u32[]{:S(2)}) %collective-permute-start.4) | collective-permute-done | bytes 131104 | tf_op jit(solution)/shard_map/ppermute | solution.py:232
  19.1 0.8 %expert_slice.2.refs_6_ = bf16[32,2048]{1,0:T(8,128)(2,1)S(1)} custom-call(bf16[32,2048]{1,0:T(8,128)(2,1)S(1)} %collective-permute-done.4.refs_0_, bf16[192,2048]{1,0:T(8,128)(2,1)S(1)} %get-tuple-element.19.refs_1_.refs_3_, bf16[192,2048]{1,0:T(8,128)(2,1)S(1)} %get-tuple-element.20.refs_2_.refs_4_, bf16[192,2048]{1,0:T(8,128)(2,1)S(1)} %get-tuple-element.21.refs_3_.refs_5_), custom_call_target="tpu_custom_call" | custom-call | flops 75497472 | bytes 2359296 | tf_op jit(solution)/shard_map/expert_slice/pallas_call | solution.py:165
  19.9 1.7 %collective-permute-start.7 = (bf16[32,2048]{1,0:T(8,128)(2,1)S(1)}, bf16[32,2048]{1,0:T(8,128)(2,1)S(1)}, u32[]{:S(2)}, u32[]{:S(2)}) collective-permute-start(bf16[32,2048]{1,0:T(8,128)(2,1)S(1)} %expert_slice.2.refs_6_), channel_id=1, source_target_pairs={{0,4},{4,0},{8,12},{12,8},{16,20},{20,16},{24,28},{28,24},{1,5},{5... | collective-permute-start | bytes 393224 | tf_op jit(solution)/shard_map/ppermute | solution.py:232
  21.6 0.0 collective-permute-done.3.refs_2_
  21.6 0.9 %expert_slice.3 = (bf16[32,2048]{1,0:T(8,128)(2,1)S(1)}, bf16[32,2048]{1,0:T(8,128)(2,1)S(1)}, bf16[32,2048]{1,0:T(8,128)(2,1)S(1)}) custom-call(bf16[32,2048]{1,0:T(8,128)(2,1)S(1)} %constant_dynamic-update-slice_fusion.refs_0_, bf16[32,2048]{1,0:T(8,128)(2,1)S(1)} %constant_dynamic-update-slice_fusion.2.refs_1_, ...), custom_call_target="tpu_custom_call" | custom-call | flops 226492416 | bytes 2359296 | tf_op jit(solution)/shard_map/expert_slice/pallas_call | solution.py:165
  22.4 1.2 %collective-permute-start.5 = (bf16[32,2048]{1,0:T(8,128)(2,1)S(1)}, bf16[32,2048]{1,0:T(8,128)(2,1)S(1)}, u32[]{:S(2)}, u32[]{:S(2)}) collective-permute-start(bf16[32,2048]{1,0:T(8,128)(2,1)S(1)} %get-tuple-element.23), channel_id=1, source_target_pairs={{0,4},{4,0},{8,12},{12,8},{16,20},{20,16},{24,28},{28,24},{1,5},{5... | collective-permute-start | bytes 393224 | tf_op jit(solution)/shard_map/ppermute | solution.py:232
  23.6 2.1 %collective-permute-done.7 = bf16[32,2048]{1,0:T(8,128)(2,1)S(1)} collective-permute-done((bf16[32,2048]{1,0:T(8,128)(2,1)S(1)}, bf16[32,2048]{1,0:T(8,128)(2,1)S(1)}, u32[]{:S(2)}, u32[]{:S(2)}) %collective-permute-start.7) | collective-permute-done | bytes 131104 | tf_op jit(solution)/shard_map/ppermute | solution.py:232
  25.8 0.7 %collective-permute-start.8 = (bf16[16,2048]{1,0:T(8,128)(2,1)S(1)}, bf16[16,2048]{1,0:T(8,128)(2,1)S(1)}, u32[]{:S(2)}, u32[]{:S(2)}) collective-permute-start(bf16[16,2048]{1,0:T(8,128)(2,1)S(1)} %get-tuple-element.25), channel_id=1, source_target_pairs={{0,16},{4,20},{8,24},{12,28},{16,0},{20,4},{24,8},{28,12},{1,17},{... | collective-permute-start | bytes 196616 | tf_op jit(solution)/shard_map/ppermute | solution.py:232
  26.5 1.0 %collective-permute-start.9 = (bf16[16,2048]{1,0:T(8,128)(2,1)S(1)}, bf16[16,2048]{1,0:T(8,128)(2,1)S(1)}, u32[]{:S(2)}, u32[]{:S(2)}) collective-permute-start(bf16[16,2048]{1,0:T(8,128)(2,1)S(1)} %get-tuple-element.26), channel_id=1, source_target_pairs={{0,24},{4,28},{8,16},{12,20},{16,8},{20,12},{24,0},{28,4},{1,25},{... | collective-permute-start | bytes 196616 | tf_op jit(solution)/shard_map/ppermute | solution.py:232
  27.5 0.0 collective-permute-done.5
  27.6 1.9 %collective-permute-start.6 = (bf16[16,2048]{1,0:T(8,128)(2,1)S(1)}, bf16[16,2048]{1,0:T(8,128)(2,1)S(1)}, u32[]{:S(2)}, u32[]{:S(2)}) collective-permute-start(bf16[16,2048]{1,0:T(8,128)(2,1)S(1)} %get-tuple-element.27), channel_id=1, source_target_pairs={{0,8},{4,12},{8,0},{12,4},{16,24},{20,28},{24,16},{28,20},{1,9},{5... | collective-permute-start | bytes 196616 | tf_op jit(solution)/shard_map/ppermute | solution.py:232
  29.4 1.6 %collective-permute-done.8 = bf16[16,2048]{1,0:T(8,128)(2,1)S(1)} collective-permute-done((bf16[16,2048]{1,0:T(8,128)(2,1)S(1)}, bf16[16,2048]{1,0:T(8,128)(2,1)S(1)}, u32[]{:S(2)}, u32[]{:S(2)}) %collective-permute-start.8) | collective-permute-done | bytes 65568 | tf_op jit(solution)/shard_map/ppermute | solution.py:232
  31.0 1.6 %collective-permute-done.9 = bf16[16,2048]{1,0:T(8,128)(2,1)S(1)} collective-permute-done((bf16[16,2048]{1,0:T(8,128)(2,1)S(1)}, bf16[16,2048]{1,0:T(8,128)(2,1)S(1)}, u32[]{:S(2)}, u32[]{:S(2)}) %collective-permute-start.9) | collective-permute-done | bytes 65568 | tf_op jit(solution)/shard_map/ppermute | solution.py:232
  32.6 0.0 collective-permute-done.6.refs_1_
  32.6 1.0 %combine.1 = bf16[128,2048]{1,0:T(8,128)(2,1)} custom-call(f32[16,128]{1,0:T(8,128)S(1)} %get-tuple-element.17.table_ref, bf16[16,2048]{1,0:T(8,128)(2,1)S(1)} %get-tuple-element.28.refs_0_, bf16[16,2048]{1,0:T(8,128)(2,1)S(1)} %collective-permute-done.6.refs_1_, bf16[16,2048]{1,0:T(8,128)(2,1)S(1)} %add_convert_fusion.refs_2_), custom_call_target="tpu_custom_call" | custom-call | tf_op jit(solution)/shard_map/combine/pallas_call | solution.py:211
  (7 shorter events, 0.1 us)
Async XLA Ops:
  1.9 10.8 %collective-permute-start.1 = (bf16[16,2048]{1,0:T(8,128)(2,1)S(1)}, bf16[16,2048]{1,0:T(8,128)(2,1)S(1)}, u32[]{:S(2)}, u32[]{:S(2)}) collective-permute-start(bf16[16,2048]{1,0:T(8,128)(2,1)S(1)} %get-tuple-element.15.rows_ref), channel_id=1, source_target_pairs={{0,24},{4,28},{8,16},{12,20},{16,8},{20,12},{24,0},{28,4},{1,25},{... | collective-permute-start | bytes 196616 | tf_op jit(solution)/shard_map/ppermute | solution.py:232
  7.0 5.7 %collective-permute-start = (bf16[16,2048]{1,0:T(8,128)(2,1)S(1)}, bf16[16,2048]{1,0:T(8,128)(2,1)S(1)}, u32[]{:S(2)}, u32[]{:S(2)}) collective-permute-start(bf16[16,2048]{1,0:T(8,128)(2,1)S(1)} %get-tuple-element.15.rows_ref), channel_id=1, source_target_pairs={{0,16},{4,20},{8,24},{12,28},{16,0},{20,4},{24,8},{28,12},{1,17},{... | collective-permute-start | bytes 196616 | tf_op jit(solution)/shard_map/ppermute | solution.py:232
  9.5 4.9 %collective-permute-start.2 = (bf16[16,2048]{1,0:T(8,128)(2,1)S(1)}, bf16[16,2048]{1,0:T(8,128)(2,1)S(1)}, u32[]{:S(2)}, u32[]{:S(2)}) collective-permute-start(bf16[16,2048]{1,0:T(8,128)(2,1)S(1)} %get-tuple-element.18), channel_id=1, source_target_pairs={{0,8},{4,12},{8,0},{12,4},{16,24},{20,28},{24,16},{28,20},{1,9},{5... | collective-permute-start | bytes 196616 | tf_op jit(solution)/shard_map/ppermute | solution.py:232
  12.7 6.3 %collective-permute-start.4 = (bf16[32,2048]{1,0:T(8,128)(2,1)S(1)}, bf16[32,2048]{1,0:T(8,128)(2,1)S(1)}, u32[]{:S(2)}, u32[]{:S(2)}) collective-permute-start(bf16[32,2048]{1,0:T(8,128)(2,1)S(1)} %constant_dynamic-update-slice_fusion.refs_0_), channel_id=1, source_target_pairs={{0,4},{4,0},{8,12},{12,8},{16,20},{20,16},{24,28},{28,24},{1,5},{5... | collective-permute-start | bytes 393224 | tf_op jit(solution)/shard_map/ppermute | solution.py:232
  14.3 7.3 %collective-permute-start.3 = (bf16[32,2048]{1,0:T(8,128)(2,1)S(1)}, bf16[32,2048]{1,0:T(8,128)(2,1)S(1)}, u32[]{:S(2)}, u32[]{:S(2)}) collective-permute-start(bf16[32,2048]{1,0:T(8,128)(2,1)S(1)} %constant_dynamic-update-slice_fusion.2.refs_1_), channel_id=1, source_target_pairs={{0,4},{4,0},{8,12},{12,8},{16,20},{20,16},{24,28},{28,24},{1,5},{5... | collective-permute-start | bytes 393224 | tf_op jit(solution)/shard_map/ppermute | solution.py:232
  19.9 5.9 %collective-permute-start.7 = (bf16[32,2048]{1,0:T(8,128)(2,1)S(1)}, bf16[32,2048]{1,0:T(8,128)(2,1)S(1)}, u32[]{:S(2)}, u32[]{:S(2)}) collective-permute-start(bf16[32,2048]{1,0:T(8,128)(2,1)S(1)} %expert_slice.2.refs_6_), channel_id=1, source_target_pairs={{0,4},{4,0},{8,12},{12,8},{16,20},{20,16},{24,28},{28,24},{1,5},{5... | collective-permute-start | bytes 393224 | tf_op jit(solution)/shard_map/ppermute | solution.py:232
  22.4 5.1 %collective-permute-start.5 = (bf16[32,2048]{1,0:T(8,128)(2,1)S(1)}, bf16[32,2048]{1,0:T(8,128)(2,1)S(1)}, u32[]{:S(2)}, u32[]{:S(2)}) collective-permute-start(bf16[32,2048]{1,0:T(8,128)(2,1)S(1)} %get-tuple-element.23), channel_id=1, source_target_pairs={{0,4},{4,0},{8,12},{12,8},{16,20},{20,16},{24,28},{28,24},{1,5},{5... | collective-permute-start | bytes 393224 | tf_op jit(solution)/shard_map/ppermute | solution.py:232
  25.8 5.2 %collective-permute-start.8 = (bf16[16,2048]{1,0:T(8,128)(2,1)S(1)}, bf16[16,2048]{1,0:T(8,128)(2,1)S(1)}, u32[]{:S(2)}, u32[]{:S(2)}) collective-permute-start(bf16[16,2048]{1,0:T(8,128)(2,1)S(1)} %get-tuple-element.25), channel_id=1, source_target_pairs={{0,16},{4,20},{8,24},{12,28},{16,0},{20,4},{24,8},{28,12},{1,17},{... | collective-permute-start | bytes 196616 | tf_op jit(solution)/shard_map/ppermute | solution.py:232
  26.5 6.1 %collective-permute-start.9 = (bf16[16,2048]{1,0:T(8,128)(2,1)S(1)}, bf16[16,2048]{1,0:T(8,128)(2,1)S(1)}, u32[]{:S(2)}, u32[]{:S(2)}) collective-permute-start(bf16[16,2048]{1,0:T(8,128)(2,1)S(1)} %get-tuple-element.26), channel_id=1, source_target_pairs={{0,24},{4,28},{8,16},{12,20},{16,8},{20,12},{24,0},{28,4},{1,25},{... | collective-permute-start | bytes 196616 | tf_op jit(solution)/shard_map/ppermute | solution.py:232
  27.6 5.1 %collective-permute-start.6 = (bf16[16,2048]{1,0:T(8,128)(2,1)S(1)}, bf16[16,2048]{1,0:T(8,128)(2,1)S(1)}, u32[]{:S(2)}, u32[]{:S(2)}) collective-permute-start(bf16[16,2048]{1,0:T(8,128)(2,1)S(1)} %get-tuple-element.27), channel_id=1, source_target_pairs={{0,8},{4,12},{8,0},{12,4},{16,24},{20,28},{24,16},{28,20},{1,9},{5... | collective-permute-start | bytes 196616 | tf_op jit(solution)/shard_map/ppermute | solution.py:232

commit v11 on v10

--- a/solution.py
+++ b/solution.py
@@ -11,7 +11,6 @@
 CAP = 16
 VMEM_LIMIT = 40 * 1024 * 1024
 WEIGHT_CHUNKS = 4
-TOKEN_CHUNKS = 4
 
 
 def in_hbm(array):
@@ -22,19 +21,13 @@
     ids_hbm, gate_hbm, tokens_hbm, gain_hbm, rows_ref, table_ref, ids_ref, gate_ref, tokens_ref, gain_ref, sems
 ):
     ids_copy, gate_copy, gain_copy = (
-        pltpu.make_async_copy(source, target, sems.at[TOKEN_CHUNKS + i])
+        pltpu.make_async_copy(source, target, sems.at[i])
         for i, (source, target) in enumerate(
             ((ids_hbm, ids_ref), (gate_hbm, gate_ref), (gain_hbm, gain_ref))
         )
     )
-    features = tokens_ref.shape[1]
-    width = features // TOKEN_CHUNKS
-    columns = [pl.ds(i * width, width) for i in range(TOKEN_CHUNKS)]
-    token_copies = [
-        pltpu.make_async_copy(tokens_hbm.at[:, some], tokens_ref.at[:, some], sems.at[i])
-        for i, some in enumerate(columns)
-    ]
-    for copy in (ids_copy, *token_copies, gain_copy, gate_copy):
+    tokens_copy = pltpu.make_async_copy(tokens_hbm, tokens_ref, sems.at[3])
+    for copy in (tokens_copy, ids_copy, gain_copy, gate_copy):
         copy.start()
     slots, tok_rows = table_ref.shape
     slot = lax.broadcasted_iota(jnp.int32, (slots, tok_rows), 0)
@@ -47,16 +40,11 @@
     chosen = jnp.where(functools.reduce(jnp.logical_or, hits), 1.0, 0.0)
     rank = jnp.dot(chosen.astype(jnp.bfloat16), earlier, preferred_element_type=jnp.float32)
     pick = jnp.where((chosen > 0.0) & (rank.astype(jnp.int32) == place), 1.0, 0.0)
-    pick_rows = pick.astype(jnp.bfloat16)
-    values, square = [], 0.0
-    for copy, some in zip(token_copies, columns):
-        copy.wait()
-        values.append(jnp.dot(pick_rows, tokens_ref[:, some], preferred_element_type=jnp.float32))
-        square = square + jnp.sum(values[-1] * values[-1], axis=-1, keepdims=True)
-    scale = lax.rsqrt(square / features + 1e-06)
+    tokens_copy.wait()
+    values = jnp.dot(pick.astype(jnp.bfloat16), tokens_ref[...], preferred_element_type=jnp.float32)
+    mean_sq = jnp.mean(values * values, axis=-1, keepdims=True)
     gain_copy.wait()
-    for part, some in zip(values, columns):
-        rows_ref[:, some] = (part * scale * gain_ref[:, some]).astype(jnp.bfloat16)
+    rows_ref[...] = (values * lax.rsqrt(mean_sq + 1e-06) * gain_ref[...]).astype(jnp.bfloat16)
     gate_copy.wait()
     weight = jnp.zeros((slots, tok_rows), jnp.float32)
     for k, hit in enumerate(hits):
@@ -80,7 +68,7 @@
             pltpu.VMEM(gate_vals.shape, gate_vals.dtype),
             pltpu.VMEM(tokens.shape, tokens.dtype),
             pltpu.VMEM(gain.shape, gain.dtype),
-            pltpu.SemaphoreType.DMA((TOKEN_CHUNKS + 3,)),
+            pltpu.SemaphoreType.DMA((4,)),
         ],
         compiler_params=pltpu.CompilerParams(vmem_limit_bytes=VMEM_LIMIT),
         name="pick_rows",

time: 33.8 us -> 33.3 us (0.985)
  Pallas kernels: 6.38 us -> 5.88 us
    pallas_call x1, Pallas kernels: 1.87 us -> 1.37 us  [pick_rows(): pl.pallas_call(pick_kernel, out_shape=(jax.ShapeDtypeStruct((slots, token...]
where the time goes in v11:
time: 33.3 us; the launch traced here: 33.2 us
  starting transfers between devices  15.1 us (45%)
  waiting for transfers between devices  11.4 us (34%)
  Pallas kernels  5.88 us (18%)
  between operations  0.72 us (2%)
    ppermute x10, starting transfers between devices, swap(): lax.ppermute(block, 'ep', [(i, i ^ distance) for i in range(devices)])  15.1 us
    ppermute x10, waiting for transfers between devices, swap(): lax.ppermute(block, 'ep', [(i, i ^ distance) for i in range(devices)])  11.4 us
    pallas_call x1, Pallas kernels, stage_weights(): pl.pallas_call(stage_kernel, out_shape=[jax.ShapeDtypeStruct(array.shape,...  1.8 us
    pallas_call x2, Pallas kernels, expert_slice(): pl.pallas_call(functools.partial(slice_kernel, count), out_shape=[jax.Sha...  1.66 us
    pallas_call x1, Pallas kernels, pick_rows(): pl.pallas_call(pick_kernel, out_shape=(jax.ShapeDtypeStruct((slots, token...  1.37 us
    pallas_call x1, Pallas kernels, combine(): pl.pallas_call(combine_kernel, out_shape=jax.ShapeDtypeStruct(shape, jnp....  1.05 us
  transfers between devices with their start and end apart: 10, of which 5 were waited for; matrix products, arithmetic and copies ran while one was open for 0% of the time, Pallas kernels for 10%

profile of v11, /device:TPU:0, one launch (start us, length us, event | category | flops | bytes accessed | tf_op | source)
XLA Modules:
  0.0 33.2 jit_solution(6372761267124377645)
XLA Ops:
  0.0 1.4 %pick_rows.1 = (bf16[16,2048]{1,0:T(8,128)(2,1)S(1)}, f32[16,128]{1,0:T(8,128)S(1)}) custom-call(s32[8,128]{1,0:T(8,128)} %bitcast.8, f32[8,128]{1,0:T(8,128)} %bitcast.9, bf16[128,2048]{1,0:T(8,128)(2,1)} %tokens_hbm.1, f32[1,2048]{1,0:T(1,128)} %bitcast.7), custom_call_target="tpu_custom_call" | custom-call | tf_op jit(solution)/shard_map/pick_rows/pallas_call | solution.py:58
  1.4 5.1 %collective-permute-start.1 = (bf16[16,2048]{1,0:T(8,128)(2,1)S(1)}, bf16[16,2048]{1,0:T(8,128)(2,1)S(1)}, u32[]{:S(2)}, u32[]{:S(2)}) collective-permute-start(bf16[16,2048]{1,0:T(8,128)(2,1)S(1)} %get-tuple-element.15.rows_ref), channel_id=1, source_target_pairs={{0,24},{4,28},{8,16},{12,20},{16,8},{20,12},{24,0},{28,4},{1,25},{... | collective-permute-start | bytes 196616 | tf_op jit(solution)/shard_map/ppermute | solution.py:220
  6.5 0.0 collective-permute-start
  7.1 1.8 %stage_weights.1 = (bf16[16,2048]{1,0:T(8,128)(2,1)S(1)}, f32[16,128]{1,0:T(8,128)S(1)}, bf16[192,2048]{1,0:T(8,128)(2,1)S(1)}, bf16[192,2048]{1,0:T(8,128)(2,1)S(1)}, bf16[192,2048]{1,0:T(8,128)(2,1)S(1)}) custom-call(s32[1]{0:T(128)S(6)} %copy.11.live_ref, bf16[16,2048]{1,0:T(8,128)(2,1)S(1)} %get-tuple-element.15.rows_ref, ...), custom_call_target="tpu_custom_call" | custom-call | flops 37748736 | bytes 2359296 | tf_op jit(solution)/shard_map/stage_weights/pallas_call | solution.py:132
  9.0 0.7 %collective-permute-start.2 = (bf16[16,2048]{1,0:T(8,128)(2,1)S(1)}, bf16[16,2048]{1,0:T(8,128)(2,1)S(1)}, u32[]{:S(2)}, u32[]{:S(2)}) collective-permute-start(bf16[16,2048]{1,0:T(8,128)(2,1)S(1)} %get-tuple-element.18), channel_id=1, source_target_pairs={{0,8},{4,12},{8,0},{12,4},{16,24},{20,28},{24,16},{28,20},{1,9},{5... | collective-permute-start | bytes 196616 | tf_op jit(solution)/shard_map/ppermute | solution.py:220
  9.7 2.5 %collective-permute-done = bf16[16,2048]{1,0:T(8,128)(2,1)S(1)} collective-permute-done((bf16[16,2048]{1,0:T(8,128)(2,1)S(1)}, bf16[16,2048]{1,0:T(8,128)(2,1)S(1)}, u32[]{:S(2)}, u32[]{:S(2)}) %collective-permute-start) | collective-permute-done | bytes 65568 | tf_op jit(solution)/shard_map/ppermute | solution.py:220
  12.2 0.0 collective-permute-done.1
  12.2 1.6 %collective-permute-start.4 = (bf16[32,2048]{1,0:T(8,128)(2,1)S(1)}, bf16[32,2048]{1,0:T(8,128)(2,1)S(1)}, u32[]{:S(2)}, u32[]{:S(2)}) collective-permute-start(bf16[32,2048]{1,0:T(8,128)(2,1)S(1)} %constant_dynamic-update-slice_fusion.refs_0_), channel_id=1, source_target_pairs={{0,4},{4,0},{8,12},{12,8},{16,20},{20,16},{24,28},{28,24},{1,5},{5... | collective-permute-start | bytes 393224 | tf_op jit(solution)/shard_map/ppermute | solution.py:220
  13.8 0.0 collective-permute-done.2
  13.8 1.2 %collective-permute-start.3 = (bf16[32,2048]{1,0:T(8,128)(2,1)S(1)}, bf16[32,2048]{1,0:T(8,128)(2,1)S(1)}, u32[]{:S(2)}, u32[]{:S(2)}) collective-permute-start(bf16[32,2048]{1,0:T(8,128)(2,1)S(1)} %constant_dynamic-update-slice_fusion.2.refs_1_), channel_id=1, source_target_pairs={{0,4},{4,0},{8,12},{12,8},{16,20},{20,16},{24,28},{28,24},{1,5},{5... | collective-permute-start | bytes 393224 | tf_op jit(solution)/shard_map/ppermute | solution.py:220
  15.0 3.5 %collective-permute-done.4.refs_0_ = bf16[32,2048]{1,0:T(8,128)(2,1)S(1)} collective-permute-done((bf16[32,2048]{1,0:T(8,128)(2,1)S(1)}, bf16[32,2048]{1,0:T(8,128)(2,1)S(1)}, u32[]{:S(2)}, u32[]{:S(2)}) %collective-permute-start.4) | collective-permute-done | bytes 131104 | tf_op jit(solution)/shard_map/ppermute | solution.py:220
  18.6 0.8 %expert_slice.2.refs_6_ = bf16[32,2048]{1,0:T(8,128)(2,1)S(1)} custom-call(bf16[32,2048]{1,0:T(8,128)(2,1)S(1)} %collective-permute-done.4.refs_0_, bf16[192,2048]{1,0:T(8,128)(2,1)S(1)} %get-tuple-element.19.refs_1_.refs_3_, bf16[192,2048]{1,0:T(8,128)(2,1)S(1)} %get-tuple-element.20.refs_2_.refs_4_, bf16[192,2048]{1,0:T(8,128)(2,1)S(1)} %get-tuple-element.21.refs_3_.refs_5_), custom_call_target="tpu_custom_call" | custom-call | flops 75497472 | bytes 2359296 | tf_op jit(solution)/shard_map/expert_slice/pallas_call | solution.py:153
  19.4 1.7 %collective-permute-start.7 = (bf16[32,2048]{1,0:T(8,128)(2,1)S(1)}, bf16[32,2048]{1,0:T(8,128)(2,1)S(1)}, u32[]{:S(2)}, u32[]{:S(2)}) collective-permute-start(bf16[32,2048]{1,0:T(8,128)(2,1)S(1)} %expert_slice.2.refs_6_), channel_id=1, source_target_pairs={{0,4},{4,0},{8,12},{12,8},{16,20},{20,16},{24,28},{28,24},{1,5},{5... | collective-permute-start | bytes 393224 | tf_op jit(solution)/shard_map/ppermute | solution.py:220
  21.1 0.0 collective-permute-done.3.refs_2_
  21.1 0.9 %expert_slice.3 = (bf16[32,2048]{1,0:T(8,128)(2,1)S(1)}, bf16[32,2048]{1,0:T(8,128)(2,1)S(1)}, bf16[32,2048]{1,0:T(8,128)(2,1)S(1)}) custom-call(bf16[32,2048]{1,0:T(8,128)(2,1)S(1)} %constant_dynamic-update-slice_fusion.refs_0_, bf16[32,2048]{1,0:T(8,128)(2,1)S(1)} %constant_dynamic-update-slice_fusion.2.refs_1_, ...), custom_call_target="tpu_custom_call" | custom-call | flops 226492416 | bytes 2359296 | tf_op jit(solution)/shard_map/expert_slice/pallas_call | solution.py:153
  21.9 1.2 %collective-permute-start.5 = (bf16[32,2048]{1,0:T(8,128)(2,1)S(1)}, bf16[32,2048]{1,0:T(8,128)(2,1)S(1)}, u32[]{:S(2)}, u32[]{:S(2)}) collective-permute-start(bf16[32,2048]{1,0:T(8,128)(2,1)S(1)} %get-tuple-element.23), channel_id=1, source_target_pairs={{0,4},{4,0},{8,12},{12,8},{16,20},{20,16},{24,28},{28,24},{1,5},{5... | collective-permute-start | bytes 393224 | tf_op jit(solution)/shard_map/ppermute | solution.py:220
  23.1 2.1 %collective-permute-done.7 = bf16[32,2048]{1,0:T(8,128)(2,1)S(1)} collective-permute-done((bf16[32,2048]{1,0:T(8,128)(2,1)S(1)}, bf16[32,2048]{1,0:T(8,128)(2,1)S(1)}, u32[]{:S(2)}, u32[]{:S(2)}) %collective-permute-start.7) | collective-permute-done | bytes 131104 | tf_op jit(solution)/shard_map/ppermute | solution.py:220
  25.3 0.7 %collective-permute-start.8 = (bf16[16,2048]{1,0:T(8,128)(2,1)S(1)}, bf16[16,2048]{1,0:T(8,128)(2,1)S(1)}, u32[]{:S(2)}, u32[]{:S(2)}) collective-permute-start(bf16[16,2048]{1,0:T(8,128)(2,1)S(1)} %get-tuple-element.25), channel_id=1, source_target_pairs={{0,16},{4,20},{8,24},{12,28},{16,0},{20,4},{24,8},{28,12},{1,17},{... | collective-permute-start | bytes 196616 | tf_op jit(solution)/shard_map/ppermute | solution.py:220
  26.0 1.0 %collective-permute-start.9 = (bf16[16,2048]{1,0:T(8,128)(2,1)S(1)}, bf16[16,2048]{1,0:T(8,128)(2,1)S(1)}, u32[]{:S(2)}, u32[]{:S(2)}) collective-permute-start(bf16[16,2048]{1,0:T(8,128)(2,1)S(1)} %get-tuple-element.26), channel_id=1, source_target_pairs={{0,24},{4,28},{8,16},{12,20},{16,8},{20,12},{24,0},{28,4},{1,25},{... | collective-permute-start | bytes 196616 | tf_op jit(solution)/shard_map/ppermute | solution.py:220
  27.0 0.0 collective-permute-done.5
  27.1 1.9 %collective-permute-start.6 = (bf16[16,2048]{1,0:T(8,128)(2,1)S(1)}, bf16[16,2048]{1,0:T(8,128)(2,1)S(1)}, u32[]{:S(2)}, u32[]{:S(2)}) collective-permute-start(bf16[16,2048]{1,0:T(8,128)(2,1)S(1)} %get-tuple-element.27), channel_id=1, source_target_pairs={{0,8},{4,12},{8,0},{12,4},{16,24},{20,28},{24,16},{28,20},{1,9},{5... | collective-permute-start | bytes 196616 | tf_op jit(solution)/shard_map/ppermute | solution.py:220
  28.9 1.6 %collective-permute-done.8 = bf16[16,2048]{1,0:T(8,128)(2,1)S(1)} collective-permute-done((bf16[16,2048]{1,0:T(8,128)(2,1)S(1)}, bf16[16,2048]{1,0:T(8,128)(2,1)S(1)}, u32[]{:S(2)}, u32[]{:S(2)}) %collective-permute-start.8) | collective-permute-done | bytes 65568 | tf_op jit(solution)/shard_map/ppermute | solution.py:220
  30.5 1.6 %collective-permute-done.9 = bf16[16,2048]{1,0:T(8,128)(2,1)S(1)} collective-permute-done((bf16[16,2048]{1,0:T(8,128)(2,1)S(1)}, bf16[16,2048]{1,0:T(8,128)(2,1)S(1)}, u32[]{:S(2)}, u32[]{:S(2)}) %collective-permute-start.9) | collective-permute-done | bytes 65568 | tf_op jit(solution)/shard_map/ppermute | solution.py:220
  32.1 0.0 collective-permute-done.6.refs_1_
  32.1 1.1 %combine.1 = bf16[128,2048]{1,0:T(8,128)(2,1)} custom-call(f32[16,128]{1,0:T(8,128)S(1)} %get-tuple-element.17.table_ref, bf16[16,2048]{1,0:T(8,128)(2,1)S(1)} %get-tuple-element.28.refs_0_, bf16[16,2048]{1,0:T(8,128)(2,1)S(1)} %collective-permute-done.6.refs_1_, bf16[16,2048]{1,0:T(8,128)(2,1)S(1)} %add_convert_fusion.refs_2_), custom_call_target="tpu_custom_call" | custom-call | tf_op jit(solution)/shard_map/combine/pallas_call | solution.py:199
  (7 shorter events, 0.1 us)
Async XLA Ops:
  1.4 10.8 %collective-permute-start.1 = (bf16[16,2048]{1,0:T(8,128)(2,1)S(1)}, bf16[16,2048]{1,0:T(8,128)(2,1)S(1)}, u32[]{:S(2)}, u32[]{:S(2)}) collective-permute-start(bf16[16,2048]{1,0:T(8,128)(2,1)S(1)} %get-tuple-element.15.rows_ref), channel_id=1, source_target_pairs={{0,24},{4,28},{8,16},{12,20},{16,8},{20,12},{24,0},{28,4},{1,25},{... | collective-permute-start | bytes 196616 | tf_op jit(solution)/shard_map/ppermute | solution.py:220
  6.5 5.7 %collective-permute-start = (bf16[16,2048]{1,0:T(8,128)(2,1)S(1)}, bf16[16,2048]{1,0:T(8,128)(2,1)S(1)}, u32[]{:S(2)}, u32[]{:S(2)}) collective-permute-start(bf16[16,2048]{1,0:T(8,128)(2,1)S(1)} %get-tuple-element.15.rows_ref), channel_id=1, source_target_pairs={{0,16},{4,20},{8,24},{12,28},{16,0},{20,4},{24,8},{28,12},{1,17},{... | collective-permute-start | bytes 196616 | tf_op jit(solution)/shard_map/ppermute | solution.py:220
  9.0 4.9 %collective-permute-start.2 = (bf16[16,2048]{1,0:T(8,128)(2,1)S(1)}, bf16[16,2048]{1,0:T(8,128)(2,1)S(1)}, u32[]{:S(2)}, u32[]{:S(2)}) collective-permute-start(bf16[16,2048]{1,0:T(8,128)(2,1)S(1)} %get-tuple-element.18), channel_id=1, source_target_pairs={{0,8},{4,12},{8,0},{12,4},{16,24},{20,28},{24,16},{28,20},{1,9},{5... | collective-permute-start | bytes 196616 | tf_op jit(solution)/shard_map/ppermute | solution.py:220
  12.2 6.3 %collective-permute-start.4 = (bf16[32,2048]{1,0:T(8,128)(2,1)S(1)}, bf16[32,2048]{1,0:T(8,128)(2,1)S(1)}, u32[]{:S(2)}, u32[]{:S(2)}) collective-permute-start(bf16[32,2048]{1,0:T(8,128)(2,1)S(1)} %constant_dynamic-update-slice_fusion.refs_0_), channel_id=1, source_target_pairs={{0,4},{4,0},{8,12},{12,8},{16,20},{20,16},{24,28},{28,24},{1,5},{5... | collective-permute-start | bytes 393224 | tf_op jit(solution)/shard_map/ppermute | solution.py:220
  13.8 7.3 %collective-permute-start.3 = (bf16[32,2048]{1,0:T(8,128)(2,1)S(1)}, bf16[32,2048]{1,0:T(8,128)(2,1)S(1)}, u32[]{:S(2)}, u32[]{:S(2)}) collective-permute-start(bf16[32,2048]{1,0:T(8,128)(2,1)S(1)} %constant_dynamic-update-slice_fusion.2.refs_1_), channel_id=1, source_target_pairs={{0,4},{4,0},{8,12},{12,8},{16,20},{20,16},{24,28},{28,24},{1,5},{5... | collective-permute-start | bytes 393224 | tf_op jit(solution)/shard_map/ppermute | solution.py:220
  19.4 5.9 %collective-permute-start.7 = (bf16[32,2048]{1,0:T(8,128)(2,1)S(1)}, bf16[32,2048]{1,0:T(8,128)(2,1)S(1)}, u32[]{:S(2)}, u32[]{:S(2)}) collective-permute-start(bf16[32,2048]{1,0:T(8,128)(2,1)S(1)} %expert_slice.2.refs_6_), channel_id=1, source_target_pairs={{0,4},{4,0},{8,12},{12,8},{16,20},{20,16},{24,28},{28,24},{1,5},{5... | collective-permute-start | bytes 393224 | tf_op jit(solution)/shard_map/ppermute | solution.py:220
  21.9 5.1 %collective-permute-start.5 = (bf16[32,2048]{1,0:T(8,128)(2,1)S(1)}, bf16[32,2048]{1,0:T(8,128)(2,1)S(1)}, u32[]{:S(2)}, u32[]{:S(2)}) collective-permute-start(bf16[32,2048]{1,0:T(8,128)(2,1)S(1)} %get-tuple-element.23), channel_id=1, source_target_pairs={{0,4},{4,0},{8,12},{12,8},{16,20},{20,16},{24,28},{28,24},{1,5},{5... | collective-permute-start | bytes 393224 | tf_op jit(solution)/shard_map/ppermute | solution.py:220
  25.3 5.2 %collective-permute-start.8 = (bf16[16,2048]{1,0:T(8,128)(2,1)S(1)}, bf16[16,2048]{1,0:T(8,128)(2,1)S(1)}, u32[]{:S(2)}, u32[]{:S(2)}) collective-permute-start(bf16[16,2048]{1,0:T(8,128)(2,1)S(1)} %get-tuple-element.25), channel_id=1, source_target_pairs={{0,16},{4,20},{8,24},{12,28},{16,0},{20,4},{24,8},{28,12},{1,17},{... | collective-permute-start | bytes 196616 | tf_op jit(solution)/shard_map/ppermute | solution.py:220
  26.0 6.1 %collective-permute-start.9 = (bf16[16,2048]{1,0:T(8,128)(2,1)S(1)}, bf16[16,2048]{1,0:T(8,128)(2,1)S(1)}, u32[]{:S(2)}, u32[]{:S(2)}) collective-permute-start(bf16[16,2048]{1,0:T(8,128)(2,1)S(1)} %get-tuple-element.26), channel_id=1, source_target_pairs={{0,24},{4,28},{8,16},{12,20},{16,8},{20,12},{24,0},{28,4},{1,25},{... | collective-permute-start | bytes 196616 | tf_op jit(solution)/shard_map/ppermute | solution.py:220
  27.1 5.1 %collective-permute-start.6 = (bf16[16,2048]{1,0:T(8,128)(2,1)S(1)}, bf16[16,2048]{1,0:T(8,128)(2,1)S(1)}, u32[]{:S(2)}, u32[]{:S(2)}) collective-permute-start(bf16[16,2048]{1,0:T(8,128)(2,1)S(1)} %get-tuple-element.27), channel_id=1, source_target_pairs={{0,8},{4,12},{8,0},{12,4},{16,24},{20,28},{24,16},{28,20},{1,9},{5... | collective-permute-start | bytes 196616 | tf_op jit(solution)/shard_map/ppermute | solution.py:220

commit v12 on v11

--- a/solution.py
+++ b/solution.py
@@ -120,7 +120,12 @@
         copy.start()
     rows_out[...] = rows_ref[...]
     token = lax.broadcasted_iota(jnp.int32, table_ref.shape, 1)
-    table_out[...] = jnp.where(token < live_ref[0], table_ref[...], 0.0)
+    table = jnp.where(token < live_ref[0], table_ref[...], 0.0)
+    pieces = []
+    for _ in range(3):
+        pieces.append(table.astype(jnp.bfloat16).astype(jnp.float32))
+        table = table - pieces[-1]
+    table_out[...] = jnp.concatenate(pieces, axis=0).T.astype(jnp.bfloat16)
     for copy in copies:
         copy.wait()
 
@@ -128,10 +133,13 @@
 def stage_weights(live_counts, rows, table, weights):
     vmem = pl.BlockSpec(memory_space=pltpu.VMEM)
     hbm = pl.BlockSpec(memory_space=pltpu.HBM)
-    arrays = (rows, table, *weights)
+    table_shape = (table.shape[1], 3 * table.shape[0])
     rows, table, *weights = pl.pallas_call(
         stage_kernel,
-        out_shape=[jax.ShapeDtypeStruct(array.shape, array.dtype) for array in arrays],
+        out_shape=[
+            jax.ShapeDtypeStruct(shape, jnp.bfloat16)
+            for shape in (rows.shape, table_shape, *(weight.shape for weight in weights))
+        ],
         in_specs=[pl.BlockSpec(memory_space=pltpu.SMEM), vmem, vmem] + [hbm] * 3,
         out_specs=[vmem] * 5,
         scratch_shapes=[pltpu.SemaphoreType.DMA((3, WEIGHT_CHUNKS))],
@@ -167,24 +175,18 @@
 
 def combine_kernel(table_ref, *refs):
     *parts, out_hbm, out_ref, sems = refs
-    table = table_ref[...]
-    pieces = []
-    for _ in range(3):
-        pieces.append(table.astype(jnp.bfloat16))
-        table = table - pieces[-1].astype(jnp.float32)
-    pieces = jnp.concatenate(pieces, axis=0)
     features = out_ref.shape[1]
     width = features // 4
     copies = []
     for i in range(4):
         columns = pl.ds(i * width, width)
         summed = functools.reduce(add_level, [part[:, columns] for part in parts])
-        out_ref[:, columns] = lax.dot_general(
-            pieces,
+        result = jnp.dot(
+            table_ref[...],
             jnp.concatenate([summed] * 3, axis=0),
-            (((0,), (0,)), ((), ())),
             preferred_element_type=jnp.float32,
-        ).astype(jnp.bfloat16)
+        )
+        out_ref[:, columns] = result.astype(jnp.bfloat16)
         copies.append(
             pltpu.make_async_copy(out_ref.at[:, columns], out_hbm.at[:, columns], sems.at[i])
         )
@@ -195,7 +197,7 @@
 
 def combine(table, parts):
     vmem = pl.BlockSpec(memory_space=pltpu.VMEM)
-    shape = (table.shape[1], parts[0].shape[1])
+    shape = (table.shape[0], parts[0].shape[1])
     return pl.pallas_call(
         combine_kernel,
         out_shape=jax.ShapeDtypeStruct(shape, jnp.bfloat16),

time: 33.3 us -> 33.3 us (level)
  no operation moved by 1% of the time
where the time goes in v12:
time: 33.3 us; the launch traced here: 33.1 us
  starting transfers between devices  15.1 us (45%)
  waiting for transfers between devices  11.4 us (34%)
  Pallas kernels  5.84 us (18%)
  between operations  0.72 us (2%)
    ppermute x10, starting transfers between devices, swap(): lax.ppermute(block, 'ep', [(i, i ^ distance) for i in range(devices)])  15.1 us
    ppermute x10, waiting for transfers between devices, swap(): lax.ppermute(block, 'ep', [(i, i ^ distance) for i in range(devices)])  11.4 us
    pallas_call x1, Pallas kernels, stage_weights(): pl.pallas_call(stage_kernel, out_shape=[jax.ShapeDtypeStruct(shape, jnp.b...  1.8 us
    pallas_call x2, Pallas kernels, expert_slice(): pl.pallas_call(functools.partial(slice_kernel, count), out_shape=[jax.Sha...  1.66 us
    pallas_call x1, Pallas kernels, pick_rows(): pl.pallas_call(pick_kernel, out_shape=(jax.ShapeDtypeStruct((slots, token...  1.37 us
    pallas_call x1, Pallas kernels, combine(): pl.pallas_call(combine_kernel, out_shape=jax.ShapeDtypeStruct(shape, jnp....  1 us
  transfers between devices with their start and end apart: 10, of which 5 were waited for; matrix products, arithmetic and copies ran while one was open for 0% of the time, Pallas kernels for 10%

profile of v12, /device:TPU:0, one launch (start us, length us, event | category | flops | bytes accessed | tf_op | source)
XLA Modules:
  0.0 33.1 jit_solution(18005529309980486510)
XLA Ops:
  0.0 1.4 %pick_rows.1 = (bf16[16,2048]{1,0:T(8,128)(2,1)S(1)}, f32[16,128]{1,0:T(8,128)S(1)}) custom-call(s32[8,128]{1,0:T(8,128)} %bitcast.8, f32[8,128]{1,0:T(8,128)} %bitcast.9, bf16[128,2048]{1,0:T(8,128)(2,1)} %tokens_hbm.1, f32[1,2048]{1,0:T(1,128)} %bitcast.7), custom_call_target="tpu_custom_call" | custom-call | tf_op jit(solution)/shard_map/pick_rows/pallas_call | solution.py:58
  1.4 5.1 %collective-permute-start.1 = (bf16[16,2048]{1,0:T(8,128)(2,1)S(1)}, bf16[16,2048]{1,0:T(8,128)(2,1)S(1)}, u32[]{:S(2)}, u32[]{:S(2)}) collective-permute-start(bf16[16,2048]{1,0:T(8,128)(2,1)S(1)} %get-tuple-element.15.rows_ref), channel_id=1, source_target_pairs={{0,24},{4,28},{8,16},{12,20},{16,8},{20,12},{24,0},{28,4},{1,25},{... | collective-permute-start | bytes 196616 | tf_op jit(solution)/shard_map/ppermute | solution.py:222
  6.5 0.0 collective-permute-start
  7.1 1.8 %stage_weights.1 = (bf16[16,2048]{1,0:T(8,128)(2,1)S(1)}, bf16[128,48]{1,0:T(8,128)(2,1)S(1)}, bf16[192,2048]{1,0:T(8,128)(2,1)S(1)}, bf16[192,2048]{1,0:T(8,128)(2,1)S(1)}, bf16[192,2048]{1,0:T(8,128)(2,1)S(1)}) custom-call(s32[1]{0:T(128)S(6)} %copy.11.live_ref, bf16[16,2048]{1,0:T(8,128)(2,1)S(1)} %get-tuple-element.15.rows_ref, ...), custom_call_target="tpu_custom_call" | custom-call | flops 37748736 | bytes 2359296 | tf_op jit(solution)/shard_map/stage_weights/pallas_call | solution.py:137
  9.0 0.7 %collective-permute-start.2 = (bf16[16,2048]{1,0:T(8,128)(2,1)S(1)}, bf16[16,2048]{1,0:T(8,128)(2,1)S(1)}, u32[]{:S(2)}, u32[]{:S(2)}) collective-permute-start(bf16[16,2048]{1,0:T(8,128)(2,1)S(1)} %get-tuple-element.18), channel_id=1, source_target_pairs={{0,8},{4,12},{8,0},{12,4},{16,24},{20,28},{24,16},{28,20},{1,9},{5... | collective-permute-start | bytes 196616 | tf_op jit(solution)/shard_map/ppermute | solution.py:222
  9.7 2.5 %collective-permute-done = bf16[16,2048]{1,0:T(8,128)(2,1)S(1)} collective-permute-done((bf16[16,2048]{1,0:T(8,128)(2,1)S(1)}, bf16[16,2048]{1,0:T(8,128)(2,1)S(1)}, u32[]{:S(2)}, u32[]{:S(2)}) %collective-permute-start) | collective-permute-done | bytes 65568 | tf_op jit(solution)/shard_map/ppermute | solution.py:222
  12.2 0.0 collective-permute-done.1
  12.2 1.6 %collective-permute-start.4 = (bf16[32,2048]{1,0:T(8,128)(2,1)S(1)}, bf16[32,2048]{1,0:T(8,128)(2,1)S(1)}, u32[]{:S(2)}, u32[]{:S(2)}) collective-permute-start(bf16[32,2048]{1,0:T(8,128)(2,1)S(1)} %constant_dynamic-update-slice_fusion.refs_0_), channel_id=1, source_target_pairs={{0,4},{4,0},{8,12},{12,8},{16,20},{20,16},{24,28},{28,24},{1,5},{5... | collective-permute-start | bytes 393224 | tf_op jit(solution)/shard_map/ppermute | solution.py:222
  13.8 0.0 collective-permute-done.2
  13.8 1.2 %collective-permute-start.3 = (bf16[32,2048]{1,0:T(8,128)(2,1)S(1)}, bf16[32,2048]{1,0:T(8,128)(2,1)S(1)}, u32[]{:S(2)}, u32[]{:S(2)}) collective-permute-start(bf16[32,2048]{1,0:T(8,128)(2,1)S(1)} %constant_dynamic-update-slice_fusion.2.refs_1_), channel_id=1, source_target_pairs={{0,4},{4,0},{8,12},{12,8},{16,20},{20,16},{24,28},{28,24},{1,5},{5... | collective-permute-start | bytes 393224 | tf_op jit(solution)/shard_map/ppermute | solution.py:222
  15.0 3.5 %collective-permute-done.4.refs_0_ = bf16[32,2048]{1,0:T(8,128)(2,1)S(1)} collective-permute-done((bf16[32,2048]{1,0:T(8,128)(2,1)S(1)}, bf16[32,2048]{1,0:T(8,128)(2,1)S(1)}, u32[]{:S(2)}, u32[]{:S(2)}) %collective-permute-start.4) | collective-permute-done | bytes 131104 | tf_op jit(solution)/shard_map/ppermute | solution.py:222
  18.6 0.8 %expert_slice.2.refs_6_ = bf16[32,2048]{1,0:T(8,128)(2,1)S(1)} custom-call(bf16[32,2048]{1,0:T(8,128)(2,1)S(1)} %collective-permute-done.4.refs_0_, bf16[192,2048]{1,0:T(8,128)(2,1)S(1)} %get-tuple-element.19.refs_1_.refs_3_, bf16[192,2048]{1,0:T(8,128)(2,1)S(1)} %get-tuple-element.20.refs_2_.refs_4_, bf16[192,2048]{1,0:T(8,128)(2,1)S(1)} %get-tuple-element.21.refs_3_.refs_5_), custom_call_target="tpu_custom_call" | custom-call | flops 75497472 | bytes 2359296 | tf_op jit(solution)/shard_map/expert_slice/pallas_call | solution.py:161
  19.4 1.7 %collective-permute-start.7 = (bf16[32,2048]{1,0:T(8,128)(2,1)S(1)}, bf16[32,2048]{1,0:T(8,128)(2,1)S(1)}, u32[]{:S(2)}, u32[]{:S(2)}) collective-permute-start(bf16[32,2048]{1,0:T(8,128)(2,1)S(1)} %expert_slice.2.refs_6_), channel_id=1, source_target_pairs={{0,4},{4,0},{8,12},{12,8},{16,20},{20,16},{24,28},{28,24},{1,5},{5... | collective-permute-start | bytes 393224 | tf_op jit(solution)/shard_map/ppermute | solution.py:222
  21.1 0.0 collective-permute-done.3.refs_2_
  21.1 0.9 %expert_slice.3 = (bf16[32,2048]{1,0:T(8,128)(2,1)S(1)}, bf16[32,2048]{1,0:T(8,128)(2,1)S(1)}, bf16[32,2048]{1,0:T(8,128)(2,1)S(1)}) custom-call(bf16[32,2048]{1,0:T(8,128)(2,1)S(1)} %constant_dynamic-update-slice_fusion.refs_0_, bf16[32,2048]{1,0:T(8,128)(2,1)S(1)} %constant_dynamic-update-slice_fusion.2.refs_1_, ...), custom_call_target="tpu_custom_call" | custom-call | flops 226492416 | bytes 2359296 | tf_op jit(solution)/shard_map/expert_slice/pallas_call | solution.py:161
  21.9 1.2 %collective-permute-start.5 = (bf16[32,2048]{1,0:T(8,128)(2,1)S(1)}, bf16[32,2048]{1,0:T(8,128)(2,1)S(1)}, u32[]{:S(2)}, u32[]{:S(2)}) collective-permute-start(bf16[32,2048]{1,0:T(8,128)(2,1)S(1)} %get-tuple-element.23), channel_id=1, source_target_pairs={{0,4},{4,0},{8,12},{12,8},{16,20},{20,16},{24,28},{28,24},{1,5},{5... | collective-permute-start | bytes 393224 | tf_op jit(solution)/shard_map/ppermute | solution.py:222
  23.1 2.1 %collective-permute-done.7 = bf16[32,2048]{1,0:T(8,128)(2,1)S(1)} collective-permute-done((bf16[32,2048]{1,0:T(8,128)(2,1)S(1)}, bf16[32,2048]{1,0:T(8,128)(2,1)S(1)}, u32[]{:S(2)}, u32[]{:S(2)}) %collective-permute-start.7) | collective-permute-done | bytes 131104 | tf_op jit(solution)/shard_map/ppermute | solution.py:222
  25.3 0.7 %collective-permute-start.8 = (bf16[16,2048]{1,0:T(8,128)(2,1)S(1)}, bf16[16,2048]{1,0:T(8,128)(2,1)S(1)}, u32[]{:S(2)}, u32[]{:S(2)}) collective-permute-start(bf16[16,2048]{1,0:T(8,128)(2,1)S(1)} %get-tuple-element.25), channel_id=1, source_target_pairs={{0,16},{4,20},{8,24},{12,28},{16,0},{20,4},{24,8},{28,12},{1,17},{... | collective-permute-start | bytes 196616 | tf_op jit(solution)/shard_map/ppermute | solution.py:222
  26.0 1.0 %collective-permute-start.9 = (bf16[16,2048]{1,0:T(8,128)(2,1)S(1)}, bf16[16,2048]{1,0:T(8,128)(2,1)S(1)}, u32[]{:S(2)}, u32[]{:S(2)}) collective-permute-start(bf16[16,2048]{1,0:T(8,128)(2,1)S(1)} %get-tuple-element.26), channel_id=1, source_target_pairs={{0,24},{4,28},{8,16},{12,20},{16,8},{20,12},{24,0},{28,4},{1,25},{... | collective-permute-start | bytes 196616 | tf_op jit(solution)/shard_map/ppermute | solution.py:222
  27.0 0.0 collective-permute-done.5
  27.1 1.9 %collective-permute-start.6 = (bf16[16,2048]{1,0:T(8,128)(2,1)S(1)}, bf16[16,2048]{1,0:T(8,128)(2,1)S(1)}, u32[]{:S(2)}, u32[]{:S(2)}) collective-permute-start(bf16[16,2048]{1,0:T(8,128)(2,1)S(1)} %get-tuple-element.27), channel_id=1, source_target_pairs={{0,8},{4,12},{8,0},{12,4},{16,24},{20,28},{24,16},{28,20},{1,9},{5... | collective-permute-start | bytes 196616 | tf_op jit(solution)/shard_map/ppermute | solution.py:222
  28.9 1.6 %collective-permute-done.8 = bf16[16,2048]{1,0:T(8,128)(2,1)S(1)} collective-permute-done((bf16[16,2048]{1,0:T(8,128)(2,1)S(1)}, bf16[16,2048]{1,0:T(8,128)(2,1)S(1)}, u32[]{:S(2)}, u32[]{:S(2)}) %collective-permute-start.8) | collective-permute-done | bytes 65568 | tf_op jit(solution)/shard_map/ppermute | solution.py:222
  30.5 1.6 %collective-permute-done.9 = bf16[16,2048]{1,0:T(8,128)(2,1)S(1)} collective-permute-done((bf16[16,2048]{1,0:T(8,128)(2,1)S(1)}, bf16[16,2048]{1,0:T(8,128)(2,1)S(1)}, u32[]{:S(2)}, u32[]{:S(2)}) %collective-permute-start.9) | collective-permute-done | bytes 65568 | tf_op jit(solution)/shard_map/ppermute | solution.py:222
  32.1 0.0 collective-permute-done.6.refs_1_
  32.1 1.0 %combine.1 = bf16[128,2048]{1,0:T(8,128)(2,1)} custom-call(bf16[128,48]{1,0:T(8,128)(2,1)S(1)} %get-tuple-element.17.table_ref, bf16[16,2048]{1,0:T(8,128)(2,1)S(1)} %get-tuple-element.28.refs_0_, bf16[16,2048]{1,0:T(8,128)(2,1)S(1)} %collective-permute-done.6.refs_1_, bf16[16,2048]{1,0:T(8,128)(2,1)S(1)} %add_convert_fusion.refs_2_), custom_call_target="tpu_custom_call" | custom-call | tf_op jit(solution)/shard_map/combine/pallas_call | solution.py:201
  (7 shorter events, 0.1 us)
Async XLA Ops:
  1.4 10.8 %collective-permute-start.1 = (bf16[16,2048]{1,0:T(8,128)(2,1)S(1)}, bf16[16,2048]{1,0:T(8,128)(2,1)S(1)}, u32[]{:S(2)}, u32[]{:S(2)}) collective-permute-start(bf16[16,2048]{1,0:T(8,128)(2,1)S(1)} %get-tuple-element.15.rows_ref), channel_id=1, source_target_pairs={{0,24},{4,28},{8,16},{12,20},{16,8},{20,12},{24,0},{28,4},{1,25},{... | collective-permute-start | bytes 196616 | tf_op jit(solution)/shard_map/ppermute | solution.py:222
  6.5 5.7 %collective-permute-start = (bf16[16,2048]{1,0:T(8,128)(2,1)S(1)}, bf16[16,2048]{1,0:T(8,128)(2,1)S(1)}, u32[]{:S(2)}, u32[]{:S(2)}) collective-permute-start(bf16[16,2048]{1,0:T(8,128)(2,1)S(1)} %get-tuple-element.15.rows_ref), channel_id=1, source_target_pairs={{0,16},{4,20},{8,24},{12,28},{16,0},{20,4},{24,8},{28,12},{1,17},{... | collective-permute-start | bytes 196616 | tf_op jit(solution)/shard_map/ppermute | solution.py:222
  9.0 4.9 %collective-permute-start.2 = (bf16[16,2048]{1,0:T(8,128)(2,1)S(1)}, bf16[16,2048]{1,0:T(8,128)(2,1)S(1)}, u32[]{:S(2)}, u32[]{:S(2)}) collective-permute-start(bf16[16,2048]{1,0:T(8,128)(2,1)S(1)} %get-tuple-element.18), channel_id=1, source_target_pairs={{0,8},{4,12},{8,0},{12,4},{16,24},{20,28},{24,16},{28,20},{1,9},{5... | collective-permute-start | bytes 196616 | tf_op jit(solution)/shard_map/ppermute | solution.py:222
  12.2 6.3 %collective-permute-start.4 = (bf16[32,2048]{1,0:T(8,128)(2,1)S(1)}, bf16[32,2048]{1,0:T(8,128)(2,1)S(1)}, u32[]{:S(2)}, u32[]{:S(2)}) collective-permute-start(bf16[32,2048]{1,0:T(8,128)(2,1)S(1)} %constant_dynamic-update-slice_fusion.refs_0_), channel_id=1, source_target_pairs={{0,4},{4,0},{8,12},{12,8},{16,20},{20,16},{24,28},{28,24},{1,5},{5... | collective-permute-start | bytes 393224 | tf_op jit(solution)/shard_map/ppermute | solution.py:222
  13.8 7.3 %collective-permute-start.3 = (bf16[32,2048]{1,0:T(8,128)(2,1)S(1)}, bf16[32,2048]{1,0:T(8,128)(2,1)S(1)}, u32[]{:S(2)}, u32[]{:S(2)}) collective-permute-start(bf16[32,2048]{1,0:T(8,128)(2,1)S(1)} %constant_dynamic-update-slice_fusion.2.refs_1_), channel_id=1, source_target_pairs={{0,4},{4,0},{8,12},{12,8},{16,20},{20,16},{24,28},{28,24},{1,5},{5... | collective-permute-start | bytes 393224 | tf_op jit(solution)/shard_map/ppermute | solution.py:222
  19.4 5.9 %collective-permute-start.7 = (bf16[32,2048]{1,0:T(8,128)(2,1)S(1)}, bf16[32,2048]{1,0:T(8,128)(2,1)S(1)}, u32[]{:S(2)}, u32[]{:S(2)}) collective-permute-start(bf16[32,2048]{1,0:T(8,128)(2,1)S(1)} %expert_slice.2.refs_6_), channel_id=1, source_target_pairs={{0,4},{4,0},{8,12},{12,8},{16,20},{20,16},{24,28},{28,24},{1,5},{5... | collective-permute-start | bytes 393224 | tf_op jit(solution)/shard_map/ppermute | solution.py:222
  21.9 5.1 %collective-permute-start.5 = (bf16[32,2048]{1,0:T(8,128)(2,1)S(1)}, bf16[32,2048]{1,0:T(8,128)(2,1)S(1)}, u32[]{:S(2)}, u32[]{:S(2)}) collective-permute-start(bf16[32,2048]{1,0:T(8,128)(2,1)S(1)} %get-tuple-element.23), channel_id=1, source_target_pairs={{0,4},{4,0},{8,12},{12,8},{16,20},{20,16},{24,28},{28,24},{1,5},{5... | collective-permute-start | bytes 393224 | tf_op jit(solution)/shard_map/ppermute | solution.py:222
  25.3 5.2 %collective-permute-start.8 = (bf16[16,2048]{1,0:T(8,128)(2,1)S(1)}, bf16[16,2048]{1,0:T(8,128)(2,1)S(1)}, u32[]{:S(2)}, u32[]{:S(2)}) collective-permute-start(bf16[16,2048]{1,0:T(8,128)(2,1)S(1)} %get-tuple-element.25), channel_id=1, source_target_pairs={{0,16},{4,20},{8,24},{12,28},{16,0},{20,4},{24,8},{28,12},{1,17},{... | collective-permute-start | bytes 196616 | tf_op jit(solution)/shard_map/ppermute | solution.py:222
  26.0 6.1 %collective-permute-start.9 = (bf16[16,2048]{1,0:T(8,128)(2,1)S(1)}, bf16[16,2048]{1,0:T(8,128)(2,1)S(1)}, u32[]{:S(2)}, u32[]{:S(2)}) collective-permute-start(bf16[16,2048]{1,0:T(8,128)(2,1)S(1)} %get-tuple-element.26), channel_id=1, source_target_pairs={{0,24},{4,28},{8,16},{12,20},{16,8},{20,12},{24,0},{28,4},{1,25},{... | collective-permute-start | bytes 196616 | tf_op jit(solution)/shard_map/ppermute | solution.py:222
  27.1 5.1 %collective-permute-start.6 = (bf16[16,2048]{1,0:T(8,128)(2,1)S(1)}, bf16[16,2048]{1,0:T(8,128)(2,1)S(1)}, u32[]{:S(2)}, u32[]{:S(2)}) collective-permute-start(bf16[16,2048]{1,0:T(8,128)(2,1)S(1)} %get-tuple-element.27), channel_id=1, source_target_pairs={{0,8},{4,12},{8,0},{12,4},{16,24},{20,28},{24,16},{28,20},{1,9},{5... | collective-permute-start | bytes 196616 | tf_op jit(solution)/shard_map/ppermute | solution.py:222

commit v13 on v12

--- a/solution.py
+++ b/solution.py
@@ -76,11 +76,11 @@
 
 
 def expert_rows(rows, gate_ref, up_ref, down_ref):
-    dims = (((1,), (1,)), ((), ()))
-    gate_act = lax.dot_general(rows, gate_ref[...], dims, preferred_element_type=jnp.float32)
-    up_act = lax.dot_general(rows, up_ref[...], dims, preferred_element_type=jnp.float32)
+    across, down = (((1,), (1,)), ((), ())), (((0,), (0,)), ((), ()))
+    gate_act = lax.dot_general(gate_ref[...], rows, across, preferred_element_type=jnp.float32)
+    up_act = lax.dot_general(up_ref[...], rows, across, preferred_element_type=jnp.float32)
     hidden = (jax.nn.silu(gate_act) * up_act).astype(jnp.bfloat16)
-    partial_out = jnp.dot(hidden, down_ref[...], preferred_element_type=jnp.float32)
+    partial_out = lax.dot_general(hidden, down_ref[...], down, preferred_element_type=jnp.float32)
     return partial_out.astype(jnp.bfloat16)
 
 

time: 33.3 us -> 33.3 us (level)
  no operation moved by 1% of the time
where the time goes in v13:
time: 33.3 us; the launch traced here: 33.1 us
  starting transfers between devices  15.1 us (45%)
  waiting for transfers between devices  11.4 us (34%)
  Pallas kernels  5.84 us (18%)
  between operations  0.72 us (2%)
    ppermute x10, starting transfers between devices, swap(): lax.ppermute(block, 'ep', [(i, i ^ distance) for i in range(devices)])  15.1 us
    ppermute x10, waiting for transfers between devices, swap(): lax.ppermute(block, 'ep', [(i, i ^ distance) for i in range(devices)])  11.4 us
    pallas_call x1, Pallas kernels, stage_weights(): pl.pallas_call(stage_kernel, out_shape=[jax.ShapeDtypeStruct(shape, jnp.b...  1.8 us
    pallas_call x2, Pallas kernels, expert_slice(): pl.pallas_call(functools.partial(slice_kernel, count), out_shape=[jax.Sha...  1.66 us
    pallas_call x1, Pallas kernels, pick_rows(): pl.pallas_call(pick_kernel, out_shape=(jax.ShapeDtypeStruct((slots, token...  1.37 us
    pallas_call x1, Pallas kernels, combine(): pl.pallas_call(combine_kernel, out_shape=jax.ShapeDtypeStruct(shape, jnp....  1 us
  transfers between devices with their start and end apart: 10, of which 5 were waited for; matrix products, arithmetic and copies ran while one was open for 0% of the time, Pallas kernels for 10%

profile of v13, /device:TPU:0, one launch (start us, length us, event | category | flops | bytes accessed | tf_op | source)
XLA Modules:
  0.0 33.1 jit_solution(15250699632832623810)
XLA Ops:
  0.0 1.4 %pick_rows.1 = (bf16[16,2048]{1,0:T(8,128)(2,1)S(1)}, f32[16,128]{1,0:T(8,128)S(1)}) custom-call(s32[8,128]{1,0:T(8,128)} %bitcast.8, f32[8,128]{1,0:T(8,128)} %bitcast.9, bf16[128,2048]{1,0:T(8,128)(2,1)} %tokens_hbm.1, f32[1,2048]{1,0:T(1,128)} %bitcast.7), custom_call_target="tpu_custom_call" | custom-call | tf_op jit(solution)/shard_map/pick_rows/pallas_call | solution.py:58
  1.4 5.1 %collective-permute-start.1 = (bf16[16,2048]{1,0:T(8,128)(2,1)S(1)}, bf16[16,2048]{1,0:T(8,128)(2,1)S(1)}, u32[]{:S(2)}, u32[]{:S(2)}) collective-permute-start(bf16[16,2048]{1,0:T(8,128)(2,1)S(1)} %get-tuple-element.15.rows_ref), channel_id=1, source_target_pairs={{0,24},{4,28},{8,16},{12,20},{16,8},{20,12},{24,0},{28,4},{1,25},{... | collective-permute-start | bytes 196616 | tf_op jit(solution)/shard_map/ppermute | solution.py:222
  6.5 0.0 collective-permute-start
  7.1 1.8 %stage_weights.1 = (bf16[16,2048]{1,0:T(8,128)(2,1)S(1)}, bf16[128,48]{1,0:T(8,128)(2,1)S(1)}, bf16[192,2048]{1,0:T(8,128)(2,1)S(1)}, bf16[192,2048]{1,0:T(8,128)(2,1)S(1)}, bf16[192,2048]{1,0:T(8,128)(2,1)S(1)}) custom-call(s32[1]{0:T(128)S(6)} %copy.11.live_ref, bf16[16,2048]{1,0:T(8,128)(2,1)S(1)} %get-tuple-element.15.rows_ref, ...), custom_call_target="tpu_custom_call" | custom-call | flops 37748736 | bytes 2359296 | tf_op jit(solution)/shard_map/stage_weights/pallas_call | solution.py:137
  9.0 0.7 %collective-permute-start.2 = (bf16[16,2048]{1,0:T(8,128)(2,1)S(1)}, bf16[16,2048]{1,0:T(8,128)(2,1)S(1)}, u32[]{:S(2)}, u32[]{:S(2)}) collective-permute-start(bf16[16,2048]{1,0:T(8,128)(2,1)S(1)} %get-tuple-element.18), channel_id=1, source_target_pairs={{0,8},{4,12},{8,0},{12,4},{16,24},{20,28},{24,16},{28,20},{1,9},{5... | collective-permute-start | bytes 196616 | tf_op jit(solution)/shard_map/ppermute | solution.py:222
  9.7 2.5 %collective-permute-done = bf16[16,2048]{1,0:T(8,128)(2,1)S(1)} collective-permute-done((bf16[16,2048]{1,0:T(8,128)(2,1)S(1)}, bf16[16,2048]{1,0:T(8,128)(2,1)S(1)}, u32[]{:S(2)}, u32[]{:S(2)}) %collective-permute-start) | collective-permute-done | bytes 65568 | tf_op jit(solution)/shard_map/ppermute | solution.py:222
  12.2 0.0 collective-permute-done.1
  12.2 1.6 %collective-permute-start.4 = (bf16[32,2048]{1,0:T(8,128)(2,1)S(1)}, bf16[32,2048]{1,0:T(8,128)(2,1)S(1)}, u32[]{:S(2)}, u32[]{:S(2)}) collective-permute-start(bf16[32,2048]{1,0:T(8,128)(2,1)S(1)} %constant_dynamic-update-slice_fusion.refs_0_), channel_id=1, source_target_pairs={{0,4},{4,0},{8,12},{12,8},{16,20},{20,16},{24,28},{28,24},{1,5},{5... | collective-permute-start | bytes 393224 | tf_op jit(solution)/shard_map/ppermute | solution.py:222
  13.8 0.0 collective-permute-done.2
  13.8 1.2 %collective-permute-start.3 = (bf16[32,2048]{1,0:T(8,128)(2,1)S(1)}, bf16[32,2048]{1,0:T(8,128)(2,1)S(1)}, u32[]{:S(2)}, u32[]{:S(2)}) collective-permute-start(bf16[32,2048]{1,0:T(8,128)(2,1)S(1)} %constant_dynamic-update-slice_fusion.2.refs_1_), channel_id=1, source_target_pairs={{0,4},{4,0},{8,12},{12,8},{16,20},{20,16},{24,28},{28,24},{1,5},{5... | collective-permute-start | bytes 393224 | tf_op jit(solution)/shard_map/ppermute | solution.py:222
  15.0 3.5 %collective-permute-done.4.refs_0_ = bf16[32,2048]{1,0:T(8,128)(2,1)S(1)} collective-permute-done((bf16[32,2048]{1,0:T(8,128)(2,1)S(1)}, bf16[32,2048]{1,0:T(8,128)(2,1)S(1)}, u32[]{:S(2)}, u32[]{:S(2)}) %collective-permute-start.4) | collective-permute-done | bytes 131104 | tf_op jit(solution)/shard_map/ppermute | solution.py:222
  18.6 0.8 %expert_slice.2.refs_6_ = bf16[32,2048]{1,0:T(8,128)(2,1)S(1)} custom-call(bf16[32,2048]{1,0:T(8,128)(2,1)S(1)} %collective-permute-done.4.refs_0_, bf16[192,2048]{1,0:T(8,128)(2,1)S(1)} %get-tuple-element.19.refs_1_.refs_3_, bf16[192,2048]{1,0:T(8,128)(2,1)S(1)} %get-tuple-element.20.refs_2_.refs_4_, bf16[192,2048]{1,0:T(8,128)(2,1)S(1)} %get-tuple-element.21.refs_3_.refs_5_), custom_call_target="tpu_custom_call" | custom-call | flops 75497472 | bytes 2359296 | tf_op jit(solution)/shard_map/expert_slice/pallas_call | solution.py:161
  19.4 1.7 %collective-permute-start.7 = (bf16[32,2048]{1,0:T(8,128)(2,1)S(1)}, bf16[32,2048]{1,0:T(8,128)(2,1)S(1)}, u32[]{:S(2)}, u32[]{:S(2)}) collective-permute-start(bf16[32,2048]{1,0:T(8,128)(2,1)S(1)} %expert_slice.2.refs_6_), channel_id=1, source_target_pairs={{0,4},{4,0},{8,12},{12,8},{16,20},{20,16},{24,28},{28,24},{1,5},{5... | collective-permute-start | bytes 393224 | tf_op jit(solution)/shard_map/ppermute | solution.py:222
  21.1 0.0 collective-permute-done.3.refs_2_
  21.1 0.9 %expert_slice.3 = (bf16[32,2048]{1,0:T(8,128)(2,1)S(1)}, bf16[32,2048]{1,0:T(8,128)(2,1)S(1)}, bf16[32,2048]{1,0:T(8,128)(2,1)S(1)}) custom-call(bf16[32,2048]{1,0:T(8,128)(2,1)S(1)} %constant_dynamic-update-slice_fusion.refs_0_, bf16[32,2048]{1,0:T(8,128)(2,1)S(1)} %constant_dynamic-update-slice_fusion.2.refs_1_, ...), custom_call_target="tpu_custom_call" | custom-call | flops 226492416 | bytes 2359296 | tf_op jit(solution)/shard_map/expert_slice/pallas_call | solution.py:161
  21.9 1.2 %collective-permute-start.5 = (bf16[32,2048]{1,0:T(8,128)(2,1)S(1)}, bf16[32,2048]{1,0:T(8,128)(2,1)S(1)}, u32[]{:S(2)}, u32[]{:S(2)}) collective-permute-start(bf16[32,2048]{1,0:T(8,128)(2,1)S(1)} %get-tuple-element.23), channel_id=1, source_target_pairs={{0,4},{4,0},{8,12},{12,8},{16,20},{20,16},{24,28},{28,24},{1,5},{5... | collective-permute-start | bytes 393224 | tf_op jit(solution)/shard_map/ppermute | solution.py:222
  23.1 2.1 %collective-permute-done.7 = bf16[32,2048]{1,0:T(8,128)(2,1)S(1)} collective-permute-done((bf16[32,2048]{1,0:T(8,128)(2,1)S(1)}, bf16[32,2048]{1,0:T(8,128)(2,1)S(1)}, u32[]{:S(2)}, u32[]{:S(2)}) %collective-permute-start.7) | collective-permute-done | bytes 131104 | tf_op jit(solution)/shard_map/ppermute | solution.py:222
  25.3 0.7 %collective-permute-start.8 = (bf16[16,2048]{1,0:T(8,128)(2,1)S(1)}, bf16[16,2048]{1,0:T(8,128)(2,1)S(1)}, u32[]{:S(2)}, u32[]{:S(2)}) collective-permute-start(bf16[16,2048]{1,0:T(8,128)(2,1)S(1)} %get-tuple-element.25), channel_id=1, source_target_pairs={{0,16},{4,20},{8,24},{12,28},{16,0},{20,4},{24,8},{28,12},{1,17},{... | collective-permute-start | bytes 196616 | tf_op jit(solution)/shard_map/ppermute | solution.py:222
  26.0 1.0 %collective-permute-start.9 = (bf16[16,2048]{1,0:T(8,128)(2,1)S(1)}, bf16[16,2048]{1,0:T(8,128)(2,1)S(1)}, u32[]{:S(2)}, u32[]{:S(2)}) collective-permute-start(bf16[16,2048]{1,0:T(8,128)(2,1)S(1)} %get-tuple-element.26), channel_id=1, source_target_pairs={{0,24},{4,28},{8,16},{12,20},{16,8},{20,12},{24,0},{28,4},{1,25},{... | collective-permute-start | bytes 196616 | tf_op jit(solution)/shard_map/ppermute | solution.py:222
  27.0 0.0 collective-permute-done.5
  27.1 1.9 %collective-permute-start.6 = (bf16[16,2048]{1,0:T(8,128)(2,1)S(1)}, bf16[16,2048]{1,0:T(8,128)(2,1)S(1)}, u32[]{:S(2)}, u32[]{:S(2)}) collective-permute-start(bf16[16,2048]{1,0:T(8,128)(2,1)S(1)} %get-tuple-element.27), channel_id=1, source_target_pairs={{0,8},{4,12},{8,0},{12,4},{16,24},{20,28},{24,16},{28,20},{1,9},{5... | collective-permute-start | bytes 196616 | tf_op jit(solution)/shard_map/ppermute | solution.py:222
  28.9 1.6 %collective-permute-done.8 = bf16[16,2048]{1,0:T(8,128)(2,1)S(1)} collective-permute-done((bf16[16,2048]{1,0:T(8,128)(2,1)S(1)}, bf16[16,2048]{1,0:T(8,128)(2,1)S(1)}, u32[]{:S(2)}, u32[]{:S(2)}) %collective-permute-start.8) | collective-permute-done | bytes 65568 | tf_op jit(solution)/shard_map/ppermute | solution.py:222
  30.5 1.6 %collective-permute-done.9 = bf16[16,2048]{1,0:T(8,128)(2,1)S(1)} collective-permute-done((bf16[16,2048]{1,0:T(8,128)(2,1)S(1)}, bf16[16,2048]{1,0:T(8,128)(2,1)S(1)}, u32[]{:S(2)}, u32[]{:S(2)}) %collective-permute-start.9) | collective-permute-done | bytes 65568 | tf_op jit(solution)/shard_map/ppermute | solution.py:222
  32.1 0.0 collective-permute-done.6.refs_1_
  32.1 1.0 %combine.1 = bf16[128,2048]{1,0:T(8,128)(2,1)} custom-call(bf16[128,48]{1,0:T(8,128)(2,1)S(1)} %get-tuple-element.17.table_ref, bf16[16,2048]{1,0:T(8,128)(2,1)S(1)} %get-tuple-element.28.refs_0_, bf16[16,2048]{1,0:T(8,128)(2,1)S(1)} %collective-permute-done.6.refs_1_, bf16[16,2048]{1,0:T(8,128)(2,1)S(1)} %add_convert_fusion.refs_2_), custom_call_target="tpu_custom_call" | custom-call | tf_op jit(solution)/shard_map/combine/pallas_call | solution.py:201
  (7 shorter events, 0.1 us)
Async XLA Ops:
  1.4 10.8 %collective-permute-start.1 = (bf16[16,2048]{1,0:T(8,128)(2,1)S(1)}, bf16[16,2048]{1,0:T(8,128)(2,1)S(1)}, u32[]{:S(2)}, u32[]{:S(2)}) collective-permute-start(bf16[16,2048]{1,0:T(8,128)(2,1)S(1)} %get-tuple-element.15.rows_ref), channel_id=1, source_target_pairs={{0,24},{4,28},{8,16},{12,20},{16,8},{20,12},{24,0},{28,4},{1,25},{... | collective-permute-start | bytes 196616 | tf_op jit(solution)/shard_map/ppermute | solution.py:222
  6.5 5.7 %collective-permute-start = (bf16[16,2048]{1,0:T(8,128)(2,1)S(1)}, bf16[16,2048]{1,0:T(8,128)(2,1)S(1)}, u32[]{:S(2)}, u32[]{:S(2)}) collective-permute-start(bf16[16,2048]{1,0:T(8,128)(2,1)S(1)} %get-tuple-element.15.rows_ref), channel_id=1, source_target_pairs={{0,16},{4,20},{8,24},{12,28},{16,0},{20,4},{24,8},{28,12},{1,17},{... | collective-permute-start | bytes 196616 | tf_op jit(solution)/shard_map/ppermute | solution.py:222
  9.0 4.9 %collective-permute-start.2 = (bf16[16,2048]{1,0:T(8,128)(2,1)S(1)}, bf16[16,2048]{1,0:T(8,128)(2,1)S(1)}, u32[]{:S(2)}, u32[]{:S(2)}) collective-permute-start(bf16[16,2048]{1,0:T(8,128)(2,1)S(1)} %get-tuple-element.18), channel_id=1, source_target_pairs={{0,8},{4,12},{8,0},{12,4},{16,24},{20,28},{24,16},{28,20},{1,9},{5... | collective-permute-start | bytes 196616 | tf_op jit(solution)/shard_map/ppermute | solution.py:222
  12.2 6.3 %collective-permute-start.4 = (bf16[32,2048]{1,0:T(8,128)(2,1)S(1)}, bf16[32,2048]{1,0:T(8,128)(2,1)S(1)}, u32[]{:S(2)}, u32[]{:S(2)}) collective-permute-start(bf16[32,2048]{1,0:T(8,128)(2,1)S(1)} %constant_dynamic-update-slice_fusion.refs_0_), channel_id=1, source_target_pairs={{0,4},{4,0},{8,12},{12,8},{16,20},{20,16},{24,28},{28,24},{1,5},{5... | collective-permute-start | bytes 393224 | tf_op jit(solution)/shard_map/ppermute | solution.py:222
  13.8 7.3 %collective-permute-start.3 = (bf16[32,2048]{1,0:T(8,128)(2,1)S(1)}, bf16[32,2048]{1,0:T(8,128)(2,1)S(1)}, u32[]{:S(2)}, u32[]{:S(2)}) collective-permute-start(bf16[32,2048]{1,0:T(8,128)(2,1)S(1)} %constant_dynamic-update-slice_fusion.2.refs_1_), channel_id=1, source_target_pairs={{0,4},{4,0},{8,12},{12,8},{16,20},{20,16},{24,28},{28,24},{1,5},{5... | collective-permute-start | bytes 393224 | tf_op jit(solution)/shard_map/ppermute | solution.py:222
  19.4 5.9 %collective-permute-start.7 = (bf16[32,2048]{1,0:T(8,128)(2,1)S(1)}, bf16[32,2048]{1,0:T(8,128)(2,1)S(1)}, u32[]{:S(2)}, u32[]{:S(2)}) collective-permute-start(bf16[32,2048]{1,0:T(8,128)(2,1)S(1)} %expert_slice.2.refs_6_), channel_id=1, source_target_pairs={{0,4},{4,0},{8,12},{12,8},{16,20},{20,16},{24,28},{28,24},{1,5},{5... | collective-permute-start | bytes 393224 | tf_op jit(solution)/shard_map/ppermute | solution.py:222
  21.9 5.1 %collective-permute-start.5 = (bf16[32,2048]{1,0:T(8,128)(2,1)S(1)}, bf16[32,2048]{1,0:T(8,128)(2,1)S(1)}, u32[]{:S(2)}, u32[]{:S(2)}) collective-permute-start(bf16[32,2048]{1,0:T(8,128)(2,1)S(1)} %get-tuple-element.23), channel_id=1, source_target_pairs={{0,4},{4,0},{8,12},{12,8},{16,20},{20,16},{24,28},{28,24},{1,5},{5... | collective-permute-start | bytes 393224 | tf_op jit(solution)/shard_map/ppermute | solution.py:222
  25.3 5.2 %collective-permute-start.8 = (bf16[16,2048]{1,0:T(8,128)(2,1)S(1)}, bf16[16,2048]{1,0:T(8,128)(2,1)S(1)}, u32[]{:S(2)}, u32[]{:S(2)}) collective-permute-start(bf16[16,2048]{1,0:T(8,128)(2,1)S(1)} %get-tuple-element.25), channel_id=1, source_target_pairs={{0,16},{4,20},{8,24},{12,28},{16,0},{20,4},{24,8},{28,12},{1,17},{... | collective-permute-start | bytes 196616 | tf_op jit(solution)/shard_map/ppermute | solution.py:222
  26.0 6.1 %collective-permute-start.9 = (bf16[16,2048]{1,0:T(8,128)(2,1)S(1)}, bf16[16,2048]{1,0:T(8,128)(2,1)S(1)}, u32[]{:S(2)}, u32[]{:S(2)}) collective-permute-start(bf16[16,2048]{1,0:T(8,128)(2,1)S(1)} %get-tuple-element.26), channel_id=1, source_target_pairs={{0,24},{4,28},{8,16},{12,20},{16,8},{20,12},{24,0},{28,4},{1,25},{... | collective-permute-start | bytes 196616 | tf_op jit(solution)/shard_map/ppermute | solution.py:222
  27.1 5.1 %collective-permute-start.6 = (bf16[16,2048]{1,0:T(8,128)(2,1)S(1)}, bf16[16,2048]{1,0:T(8,128)(2,1)S(1)}, u32[]{:S(2)}, u32[]{:S(2)}) collective-permute-start(bf16[16,2048]{1,0:T(8,128)(2,1)S(1)} %get-tuple-element.27), channel_id=1, source_target_pairs={{0,8},{4,12},{8,0},{12,4},{16,24},{20,28},{24,16},{28,20},{1,9},{5... | collective-permute-start | bytes 196616 | tf_op jit(solution)/shard_map/ppermute | solution.py:222

commit v14 on v12

--- a/solution.py
+++ b/solution.py
@@ -238,8 +238,9 @@
     outer_y, inner_y = swap(devices, 1, outer), swap(devices, 1, inner)
     (outer_y,) = expert_slice((outer_y,), weights)
     outer, inner, inner_y = expert_slice((outer, inner, inner_y), weights, (outer_y,))
-    outer_y, inner_y = swap(devices, 1, outer_y), swap(devices, 1, inner_y)
-    far, farther = (add_level(outer[at], outer_y[at]) for at in (slice(slots), slice(slots, None)))
+    farther_y, far_y = swap(devices, 1, outer_y[slots:]), swap(devices, 1, outer_y[:slots])
+    inner_y = swap(devices, 1, inner_y)
+    far, farther = add_level(outer[:slots], far_y), add_level(outer[slots:], farther_y)
     own, near = (add_level(inner[at], inner_y[at]) for at in (slice(slots), slice(slots, None)))
     farther, far = swap(devices, 6, farther), swap(devices, 4, far)
     parts = [own, swap(devices, 2, near), add_level(far, farther)]

time: 33.3 us -> 34.4 us (1.033)
  starting transfers between devices: 15.1 us -> 17 us
  waiting for transfers between devices: 11.4 us -> 10.5 us
    ppermute x10 -> x11, starting transfers between devices: 15.1 us -> 17 us  [swap(): lax.ppermute(block, 'ep', [(i, i ^ distance) for i in range(devices)])]
    ppermute x10 -> x11, waiting for transfers between devices: 11.4 us -> 10.5 us  [swap(): lax.ppermute(block, 'ep', [(i, i ^ distance) for i in range(devices)])]
  transfers between devices with their start and end apart: 10 -> 11, of which waited for: 5 -> 6; matrix products, arithmetic and copies ran while one was open for 0% -> 0% of each run, Pallas kernels for 10% -> 10%
where the time goes in v14:
time: 34.4 us; the launch traced here: 34.2 us
  starting transfers between devices  17 us (49%)
  waiting for transfers between devices  10.5 us (31%)
  Pallas kernels  5.84 us (17%)
  between operations  0.73 us (2%)
    ppermute x11, starting transfers between devices, swap(): lax.ppermute(block, 'ep', [(i, i ^ distance) for i in range(devices)])  17 us
    ppermute x11, waiting for transfers between devices, swap(): lax.ppermute(block, 'ep', [(i, i ^ distance) for i in range(devices)])  10.5 us
    pallas_call x1, Pallas kernels, stage_weights(): pl.pallas_call(stage_kernel, out_shape=[jax.ShapeDtypeStruct(shape, jnp.b...  1.8 us
    pallas_call x2, Pallas kernels, expert_slice(): pl.pallas_call(functools.partial(slice_kernel, count), out_shape=[jax.Sha...  1.66 us
    pallas_call x1, Pallas kernels, pick_rows(): pl.pallas_call(pick_kernel, out_shape=(jax.ShapeDtypeStruct((slots, token...  1.37 us
    pallas_call x1, Pallas kernels, combine(): pl.pallas_call(combine_kernel, out_shape=jax.ShapeDtypeStruct(shape, jnp....  1.01 us
  transfers between devices with their start and end apart: 11, of which 6 were waited for; matrix products, arithmetic and copies ran while one was open for 0% of the time, Pallas kernels for 10%

profile of v14, /device:TPU:0, one launch (start us, length us, event | category | flops | bytes accessed | tf_op | source)
XLA Modules:
  0.0 34.2 jit_solution(10519042936576851227)
XLA Ops:
  0.0 1.4 %pick_rows.1 = (bf16[16,2048]{1,0:T(8,128)(2,1)S(1)}, f32[16,128]{1,0:T(8,128)S(1)}) custom-call(s32[8,128]{1,0:T(8,128)} %bitcast.8, f32[8,128]{1,0:T(8,128)} %bitcast.9, bf16[128,2048]{1,0:T(8,128)(2,1)} %tokens_hbm.1, f32[1,2048]{1,0:T(1,128)} %bitcast.7), custom_call_target="tpu_custom_call" | custom-call | tf_op jit(solution)/shard_map/pick_rows/pallas_call | solution.py:58
  1.4 4.1 %collective-permute-start = (bf16[16,2048]{1,0:T(8,128)(2,1)S(1)}, bf16[16,2048]{1,0:T(8,128)(2,1)S(1)}, u32[]{:S(2)}, u32[]{:S(2)}) collective-permute-start(bf16[16,2048]{1,0:T(8,128)(2,1)S(1)} %get-tuple-element.15.rows_ref), channel_id=1, source_target_pairs={{0,16},{4,20},{8,24},{12,28},{16,0},{20,4},{24,8},{28,12},{1,17},{... | collective-permute-start | bytes 196616 | tf_op jit(solution)/shard_map/ppermute | solution.py:222
  5.5 1.3 %collective-permute-start.1 = (bf16[16,2048]{1,0:T(8,128)(2,1)S(1)}, bf16[16,2048]{1,0:T(8,128)(2,1)S(1)}, u32[]{:S(2)}, u32[]{:S(2)}) collective-permute-start(bf16[16,2048]{1,0:T(8,128)(2,1)S(1)} %get-tuple-element.15.rows_ref), channel_id=1, source_target_pairs={{0,24},{4,28},{8,16},{12,20},{16,8},{20,12},{24,0},{28,4},{1,25},{... | collective-permute-start | bytes 196616 | tf_op jit(solution)/shard_map/ppermute | solution.py:222
  7.5 1.8 %stage_weights.1 = (bf16[16,2048]{1,0:T(8,128)(2,1)S(1)}, bf16[128,48]{1,0:T(8,128)(2,1)S(1)}, bf16[192,2048]{1,0:T(8,128)(2,1)S(1)}, bf16[192,2048]{1,0:T(8,128)(2,1)S(1)}, bf16[192,2048]{1,0:T(8,128)(2,1)S(1)}) custom-call(s32[1]{0:T(128)S(6)} %copy.11.live_ref, bf16[16,2048]{1,0:T(8,128)(2,1)S(1)} %get-tuple-element.15.rows_ref, ...), custom_call_target="tpu_custom_call" | custom-call | flops 37748736 | bytes 2359296 | tf_op jit(solution)/shard_map/stage_weights/pallas_call | solution.py:137
  9.3 0.3 collective-permute-start.2
  9.6 0.0 collective-permute-done
  9.6 2.1 %collective-permute-done.1 = bf16[16,2048]{1,0:T(8,128)(2,1)S(1)} collective-permute-done((bf16[16,2048]{1,0:T(8,128)(2,1)S(1)}, bf16[16,2048]{1,0:T(8,128)(2,1)S(1)}, u32[]{:S(2)}, u32[]{:S(2)}) %collective-permute-start.1) | collective-permute-done | bytes 65568 | tf_op jit(solution)/shard_map/ppermute | solution.py:222
  11.7 1.5 %collective-permute-start.4 = (bf16[32,2048]{1,0:T(8,128)(2,1)S(1)}, bf16[32,2048]{1,0:T(8,128)(2,1)S(1)}, u32[]{:S(2)}, u32[]{:S(2)}) collective-permute-start(bf16[32,2048]{1,0:T(8,128)(2,1)S(1)} %constant_dynamic-update-slice_fusion.refs_0_), channel_id=1, source_target_pairs={{0,4},{4,0},{8,12},{12,8},{16,20},{20,16},{24,28},{28,24},{1,5},{5... | collective-permute-start | bytes 393224 | tf_op jit(solution)/shard_map/ppermute | solution.py:222
  13.2 0.4 %collective-permute-done.2 = bf16[16,2048]{1,0:T(8,128)(2,1)S(1)} collective-permute-done((bf16[16,2048]{1,0:T(8,128)(2,1)S(1)}, bf16[16,2048]{1,0:T(8,128)(2,1)S(1)}, u32[]{:S(2)}, u32[]{:S(2)}) %collective-permute-start.2) | collective-permute-done | bytes 65568 | tf_op jit(solution)/shard_map/ppermute | solution.py:222
  13.6 1.5 %collective-permute-start.3 = (bf16[32,2048]{1,0:T(8,128)(2,1)S(1)}, bf16[32,2048]{1,0:T(8,128)(2,1)S(1)}, u32[]{:S(2)}, u32[]{:S(2)}) collective-permute-start(bf16[32,2048]{1,0:T(8,128)(2,1)S(1)} %constant_dynamic-update-slice_fusion.2.refs_1_), channel_id=1, source_target_pairs={{0,4},{4,0},{8,12},{12,8},{16,20},{20,16},{24,28},{28,24},{1,5},{5... | collective-permute-start | bytes 393224 | tf_op jit(solution)/shard_map/ppermute | solution.py:222
  15.1 2.6 %collective-permute-done.4.refs_0_ = bf16[32,2048]{1,0:T(8,128)(2,1)S(1)} collective-permute-done((bf16[32,2048]{1,0:T(8,128)(2,1)S(1)}, bf16[32,2048]{1,0:T(8,128)(2,1)S(1)}, u32[]{:S(2)}, u32[]{:S(2)}) %collective-permute-start.4) | collective-permute-done | bytes 131104 | tf_op jit(solution)/shard_map/ppermute | solution.py:222
  17.8 0.8 %expert_slice.2.refs_6_ = bf16[32,2048]{1,0:T(8,128)(2,1)S(1)} custom-call(bf16[32,2048]{1,0:T(8,128)(2,1)S(1)} %collective-permute-done.4.refs_0_, bf16[192,2048]{1,0:T(8,128)(2,1)S(1)} %get-tuple-element.19.refs_1_.refs_3_, bf16[192,2048]{1,0:T(8,128)(2,1)S(1)} %get-tuple-element.20.refs_2_.refs_4_, bf16[192,2048]{1,0:T(8,128)(2,1)S(1)} %get-tuple-element.21.refs_3_.refs_5_), custom_call_target="tpu_custom_call" | custom-call | flops 75497472 | bytes 2359296 | tf_op jit(solution)/shard_map/expert_slice/pallas_call | solution.py:161
  18.6 1.6 %collective-permute-start.7 = (bf16[16,2048]{1,0:T(8,128)(2,1)S(1)}, bf16[16,2048]{1,0:T(8,128)(2,1)S(1)}, u32[]{:S(2)}, u32[]{:S(2)}) collective-permute-start(bf16[16,2048]{1,0:T(8,128)(2,1)S(1)} %get-tuple-element.29), channel_id=1, source_target_pairs={{0,4},{4,0},{8,12},{12,8},{16,20},{20,16},{24,28},{28,24},{1,5},{5... | collective-permute-start | bytes 196616 | tf_op jit(solution)/shard_map/ppermute | solution.py:222
  20.2 0.5 %collective-permute-start.9 = (bf16[16,2048]{1,0:T(8,128)(2,1)S(1)}, bf16[16,2048]{1,0:T(8,128)(2,1)S(1)}, u32[]{:S(2)}, u32[]{:S(2)}) collective-permute-start(bf16[16,2048]{1,0:T(8,128)(2,1)S(1)} %get-tuple-element.30), channel_id=1, source_target_pairs={{0,4},{4,0},{8,12},{12,8},{16,20},{20,16},{24,28},{28,24},{1,5},{5... | collective-permute-start | bytes 196616 | tf_op jit(solution)/shard_map/ppermute | solution.py:222
  20.7 0.0 collective-permute-done.3.refs_2_
  20.7 0.9 %expert_slice.3 = (bf16[32,2048]{1,0:T(8,128)(2,1)S(1)}, bf16[32,2048]{1,0:T(8,128)(2,1)S(1)}, bf16[32,2048]{1,0:T(8,128)(2,1)S(1)}) custom-call(bf16[32,2048]{1,0:T(8,128)(2,1)S(1)} %constant_dynamic-update-slice_fusion.refs_0_, bf16[32,2048]{1,0:T(8,128)(2,1)S(1)} %constant_dynamic-update-slice_fusion.2.refs_1_, ...), custom_call_target="tpu_custom_call" | custom-call | flops 226492416 | bytes 2359296 | tf_op jit(solution)/shard_map/expert_slice/pallas_call | solution.py:161
  21.6 1.6 %collective-permute-start.5 = (bf16[32,2048]{1,0:T(8,128)(2,1)S(1)}, bf16[32,2048]{1,0:T(8,128)(2,1)S(1)}, u32[]{:S(2)}, u32[]{:S(2)}) collective-permute-start(bf16[32,2048]{1,0:T(8,128)(2,1)S(1)} %get-tuple-element.23), channel_id=1, source_target_pairs={{0,4},{4,0},{8,12},{12,8},{16,20},{20,16},{24,28},{28,24},{1,5},{5... | collective-permute-start | bytes 393224 | tf_op jit(solution)/shard_map/ppermute | solution.py:222
  23.2 0.0 collective-permute-done.7
  23.2 1.3 %collective-permute-done.9 = bf16[16,2048]{1,0:T(8,128)(2,1)S(1)} collective-permute-done((bf16[16,2048]{1,0:T(8,128)(2,1)S(1)}, bf16[16,2048]{1,0:T(8,128)(2,1)S(1)}, u32[]{:S(2)}, u32[]{:S(2)}) %collective-permute-start.9) | collective-permute-done | bytes 65568 | tf_op jit(solution)/shard_map/ppermute | solution.py:222
  24.5 2.8 %collective-permute-start.10 = (bf16[16,2048]{1,0:T(8,128)(2,1)S(1)}, bf16[16,2048]{1,0:T(8,128)(2,1)S(1)}, u32[]{:S(2)}, u32[]{:S(2)}) collective-permute-start(bf16[16,2048]{1,0:T(8,128)(2,1)S(1)} %get-tuple-element.28), channel_id=1, source_target_pairs={{0,24},{4,28},{8,16},{12,20},{16,8},{20,12},{24,0},{28,4},{1,25},{... | collective-permute-start | bytes 196616 | tf_op jit(solution)/shard_map/ppermute | solution.py:222
  27.3 0.4 %collective-permute-start.8 = (bf16[16,2048]{1,0:T(8,128)(2,1)S(1)}, bf16[16,2048]{1,0:T(8,128)(2,1)S(1)}, u32[]{:S(2)}, u32[]{:S(2)}) collective-permute-start(bf16[16,2048]{1,0:T(8,128)(2,1)S(1)} %get-tuple-element.27), channel_id=1, source_target_pairs={{0,16},{4,20},{8,24},{12,28},{16,0},{20,4},{24,8},{28,12},{1,17},{... | collective-permute-start | bytes 196616 | tf_op jit(solution)/shard_map/ppermute | solution.py:222
  27.7 0.0 collective-permute-done.5
  27.8 1.3 %collective-permute-start.6 = (bf16[16,2048]{1,0:T(8,128)(2,1)S(1)}, bf16[16,2048]{1,0:T(8,128)(2,1)S(1)}, u32[]{:S(2)}, u32[]{:S(2)}) collective-permute-start(bf16[16,2048]{1,0:T(8,128)(2,1)S(1)} %get-tuple-element.25), channel_id=1, source_target_pairs={{0,8},{4,12},{8,0},{12,4},{16,24},{20,28},{24,16},{28,20},{1,9},{5... | collective-permute-start | bytes 196616 | tf_op jit(solution)/shard_map/ppermute | solution.py:222
  29.1 1.6 %collective-permute-done.10 = bf16[16,2048]{1,0:T(8,128)(2,1)S(1)} collective-permute-done((bf16[16,2048]{1,0:T(8,128)(2,1)S(1)}, bf16[16,2048]{1,0:T(8,128)(2,1)S(1)}, u32[]{:S(2)}, u32[]{:S(2)}) %collective-permute-start.10) | collective-permute-done | bytes 65568 | tf_op jit(solution)/shard_map/ppermute | solution.py:222
  30.7 2.5 %collective-permute-done.8 = bf16[16,2048]{1,0:T(8,128)(2,1)S(1)} collective-permute-done((bf16[16,2048]{1,0:T(8,128)(2,1)S(1)}, bf16[16,2048]{1,0:T(8,128)(2,1)S(1)}, u32[]{:S(2)}, u32[]{:S(2)}) %collective-permute-start.8) | collective-permute-done | bytes 65568 | tf_op jit(solution)/shard_map/ppermute | solution.py:222
  33.2 0.0 collective-permute-done.6.refs_1_
  33.2 1.0 %combine.1 = bf16[128,2048]{1,0:T(8,128)(2,1)} custom-call(bf16[128,48]{1,0:T(8,128)(2,1)S(1)} %get-tuple-element.17.table_ref, bf16[16,2048]{1,0:T(8,128)(2,1)S(1)} %get-tuple-element.26.refs_0_, bf16[16,2048]{1,0:T(8,128)(2,1)S(1)} %collective-permute-done.6.refs_1_, bf16[16,2048]{1,0:T(8,128)(2,1)S(1)} %add_convert_fusion.refs_2_), custom_call_target="tpu_custom_call" | custom-call | tf_op jit(solution)/shard_map/combine/pallas_call | solution.py:201
  (8 shorter events, 0.1 us)
Async XLA Ops:
  1.4 8.2 %collective-permute-start = (bf16[16,2048]{1,0:T(8,128)(2,1)S(1)}, bf16[16,2048]{1,0:T(8,128)(2,1)S(1)}, u32[]{:S(2)}, u32[]{:S(2)}) collective-permute-start(bf16[16,2048]{1,0:T(8,128)(2,1)S(1)} %get-tuple-element.15.rows_ref), channel_id=1, source_target_pairs={{0,16},{4,20},{8,24},{12,28},{16,0},{20,4},{24,8},{28,12},{1,17},{... | collective-permute-start | bytes 196616 | tf_op jit(solution)/shard_map/ppermute | solution.py:222
  5.5 6.2 %collective-permute-start.1 = (bf16[16,2048]{1,0:T(8,128)(2,1)S(1)}, bf16[16,2048]{1,0:T(8,128)(2,1)S(1)}, u32[]{:S(2)}, u32[]{:S(2)}) collective-permute-start(bf16[16,2048]{1,0:T(8,128)(2,1)S(1)} %get-tuple-element.15.rows_ref), channel_id=1, source_target_pairs={{0,24},{4,28},{8,16},{12,20},{16,8},{20,12},{24,0},{28,4},{1,25},{... | collective-permute-start | bytes 196616 | tf_op jit(solution)/shard_map/ppermute | solution.py:222
  9.3 4.3 %collective-permute-start.2 = (bf16[16,2048]{1,0:T(8,128)(2,1)S(1)}, bf16[16,2048]{1,0:T(8,128)(2,1)S(1)}, u32[]{:S(2)}, u32[]{:S(2)}) collective-permute-start(bf16[16,2048]{1,0:T(8,128)(2,1)S(1)} %get-tuple-element.18), channel_id=1, source_target_pairs={{0,8},{4,12},{8,0},{12,4},{16,24},{20,28},{24,16},{28,20},{1,9},{5... | collective-permute-start | bytes 196616 | tf_op jit(solution)/shard_map/ppermute | solution.py:222
  11.7 6.1 %collective-permute-start.4 = (bf16[32,2048]{1,0:T(8,128)(2,1)S(1)}, bf16[32,2048]{1,0:T(8,128)(2,1)S(1)}, u32[]{:S(2)}, u32[]{:S(2)}) collective-permute-start(bf16[32,2048]{1,0:T(8,128)(2,1)S(1)} %constant_dynamic-update-slice_fusion.refs_0_), channel_id=1, source_target_pairs={{0,4},{4,0},{8,12},{12,8},{16,20},{20,16},{24,28},{28,24},{1,5},{5... | collective-permute-start | bytes 393224 | tf_op jit(solution)/shard_map/ppermute | solution.py:222
  13.6 7.1 %collective-permute-start.3 = (bf16[32,2048]{1,0:T(8,128)(2,1)S(1)}, bf16[32,2048]{1,0:T(8,128)(2,1)S(1)}, u32[]{:S(2)}, u32[]{:S(2)}) collective-permute-start(bf16[32,2048]{1,0:T(8,128)(2,1)S(1)} %constant_dynamic-update-slice_fusion.2.refs_1_), channel_id=1, source_target_pairs={{0,4},{4,0},{8,12},{12,8},{16,20},{20,16},{24,28},{28,24},{1,5},{5... | collective-permute-start | bytes 393224 | tf_op jit(solution)/shard_map/ppermute | solution.py:222
  18.6 4.6 %collective-permute-start.7 = (bf16[16,2048]{1,0:T(8,128)(2,1)S(1)}, bf16[16,2048]{1,0:T(8,128)(2,1)S(1)}, u32[]{:S(2)}, u32[]{:S(2)}) collective-permute-start(bf16[16,2048]{1,0:T(8,128)(2,1)S(1)} %get-tuple-element.29), channel_id=1, source_target_pairs={{0,4},{4,0},{8,12},{12,8},{16,20},{20,16},{24,28},{28,24},{1,5},{5... | collective-permute-start | bytes 196616 | tf_op jit(solution)/shard_map/ppermute | solution.py:222
  20.2 4.3 %collective-permute-start.9 = (bf16[16,2048]{1,0:T(8,128)(2,1)S(1)}, bf16[16,2048]{1,0:T(8,128)(2,1)S(1)}, u32[]{:S(2)}, u32[]{:S(2)}) collective-permute-start(bf16[16,2048]{1,0:T(8,128)(2,1)S(1)} %get-tuple-element.30), channel_id=1, source_target_pairs={{0,4},{4,0},{8,12},{12,8},{16,20},{20,16},{24,28},{28,24},{1,5},{5... | collective-permute-start | bytes 196616 | tf_op jit(solution)/shard_map/ppermute | solution.py:222
  21.6 6.2 %collective-permute-start.5 = (bf16[32,2048]{1,0:T(8,128)(2,1)S(1)}, bf16[32,2048]{1,0:T(8,128)(2,1)S(1)}, u32[]{:S(2)}, u32[]{:S(2)}) collective-permute-start(bf16[32,2048]{1,0:T(8,128)(2,1)S(1)} %get-tuple-element.23), channel_id=1, source_target_pairs={{0,4},{4,0},{8,12},{12,8},{16,20},{20,16},{24,28},{28,24},{1,5},{5... | collective-permute-start | bytes 393224 | tf_op jit(solution)/shard_map/ppermute | solution.py:222
  24.5 6.1 %collective-permute-start.10 = (bf16[16,2048]{1,0:T(8,128)(2,1)S(1)}, bf16[16,2048]{1,0:T(8,128)(2,1)S(1)}, u32[]{:S(2)}, u32[]{:S(2)}) collective-permute-start(bf16[16,2048]{1,0:T(8,128)(2,1)S(1)} %get-tuple-element.28), channel_id=1, source_target_pairs={{0,24},{4,28},{8,16},{12,20},{16,8},{20,12},{24,0},{28,4},{1,25},{... | collective-permute-start | bytes 196616 | tf_op jit(solution)/shard_map/ppermute | solution.py:222
  27.3 5.9 %collective-permute-start.8 = (bf16[16,2048]{1,0:T(8,128)(2,1)S(1)}, bf16[16,2048]{1,0:T(8,128)(2,1)S(1)}, u32[]{:S(2)}, u32[]{:S(2)}) collective-permute-start(bf16[16,2048]{1,0:T(8,128)(2,1)S(1)} %get-tuple-element.27), channel_id=1, source_target_pairs={{0,16},{4,20},{8,24},{12,28},{16,0},{20,4},{24,8},{28,12},{1,17},{... | collective-permute-start | bytes 196616 | tf_op jit(solution)/shard_map/ppermute | solution.py:222
  27.8 5.5 %collective-permute-start.6 = (bf16[16,2048]{1,0:T(8,128)(2,1)S(1)}, bf16[16,2048]{1,0:T(8,128)(2,1)S(1)}, u32[]{:S(2)}, u32[]{:S(2)}) collective-permute-start(bf16[16,2048]{1,0:T(8,128)(2,1)S(1)} %get-tuple-element.25), channel_id=1, source_target_pairs={{0,8},{4,12},{8,0},{12,4},{16,24},{20,28},{24,16},{28,20},{1,9},{5... | collective-permute-start | bytes 196616 | tf_op jit(solution)/shard_map/ppermute | solution.py:222
